TPU v7x, 32 devices: a whole 2x2x4 slice. The times are simulated.
32 devices in a mesh: grp: 2 (over x), inp: 4 (over y, core), out: 4 (over z).
Axes of the slice: x: 2, y: 2, z: 4, core: 2. Of those that a mesh axis runs over, the one named last changes fastest.
Arguments:
- activations: bfloat16 [4, 512, 8192], P('grp', 'out', 'inp'), parts along dimension 0, may hold values from -6 to 6
- out_grads: bfloat16 [4, 512, 28672], P('grp', 'inp', 'out'), parts along dimension 0, may hold values from -6 to 6
- query_grads: bfloat16 [2, 28672, 8192], P(None, 'out', 'inp'), may hold values from -0.00036621094 to 0.00036621094
- token_ids: int32 [4, 512], P('grp'), parts along dimension 0, may hold values from 0 to 128255
- loss_mask: int32 [4, 512], P('grp'), parts along dimension 0, may hold values 0 or 1
Outputs:
- scores: float32 [2, 4, 512], P(None, 'grp'), parts along dimension 1
There are 2 independent parts, one for each index of `grp`. A program takes and returns all parts, laid end to end along the dimension named above; an argument that names none is the same for every part. Nothing has to cross between parts.
All inputs are finite; a program needn't handle non-finite values.
Results may differ from a plain program's by a relative error of at most 0.0003.
Values may be sent and summed in bfloat16 or wider, within the bound.
No kernel may reach another device: no remote copies, remote signals or barrier semaphores. Data moves between devices by JAX's collectives and lax.ppermute only.
A program may use at most 128 MiB of HBM per device.

v0:
```python
import jax
import jax.numpy as jnp
from jax import lax
from jax.sharding import PartitionSpec as P


def shards(activations, out_grads, query_grads, token_ids, loss_mask):
    blocks = activations.shape[0]
    partials = []
    for number in range(blocks):
        gathered = lax.all_gather(activations[number], "out", axis=0, tiled=True)
        projected = jnp.einsum(
            "to,qoi->tqi",
            lax.all_gather(out_grads[number], "inp", axis=0, tiled=True),
            query_grads,
            preferred_element_type=jnp.float32,
        )
        partial_value = jnp.sum(projected * gathered.astype(jnp.float32)[:, None, :], axis=2)
        partial_value = lax.psum(partial_value, ("inp", "out"))
        partials.append(partial_value)
    stacked = jnp.stack(partials)
    equal = token_ids[:, :, None] == token_ids[:, None, :]
    counts = jnp.sum(equal.astype(jnp.int32), axis=2)
    weight = loss_mask.astype(jnp.float32) / counts.astype(jnp.float32)
    return jnp.transpose(stacked * weight[:, :, None], (2, 0, 1))


def solution(mesh):
    in_specs = (
        P("grp", "out", "inp"),
        P("grp", "inp", "out"),
        P(None, "out", "inp"),
        P("grp", None),
        P("grp", None),
    )
    out_specs = P(None, "grp", None)
    return jax.shard_map(shards, mesh=mesh, in_specs=in_specs, out_specs=out_specs, check_vma=False)
```

profile of v0, /device:TPU:0, one launch (start us, length us, event | category | flops | bytes accessed | tf_op | source)
XLA Modules:
  0.0 290.1 jit_solution(5545557528172188764)
XLA Ops:
  6.5 0.0 copy-start
  6.5 0.0 copy-start.1
  6.5 0.0 all-gather.15.cloned.1.call-start
  6.5 2.3 fusion.10
  8.9 0.0 all-gather.15.cloned.1.call-update
  8.9 0.0 all-gather.11.cloned.1.call-start
  8.9 0.7 all-gather.11.cloned.1.call-update
  9.6 0.0 all-gather.13.cloned.1.call-start
  9.7 4.1 %fusion.9 = (bf16[1,128,7168]{2,1,0:T(8,128)(2,1)}, bf16[1,128,7168]{2,1,0:T(8,128)(2,1)}) fusion(bf16[2,128,7168]{2,1,0:T(8,128)(2,1)} %param.6), kind=kLoop, calls=%fused_computation.12 | loop fusion | bytes 7340032 | tf_op jit(solution)/shard_map/slice | solution.py:14
  13.8 0.0 all-gather.13.cloned.1.call-update
  13.8 0.0 all-gather.9.cloned.1.call-start
  13.9 0.5 all-gather.9.cloned.1.call-update
  14.4 0.0 copy-done
  14.4 0.4 convert_reduce_fusion
  14.8 0.0 copy-done.1
  14.8 42.8 %all-gather.15.cloned.1.call-done = bf16[1,512,2048]{2,1,0:T(8,128)(2,1)} async-done(((bf16[1,128,2048]{2,1,0:T(8,128)(2,1)}), bf16[1,512,2048]{2,1,0:T(8,128)(2,1)}) %all-gather.15.cloned.1.call-update) | async-done | bytes 2097168 | tf_op jit(solution)/shard_map/all_gather | solution.py:11
  57.7 4.1 %bitcast_convert_fusion = f32[512,2048]{1,0:T(8,128)} fusion(bf16[1,512,2048]{2,1,0:T(8,128)(2,1)} %all-gather.15.cloned.1.call-done), kind=kLoop, calls=%fused_computation.6 | loop fusion | flops 1048576 | bytes 6291456 | tf_op jit(solution)/shard_map/convert_element_type | solution.py:18
  61.8 42.2 %all-gather.11.cloned.1.call-done = bf16[1,512,2048]{2,1,0:T(8,128)(2,1)} async-done(((bf16[1,128,2048]{2,1,0:T(8,128)(2,1)}), bf16[1,512,2048]{2,1,0:T(8,128)(2,1)}) %all-gather.11.cloned.1.call-update) | async-done | bytes 2097168 | tf_op jit(solution)/shard_map/all_gather | solution.py:11
  103.9 4.1 %bitcast_convert_fusion.1 = f32[512,2048]{1,0:T(8,128)} fusion(bf16[1,512,2048]{2,1,0:T(8,128)(2,1)} %all-gather.11.cloned.1.call-done), kind=kLoop, calls=%fused_computation.7 | loop fusion | flops 1048576 | bytes 6291456 | tf_op jit(solution)/shard_map/convert_element_type | solution.py:18
  108.1 48.5 %all-gather.13.cloned.1.call-done = bf16[1,512,7168]{2,1,0:T(8,128)(2,1)} async-done(((bf16[1,128,7168]{2,1,0:T(8,128)(2,1)}), bf16[1,512,7168]{2,1,0:T(8,128)(2,1)}) %all-gather.13.cloned.1.call-update) | async-done | bytes 7340048 | tf_op jit(solution)/shard_map/all_gather | solution.py:14
  156.6 39.0 %multiply_reduce_fusion = f32[512,2]{0,1:T(2,128)S(1)} fusion(f32[512,2048]{1,0:T(8,128)} %bitcast_convert_fusion, bf16[2,7168,2048]{2,1,0:T(8,128)(2,1)} %param.7, bf16[1,512,7168]{2,1,0:T(8,128)(2,1)} %all-gather.13.cloned.1.call-done), kind=kOutput, calls=%fused_computation | convolution fusion | flops 30068965376 | bytes 70258688 | tf_op jit(solution)/shard_map/to,qoi->tqi/dot_general | solution.py:12
  195.6 14.8 %all-gather.9.cloned.1.call-done = bf16[1,512,7168]{2,1,0:T(8,128)(2,1)} async-done(((bf16[1,128,7168]{2,1,0:T(8,128)(2,1)}), bf16[1,512,7168]{2,1,0:T(8,128)(2,1)}) %all-gather.9.cloned.1.call-update) | async-done | bytes 7340048 | tf_op jit(solution)/shard_map/all_gather | solution.py:14
  210.4 38.8 %multiply_reduce_fusion.1 = f32[512,2]{0,1:T(2,128)S(1)} fusion(f32[512,2048]{1,0:T(8,128)} %bitcast_convert_fusion.1, bf16[2,7168,2048]{2,1,0:T(8,128)(2,1)} %param.7, bf16[1,512,7168]{2,1,0:T(8,128)(2,1)} %all-gather.9.cloned.1.call-done), kind=kOutput, calls=%fused_computation.1 | convolution fusion | flops 30068965376 | bytes 70258688 | tf_op jit(solution)/shard_map/to,qoi->tqi/dot_general | solution.py:12
  249.2 33.8 %all-reduce = (f32[1,512,2]{1,0,2:T(1,128)S(1)}, f32[1,512,2]{1,0,2:T(1,128)S(1)}) all-reduce(f32[1,512,2]{1,0,2:T(1,128)S(1)} %stack.10, f32[1,512,2]{1,0,2:T(1,128)S(1)} %stack.9), channel_id=1, replica_groups=mesh['grp'=2,'inp'=4,'out'=4] {'inp','out'}, use_global_device_ids=true, to_apply=%region_3.0 | all-reduce | flops 2048 | bytes 16384 | tf_op jit(solution)/shard_map/psum | solution.py:19
  283.0 0.6 fusion.8
  (3 shorter events, 0.0 us)
Async XLA Ops:
  6.5 7.9 %copy-start = (s32[2,512]{1,0:T(2,128)S(1)}, s32[2,512]{1,0:T(2,128)}, u32[]{:S(2)}) copy-start(s32[2,512]{1,0:T(2,128)} %param.8) | copy-start | bytes 12292
  6.5 8.3 %copy-start.1 = (s32[2,512]{1,0:T(2,128)S(1)}, s32[2,512]{1,0:T(2,128)}, u32[]{:S(2)}) copy-start(s32[2,512]{1,0:T(2,128)} %param.9) | copy-start | bytes 12292
  6.5 51.1 %all-gather.15.cloned.1.call-start = ((), (), s32[]{:S(2)}) async-start(), calls=%async_computation.3 | async-start | bytes 2621440 | tf_op jit(solution)/shard_map/all_gather | solution.py:11
  8.9 95.0 %all-gather.11.cloned.1.call-start = ((), (), s32[]{:S(2)}) async-start(), calls=%async_computation.1 | async-start | bytes 2621440 | tf_op jit(solution)/shard_map/all_gather | solution.py:11
  9.6 146.9 %all-gather.13.cloned.1.call-start = ((), (), s32[]{:S(2)}) async-start(), calls=%async_computation.2 | async-start | bytes 9175040 | tf_op jit(solution)/shard_map/all_gather | solution.py:14
  13.8 196.5 %all-gather.9.cloned.1.call-start = ((), (), s32[]{:S(2)}) async-start(), calls=%async_computation | async-start | bytes 9175040 | tf_op jit(solution)/shard_map/all_gather | solution.py:14
Sparse Core Ops, SparseCore 0:
  9.0 48.6 all-gather.14
  59.2 44.6 all-gather.10
  105.5 51.0 all-gather.12
  158.0 52.3 all-gather.8
where the time goes:
time: 290 us
  waiting for transfers between devices  150 us (52%)
  matrix products  77.8 us (27%)
  blocking collectives  33.8 us (12%)
  between operations  13.2 us (5%)
  other arithmetic  9.25 us (3%)
  local copies, waits for them, and re-layouts  6.45 us (2%)
    all_gather x2, waiting for transfers between devices, shards(): gathered = lax.all_gather(activations[number], 'out', axis=0, tiled=True)  85 us
    dot_general x2, matrix products, shards(): jnp.einsum('to,qoi->tqi', lax.all_gather(out_grads[number], 'inp', axis=0...  77.8 us
    all_gather x2, waiting for transfers between devices, shards(): lax.all_gather(out_grads[number], 'inp', axis=0, tiled=True)  63.3 us
    psum x1, blocking collectives, shards(): partial_value = lax.psum(partial_value, ('inp', 'out'))  33.8 us
    convert_element_type x2, other arithmetic, shards(): gathered.astype(jnp.float32)[:, None, :]  8.22 us
  transfers between devices with their start and end apart: 4, of which 4 were waited for; matrix products, arithmetic and copies ran while one was open for 18% of the time, Pallas kernels for 0%

commit v1 on v0

v1 whole, which is shorter than its diff:
```python
import functools

import jax
import jax.numpy as jnp
from jax import lax
from jax.experimental import pallas as pl
from jax.experimental.pallas import tpu as pltpu
from jax.sharding import PartitionSpec as P

VMEM_LIMIT = 40 * 1024 * 1024


def matmul_kernel(parts, accumulate, *refs):
    g_refs, refs = refs[:parts], refs[parts:]
    q_ref, refs = refs[0], refs[1:]
    if accumulate:
        before_ref, refs = refs[0], refs[1:]
    out_ref, x_ref, sems = refs
    rows = x_ref.shape[0] // parts

    @pl.when((pl.program_id(0) == 0) & (pl.program_id(1) == 0))
    def _():
        copies = [
            pltpu.make_async_copy(g_ref, x_ref.at[pl.ds(at * rows, rows)], sems.at[at])
            for at, g_ref in enumerate(g_refs)
        ]
        for copy in copies:
            copy.start()
        for copy in copies:
            copy.wait()

    product = jnp.dot(x_ref[...], q_ref[0], preferred_element_type=jnp.float32)
    if accumulate:
        product = product + before_ref[0]
    out_ref[0] = product


def tile_of(length, most):
    size = min(length, most)
    while length % size:
        size -= 128
    return size


def project(parts, query_grads, chunk, before=None, tile=512):
    rows, depth = parts[0].shape
    queries, _, width = query_grads.shape
    tile = tile_of(width, tile)
    total = rows * len(parts)
    out_spec = pl.BlockSpec((1, total, tile), lambda q, i: (q, 0, i))
    in_specs = [pl.BlockSpec(memory_space=pl.ANY)] * len(parts)
    in_specs.append(pl.BlockSpec((1, depth, tile), lambda q, i: (q, chunk, i)))
    operands = [*parts, query_grads]
    aliases = {}
    if before is not None:
        aliases = {len(operands): 0}
        in_specs.append(out_spec)
        operands.append(before)
    return pl.pallas_call(
        functools.partial(matmul_kernel, len(parts), before is not None),
        grid=(queries, width // tile),
        in_specs=in_specs,
        out_specs=out_spec,
        out_shape=jax.ShapeDtypeStruct((queries, total, width), jnp.float32),
        scratch_shapes=[
            pltpu.VMEM((total, depth), jnp.bfloat16),
            pltpu.SemaphoreType.DMA((len(parts),)),
        ],
        input_output_aliases=aliases,
        cost_estimate=pl.CostEstimate(
            flops=2 * queries * total * depth * width,
            bytes_accessed=2 * queries * depth * width + 4 * queries * total * width * (1 + len(aliases)),
            transcendentals=0,
        ),
        compiler_params=pltpu.CompilerParams(vmem_limit_bytes=VMEM_LIMIT),
        name="project",
    )(*operands)


def xor_sum(value, axis, size):
    if size & (size - 1):
        return lax.psum(value, axis)
    terms = [value]
    for other in range(1, size):
        terms.append(lax.ppermute(value, axis, [(at, at ^ other) for at in range(size)]))
    while len(terms) > 1:
        terms = [terms[at] + terms[at + 1] for at in range(0, len(terms), 2)]
    return terms[0]


def shards(inp_size, out_size, activations, out_grads, query_grads, token_ids, loss_mask):
    blocks, shard, depth = out_grads.shape
    queries, _, width = query_grads.shape
    tokens = token_ids.shape[1]
    pair = 2 if inp_size % 2 == 0 else 1
    chips = inp_size // pair
    me = lax.axis_index("inp")
    chunks = 4 if depth % 512 == 0 else 1
    part = depth // chunks

    def flip(value):
        return lax.ppermute(value, "inp", [(at, at ^ 1) for at in range(inp_size)])

    def shift(value, by):
        return lax.ppermute(value, "inp", [(at, (at + pair * by) % inp_size) for at in range(inp_size)])

    own = out_grads.reshape(blocks * shard, depth)
    arrived = []
    for chunk in range(chunks):
        piece = own[:, chunk * part:(chunk + 1) * part]
        if chunk >= 2:
            piece, _ = lax.optimization_barrier((piece, arrived[chunk - 2]))
        arrived.append([shift(piece, by) for by in range(1, chips)])
    near = [own] + ([flip(own)] if pair == 2 else [])
    gathered = lax.all_gather(activations, "out", axis=1, tiled=True)

    near_sum = project(near, query_grads, 0, tile=256)
    far_sum = None
    if chips > 1:
        for chunk in range(chunks):
            far = []
            for piece in arrived[chunk]:
                far.append(piece)
                if pair == 2:
                    far.append(flip(piece))
            far_sum = project(far, query_grads, chunk, far_sum)

    raw = []
    sources = []
    for number in range(inp_size):
        by, other = divmod(number, pair)
        source = (me - pair * by + inp_size) % inp_size
        source = source ^ other if pair == 2 else source
        sources.append(source)
        block = lax.dynamic_slice_in_dim(gathered, source * shard, shard, axis=1)
        held = near_sum if by == 0 else far_sum
        first = number if by == 0 else number - pair
        rows = held[:, first * blocks * shard:(first + 1) * blocks * shard].reshape(queries, blocks, shard, width)
        raw.append(jnp.sum(rows * block.astype(jnp.float32)[None], axis=3))
    placed = []
    for at in range(inp_size):
        placed.append(sum(jnp.where(source == at, value, 0.0) for source, value in zip(sources, raw)))
    raw = jnp.stack(placed, axis=2).reshape(queries, blocks, tokens)
    raw = xor_sum(xor_sum(raw, "inp", inp_size), "out", out_size)
    equal = token_ids[:, :, None] == token_ids[:, None, :]
    counts = jnp.sum(equal.astype(jnp.int32), axis=2)
    weight = loss_mask.astype(jnp.float32) / counts.astype(jnp.float32)
    return raw * weight[None]


def solution(mesh):
    in_specs = (
        P("grp", "out", "inp"),
        P("grp", "inp", "out"),
        P(None, "out", "inp"),
        P("grp", None),
        P("grp", None),
    )
    out_specs = P(None, "grp", None)
    body = functools.partial(shards, mesh.shape["inp"], mesh.shape["out"])
    return jax.shard_map(body, mesh=mesh, in_specs=in_specs, out_specs=out_specs, check_vma=False)
```

time: 290 us -> 225 us (0.78)
  Pallas kernels: 0 us -> 94.4 us
  matrix products: 77.8 us -> 0 us
  waiting for transfers between devices: 150 us -> 80.8 us
  blocking collectives: 33.8 us -> 0 us
  starting transfers between devices: 0.12 us -> 14.1 us
  local copies, waits for them, and re-layouts: 6.45 us -> 9.81 us
    all_gather x4 -> x1, waiting for transfers between devices: 148 us -> 0.02 us  [shards(): gathered = lax.all_gather(activations, 'out', axis=1, tiled=True)]
    pallas_call x0 -> x5, Pallas kernels: none -> 94.4 us  [project(): pl.pallas_call(functools.partial(matmul_kernel, len(parts), before is not...]
    ppermute x0 -> x15, waiting for transfers between devices: none -> 80.7 us  [the longest x4 74.6 us: shift(): lax.ppermute(value, 'inp', [(at, (at + pair * by) % inp_size) for at in r...]
    dot_general x2 -> x0, matrix products: 77.8 us -> none  [shards(): jnp.einsum('to,qoi->tqi', lax.all_gather(out_grads[number], 'inp', axis=0...]
    psum x1 -> x0, blocking collectives: 33.8 us -> none  [shards(): partial_value = lax.psum(partial_value, ('inp', 'out'))]
    ppermute x0 -> x15, starting transfers between devices: none -> 14.1 us  [the longest x4 7.12 us: shift(): lax.ppermute(value, 'inp', [(at, (at + pair * by) % inp_size) for at in r...]
    convert_element_type x2 -> x0, other arithmetic: 8.22 us -> none  [shards(): gathered.astype(jnp.float32)[:, None, :]]
    reduce_sum x0 -> x2, other arithmetic: none -> 6.05 us  [shards(): raw.append(jnp.sum(rows * block.astype(jnp.float32)[None], axis=3))]
  transfers between devices with their start and end apart: 4 -> 16, of which waited for: 4 -> 8; matrix products, arithmetic and copies ran while one was open for 18% -> 0% of each run, Pallas kernels for 0% -> 42%
where the time goes in v1:
time: 225 us; the launch traced here: 224 us
  Pallas kernels  94.4 us (42%)
  waiting for transfers between devices  80.8 us (36%)
  starting transfers between devices  14.1 us (6%)
  between operations  13.7 us (6%)
  other arithmetic  10.7 us (5%)
  local copies, waits for them, and re-layouts  9.81 us (4%)
    pallas_call x5, Pallas kernels, project(): pl.pallas_call(functools.partial(matmul_kernel, len(parts), before is not...  94.4 us
    ppermute x4, waiting for transfers between devices, shift(): lax.ppermute(value, 'inp', [(at, (at + pair * by) % inp_size) for at in r...  74.6 us
    ppermute x4, starting transfers between devices, shift(): lax.ppermute(value, 'inp', [(at, (at + pair * by) % inp_size) for at in r...  7.12 us
    ppermute x6, starting transfers between devices, xor_sum(): lax.ppermute(value, axis, [(at, at ^ other) for at in range(size)])  6.42 us
    ppermute x6, waiting for transfers between devices, xor_sum(): lax.ppermute(value, axis, [(at, at ^ other) for at in range(size)])  6.14 us
    reduce_sum x2, other arithmetic, shards(): raw.append(jnp.sum(rows * block.astype(jnp.float32)[None], axis=3))  6.05 us
  transfers between devices with their start and end apart: 16, of which 8 were waited for; matrix products, arithmetic and copies ran while one was open for 0% of the time, Pallas kernels for 42%

profile of v1, /device:TPU:0, one launch (start us, length us, event | category | flops | bytes accessed | tf_op | source)
XLA Modules:
  0.0 223.5 jit_solution(13649495932701244781)
XLA Ops:
  6.5 3.5 %fusion.4 = (bf16[256,1792]{1,0:T(8,128)(2,1)S(1)}, bf16[256,1792]{1,0:T(8,128)(2,1)}, bf16[256,1792]{1,0:T(8,128)(2,1)S(1)}, bf16[256,1792]{1,0:T(8,128)(2,1)}) fusion(bf16[256,7168]{1,0:T(8,128)(2,1)} %bitcast.refs_0_), kind=kLoop, calls=%fused_computation.21 | loop fusion | bytes 7340032 | tf_op jit(solution)/shard_map/slice | solution.py:110
  10.1 3.0 %collective-permute-start.1 = (bf16[256,1792]{1,0:T(8,128)(2,1)S(1)}, bf16[256,1792]{1,0:T(8,128)(2,1)S(1)}, u32[]{:S(2)}, u32[]{:S(2)}) collective-permute-start(bf16[256,1792]{1,0:T(8,128)(2,1)S(1)} %get-tuple-element.19), channel_id=1, source_target_pairs={{0,8},{4,12},{8,0},{12,4},{1,9},{5,13},{9,1},{13,5},{2,10},{6,14},... | collective-permute-start | bytes 2752520 | tf_op jit(solution)/shard_map/ppermute | solution.py:105
  13.0 0.0 collective-permute-start.4
  13.1 21.1 %collective-permute-done.1.refs_0_ = bf16[256,1792]{1,0:T(8,128)(2,1)S(1)} collective-permute-done((bf16[256,1792]{1,0:T(8,128)(2,1)S(1)}, bf16[256,1792]{1,0:T(8,128)(2,1)S(1)}, u32[]{:S(2)}, u32[]{:S(2)}) %collective-permute-start.1) | collective-permute-done | bytes 917536 | tf_op jit(solution)/shard_map/ppermute | solution.py:105
  34.2 2.1 collective-permute-start.2
  36.3 17.6 %collective-permute-done.4.refs_0_ = bf16[256,1792]{1,0:T(8,128)(2,1)S(1)} collective-permute-done((bf16[256,1792]{1,0:T(8,128)(2,1)S(1)}, bf16[256,1792]{1,0:T(8,128)(2,1)S(1)}, u32[]{:S(2)}, u32[]{:S(2)}) %collective-permute-start.4) | collective-permute-done | bytes 917536 | tf_op jit(solution)/shard_map/ppermute | solution.py:105
  53.9 2.1 collective-permute-start.5
  55.9 0.0 collective-permute-start.8
  55.9 0.5 collective-permute-start
  56.4 0.0 all-gather.2.cloned.1.call-update
  56.5 0.1 collective-permute-start.7
  56.6 16.9 %collective-permute-done.2.refs_0_ = bf16[256,1792]{1,0:T(8,128)(2,1)S(1)} collective-permute-done((bf16[256,1792]{1,0:T(8,128)(2,1)}, bf16[256,1792]{1,0:T(8,128)(2,1)S(1)}, u32[]{:S(2)}, u32[]{:S(2)}) %collective-permute-start.2) | collective-permute-done | bytes 917536 | tf_op jit(solution)/shard_map/ppermute | solution.py:105
  73.5 0.0 collective-permute-start.3
  73.5 18.9 %collective-permute-done.5.refs_0_ = bf16[256,1792]{1,0:T(8,128)(2,1)} collective-permute-done((bf16[256,1792]{1,0:T(8,128)(2,1)}, bf16[256,1792]{1,0:T(8,128)(2,1)}, u32[]{:S(2)}, u32[]{:S(2)}) %collective-permute-start.5) | collective-permute-done | bytes 917536 | tf_op jit(solution)/shard_map/ppermute | solution.py:105
  92.5 0.0 collective-permute-start.6
  92.5 13.6 %project.6.refs_3_ = f32[2,512,2048]{2,1,0:T(8,128)S(1)} custom-call(bf16[256,1792]{1,0:T(8,128)(2,1)S(1)} %collective-permute-done.4.refs_0_, bf16[256,1792]{1,0:T(8,128)(2,1)} %collective-permute-done.8.refs_1_, bf16[2,7168,2048]{2,1,0:T(8,128)(2,1)} %refs_2_.9), custom_call_target="tpu_custom_call" | custom-call | flops 7516192768 | bytes 23068672 | tf_op jit(solution)/shard_map/project/pallas_call | solution.py:59
  106.1 0.0 collective-permute-done.7.refs_1_
  106.1 13.8 %project.7.refs_3_ = f32[2,512,2048]{2,1,0:T(8,128)S(1)} custom-call(bf16[256,1792]{1,0:T(8,128)(2,1)S(1)} %collective-permute-done.1.refs_0_, bf16[256,1792]{1,0:T(8,128)(2,1)} %collective-permute-done.7.refs_1_, bf16[2,7168,2048]{2,1,0:T(8,128)(2,1)} %refs_2_.9, f32[2,512,2048]{2,1,0:T(8,128)S(1)} %project.6.refs_3_), custom_call_target="tpu_custom_call", output_to_operand_aliasing={{}: (3, {})} | custom-call | flops 7516192768 | bytes 31457280 | tf_op jit(solution)/shard_map/project/pallas_call | solution.py:59
  119.9 0.0 collective-permute-done.6.refs_1_
  119.9 13.5 %project.8.refs_3_ = f32[2,512,2048]{2,1,0:T(8,128)S(1)} custom-call(bf16[256,1792]{1,0:T(8,128)(2,1)} %collective-permute-done.5.refs_0_, bf16[256,1792]{1,0:T(8,128)(2,1)S(1)} %collective-permute-done.6.refs_1_, bf16[2,7168,2048]{2,1,0:T(8,128)(2,1)} %refs_2_.9, f32[2,512,2048]{2,1,0:T(8,128)S(1)} %project.7.refs_3_), custom_call_target="tpu_custom_call", output_to_operand_aliasing={{}: (3, {})} | custom-call | flops 7516192768 | bytes 31457280 | tf_op jit(solution)/shard_map/project/pallas_call | solution.py:59
  133.5 0.0 collective-permute-done.3.refs_1_
  133.5 12.7 %project.9 = f32[2,512,2048]{2,1,0:T(8,128)S(1)} custom-call(bf16[256,1792]{1,0:T(8,128)(2,1)S(1)} %collective-permute-done.2.refs_0_, bf16[256,1792]{1,0:T(8,128)(2,1)S(1)} %collective-permute-done.3.refs_1_, bf16[2,7168,2048]{2,1,0:T(8,128)(2,1)} %refs_2_.9, f32[2,512,2048]{2,1,0:T(8,128)S(1)} %project.8.refs_3_), custom_call_target="tpu_custom_call", output_to_operand_aliasing={{}: (3, {})} | custom-call | flops 7516192768 | bytes 31457280 | tf_op jit(solution)/shard_map/project/pallas_call | solution.py:59
  146.1 3.2 %copy-done = f32[2,512,2048]{2,1,0:T(8,128)} copy-done((f32[2,512,2048]{2,1,0:T(8,128)}, f32[2,512,2048]{2,1,0:T(8,128)S(1)}, u32[]{:S(2)}) %copy-start) | copy-done | bytes 8388632
  149.4 40.8 %project.5 = f32[2,512,2048]{2,1,0:T(8,128)} custom-call(bf16[256,7168]{1,0:T(8,128)(2,1)} %bitcast.refs_0_, bf16[256,7168]{1,0:T(8,128)(2,1)} %collective-permute-done.refs_1_, bf16[2,7168,2048]{2,1,0:T(8,128)(2,1)} %refs_2_.9), custom_call_target="tpu_custom_call" | custom-call | flops 30064771072 | bytes 67108864 | tf_op jit(solution)/shard_map/project/pallas_call | solution.py:59
  190.2 0.0 all-gather.2.cloned.1.call-done
  190.2 0.0 slice-start
  190.2 2.9 %constant_dynamic-slice_fusion.2 = (bf16[2,128,2048]{2,1,0:T(8,128)(2,1)S(1)}, bf16[2,128,2048]{2,1,0:T(8,128)(2,1)S(1)}, bf16[2,128,2048]{2,1,0:T(8,128)(2,1)S(1)}, bf16[2,128,2048]{2,1,0:T(8,128)(2,1)S(1)}) fusion(bf16[2,512,2048]{2,1,0:T(8,128)(2,1)} %all-gather.2.cloned.1.call-done, s32[]{:T(128)S(6)} %select_n.258, s32[]{:T(128)S(6)} %select_n.265, ...), kind=kLoop, calls=%fused_computation.19 | loop fusion | bytes 8388624 | tf_op jit(solution)/shard_map/dynamic_slice | solution.py:135
  193.2 0.0 slice-start.1
  193.2 0.2 convert.6
  193.4 1.6 convert.7
  195.0 0.2 convert.4
  195.2 1.6 convert.5
  196.8 3.3 %fusion.1 = (f32[2,256]{1,0:T(2,128)S(1)}, f32[2,256]{1,0:T(2,128)S(1)}) fusion(f32[2,512,2048]{2,1,0:T(8,128)S(1)} %bitcast.10, f32[256,2048]{1,0:T(8,128)S(1)} %convert.6, f32[256,2048]{1,0:T(8,128)} %convert.7), kind=kLoop, calls=%fused_computation.3 | loop fusion | flops 4193280 | bytes 12587008 | tf_op jit(solution)/shard_map/reduce_sum | solution.py:139
  200.1 0.0 slice-done.3
  200.1 2.8 %fusion.3 = (f32[2,256]{1,0:T(2,128)S(1)}, f32[2,256]{1,0:T(2,128)S(1)}) fusion(f32[2,512,2048]{2,1,0:T(8,128)S(1)} %bitcast.12, f32[256,2048]{1,0:T(8,128)S(1)} %convert.4, f32[256,2048]{1,0:T(8,128)} %convert.5), kind=kLoop, calls=%fused_computation.7 | loop fusion | flops 4193280 | bytes 12587008 | tf_op jit(solution)/shard_map/reduce_sum | solution.py:139
  203.1 1.8 collective-permute-start.10
  204.9 0.2 collective-permute-start.11
  205.1 0.2 collective-permute-start.9
  205.3 0.4 convert_reduce_fusion
  205.7 1.1 collective-permute-done.10
  206.8 1.2 collective-permute-done.11
  208.0 0.0 collective-permute-done.9
  208.0 2.6 %collective-permute-start.13 = (f32[2,2,512]{2,1,0:T(2,128)S(1)}, f32[2,2,512]{2,1,0:T(2,128)S(1)}, u32[]{:S(2)}, u32[]{:S(2)}) collective-permute-start(f32[2,2,512]{2,1,0:T(2,128)S(1)} %add_add_fusion), channel_id=1, source_target_pairs={{0,2},{1,3},{2,0},{3,1},{4,6},{5,7},{6,4},{7,5},{8,10},{9,11},{10,... | collective-permute-start | bytes 24584 | tf_op jit(solution)/shard_map/ppermute | solution.py:85
  210.6 1.3 collective-permute-start.14
  212.0 0.2 collective-permute-start.12
  212.2 0.4 collective-permute-done.13
  212.6 3.5 %collective-permute-done.14 = f32[2,2,512]{2,1,0:T(2,128)S(1)} collective-permute-done((f32[2,2,512]{2,1,0:T(2,128)S(1)}, f32[2,2,512]{2,1,0:T(2,128)S(1)}, u32[]{:S(2)}, u32[]{:S(2)}) %collective-permute-start.14) | collective-permute-done | bytes 8224 | tf_op jit(solution)/shard_map/ppermute | solution.py:85
  216.1 0.6 add_multiply_fusion
  (26 shorter events, 0.2 us)
Async XLA Ops:
  6.5 183.7 %all-gather.2.cloned.1.call-start = ((), (), s32[]{:S(2)}) async-start(), calls=%async_computation | async-start | bytes 5242880 | tf_op jit(solution)/shard_map/all_gather | solution.py:115
  10.1 24.1 %collective-permute-start.1 = (bf16[256,1792]{1,0:T(8,128)(2,1)S(1)}, bf16[256,1792]{1,0:T(8,128)(2,1)S(1)}, u32[]{:S(2)}, u32[]{:S(2)}) collective-permute-start(bf16[256,1792]{1,0:T(8,128)(2,1)S(1)} %get-tuple-element.19), channel_id=1, source_target_pairs={{0,8},{4,12},{8,0},{12,4},{1,9},{5,13},{9,1},{13,5},{2,10},{6,14},... | collective-permute-start | bytes 2752520 | tf_op jit(solution)/shard_map/ppermute | solution.py:105
  13.0 40.8 %collective-permute-start.4 = (bf16[256,1792]{1,0:T(8,128)(2,1)S(1)}, bf16[256,1792]{1,0:T(8,128)(2,1)S(1)}, u32[]{:S(2)}, u32[]{:S(2)}) collective-permute-start(bf16[256,1792]{1,0:T(8,128)(2,1)S(1)} %get-tuple-element.17), channel_id=1, source_target_pairs={{0,8},{4,12},{8,0},{12,4},{1,9},{5,13},{9,1},{13,5},{2,10},{6,14},... | collective-permute-start | bytes 2752520 | tf_op jit(solution)/shard_map/ppermute | solution.py:105
  34.2 39.3 %collective-permute-start.2 = (bf16[256,1792]{1,0:T(8,128)(2,1)}, bf16[256,1792]{1,0:T(8,128)(2,1)S(1)}, u32[]{:S(2)}, u32[]{:S(2)}) collective-permute-start(bf16[256,1792]{1,0:T(8,128)(2,1)} %get-tuple-element.7), channel_id=1, source_target_pairs={{0,8},{4,12},{8,0},{12,4},{1,9},{5,13},{9,1},{13,5},{2,10},{6,14},... | collective-permute-start | bytes 2752520 | tf_op jit(solution)/shard_map/ppermute | solution.py:105
  53.9 38.6 %collective-permute-start.5 = (bf16[256,1792]{1,0:T(8,128)(2,1)}, bf16[256,1792]{1,0:T(8,128)(2,1)}, u32[]{:S(2)}, u32[]{:S(2)}) collective-permute-start(bf16[256,1792]{1,0:T(8,128)(2,1)} %get-tuple-element.8), channel_id=1, source_target_pairs={{0,8},{4,12},{8,0},{12,4},{1,9},{5,13},{9,1},{13,5},{2,10},{6,14},... | collective-permute-start | bytes 2752520 | tf_op jit(solution)/shard_map/ppermute | solution.py:105
  55.9 36.5 %collective-permute-start.8 = (bf16[256,1792]{1,0:T(8,128)(2,1)S(1)}, bf16[256,1792]{1,0:T(8,128)(2,1)}, u32[]{:S(2)}, u32[]{:S(2)}) collective-permute-start(bf16[256,1792]{1,0:T(8,128)(2,1)S(1)} %collective-permute-done.4.refs_0_), channel_id=1, source_target_pairs={{0,4},{4,0},{8,12},{12,8},{1,5},{5,1},{9,13},{13,9},{2,6},{6,2},{1... | collective-permute-start | bytes 2752520 | tf_op jit(solution)/shard_map/ppermute | solution.py:102
  55.9 93.5 %collective-permute-start = (bf16[256,7168]{1,0:T(8,128)(2,1)}, bf16[256,7168]{1,0:T(8,128)(2,1)}, u32[]{:S(2)}, u32[]{:S(2)}) collective-permute-start(bf16[256,7168]{1,0:T(8,128)(2,1)} %bitcast.refs_0_), channel_id=1, source_target_pairs={{0,4},{4,0},{8,12},{12,8},{1,5},{5,1},{9,13},{13,9},{2,6},{6,2},{1... | collective-permute-start | bytes 11010056 | tf_op jit(solution)/shard_map/ppermute | solution.py:102
  56.5 49.7 %collective-permute-start.7 = (bf16[256,1792]{1,0:T(8,128)(2,1)S(1)}, bf16[256,1792]{1,0:T(8,128)(2,1)}, u32[]{:S(2)}, u32[]{:S(2)}) collective-permute-start(bf16[256,1792]{1,0:T(8,128)(2,1)S(1)} %collective-permute-done.1.refs_0_), channel_id=1, source_target_pairs={{0,4},{4,0},{8,12},{12,8},{1,5},{5,1},{9,13},{13,9},{2,6},{6,2},{1... | collective-permute-start | bytes 2752520 | tf_op jit(solution)/shard_map/ppermute | solution.py:102
  73.5 59.9 %collective-permute-start.3 = (bf16[256,1792]{1,0:T(8,128)(2,1)S(1)}, bf16[256,1792]{1,0:T(8,128)(2,1)S(1)}, u32[]{:S(2)}, u32[]{:S(2)}) collective-permute-start(bf16[256,1792]{1,0:T(8,128)(2,1)S(1)} %collective-permute-done.2.refs_0_), channel_id=1, source_target_pairs={{0,4},{4,0},{8,12},{12,8},{1,5},{5,1},{9,13},{13,9},{2,6},{6,2},{1... | collective-permute-start | bytes 2752520 | tf_op jit(solution)/shard_map/ppermute | solution.py:102
  92.5 27.4 %collective-permute-start.6 = (bf16[256,1792]{1,0:T(8,128)(2,1)}, bf16[256,1792]{1,0:T(8,128)(2,1)S(1)}, u32[]{:S(2)}, u32[]{:S(2)}) collective-permute-start(bf16[256,1792]{1,0:T(8,128)(2,1)} %collective-permute-done.5.refs_0_), channel_id=1, source_target_pairs={{0,4},{4,0},{8,12},{12,8},{1,5},{5,1},{9,13},{13,9},{2,6},{6,2},{1... | collective-permute-start | bytes 2752520 | tf_op jit(solution)/shard_map/ppermute | solution.py:102
  146.1 3.2 %copy-start = (f32[2,512,2048]{2,1,0:T(8,128)}, f32[2,512,2048]{2,1,0:T(8,128)S(1)}, u32[]{:S(2)}) copy-start(f32[2,512,2048]{2,1,0:T(8,128)S(1)} %project.9) | copy-start | bytes 25165828
  190.2 6.6 %slice-start = ((s8[8388608]{0:T(1024)(128)(4,1)}), s8[4194304]{0:T(1024)(128)(4,1)S(1)}, s32[]{:S(2)}) async-start(s8[8388608]{0:T(1024)(128)(4,1)} %bitcast.9), calls=%async_computation.1 | async-start | bytes 8388608
  193.2 3.7 %slice-start.1 = ((s8[8388608]{0:T(1024)(128)(4,1)}), s8[4194304]{0:T(1024)(128)(4,1)S(1)}, s32[]{:S(2)}) async-start(s8[8388608]{0:T(1024)(128)(4,1)} %bitcast.9), calls=%async_computation.2 | async-start | bytes 8388608
  195.2 4.9 %slice-start.2 = ((s8[8388608]{0:T(1024)(128)(4,1)}), s8[4194304]{0:T(1024)(128)(4,1)S(1)}, s32[]{:S(2)}) async-start(s8[8388608]{0:T(1024)(128)(4,1)} %bitcast.11), calls=%async_computation.3 | async-start | bytes 8388608
  196.8 3.3 %slice-start.3 = ((s8[8388608]{0:T(1024)(128)(4,1)}), s8[4194304]{0:T(1024)(128)(4,1)S(1)}, s32[]{:S(2)}) async-start(s8[8388608]{0:T(1024)(128)(4,1)} %bitcast.11), calls=%async_computation.4 | async-start | bytes 8388608
  200.1 5.1 %copy-start.1 = (s32[2,512]{1,0:T(2,128)S(1)}, s32[2,512]{1,0:T(2,128)}, u32[]{:S(2)}) copy-start(s32[2,512]{1,0:T(2,128)} %param.8) | copy-start | bytes 12292
  200.1 12.0 %copy-start.2 = (s32[2,512]{1,0:T(2,128)S(1)}, s32[2,512]{1,0:T(2,128)}, u32[]{:S(2)}) copy-start(s32[2,512]{1,0:T(2,128)} %param.9) | copy-start | bytes 12292
  203.1 3.7 %collective-permute-start.10 = (f32[2,2,512]{2,1,0:T(2,128)S(1)}, f32[2,2,512]{2,1,0:T(2,128)S(1)}, u32[]{:S(2)}, u32[]{:S(2)}) collective-permute-start(f32[2,2,512]{2,1,0:T(2,128)S(1)} %reshape.306), channel_id=1, source_target_pairs={{0,8},{4,12},{8,0},{12,4},{1,9},{5,13},{9,1},{13,5},{2,10},{6,14},... | collective-permute-start | bytes 24584 | tf_op jit(solution)/shard_map/ppermute | solution.py:85
  204.9 3.1 %collective-permute-start.11 = (f32[2,2,512]{2,1,0:T(2,128)S(1)}, f32[2,2,512]{2,1,0:T(2,128)S(1)}, u32[]{:S(2)}, u32[]{:S(2)}) collective-permute-start(f32[2,2,512]{2,1,0:T(2,128)S(1)} %reshape.306), channel_id=1, source_target_pairs={{0,12},{4,8},{8,4},{12,0},{1,13},{5,9},{9,5},{13,1},{2,14},{6,10},... | collective-permute-start | bytes 24584 | tf_op jit(solution)/shard_map/ppermute | solution.py:85
  205.1 2.9 %collective-permute-start.9 = (f32[2,2,512]{2,1,0:T(2,128)S(1)}, f32[2,2,512]{2,1,0:T(2,128)S(1)}, u32[]{:S(2)}, u32[]{:S(2)}) collective-permute-start(f32[2,2,512]{2,1,0:T(2,128)S(1)} %reshape.306), channel_id=1, source_target_pairs={{0,4},{4,0},{8,12},{12,8},{1,5},{5,1},{9,13},{13,9},{2,6},{6,2},{1... | collective-permute-start | bytes 24584 | tf_op jit(solution)/shard_map/ppermute | solution.py:85
  208.0 4.6 %collective-permute-start.13 = (f32[2,2,512]{2,1,0:T(2,128)S(1)}, f32[2,2,512]{2,1,0:T(2,128)S(1)}, u32[]{:S(2)}, u32[]{:S(2)}) collective-permute-start(f32[2,2,512]{2,1,0:T(2,128)S(1)} %add_add_fusion), channel_id=1, source_target_pairs={{0,2},{1,3},{2,0},{3,1},{4,6},{5,7},{6,4},{7,5},{8,10},{9,11},{10,... | collective-permute-start | bytes 24584 | tf_op jit(solution)/shard_map/ppermute | solution.py:85
  210.6 5.4 %collective-permute-start.14 = (f32[2,2,512]{2,1,0:T(2,128)S(1)}, f32[2,2,512]{2,1,0:T(2,128)S(1)}, u32[]{:S(2)}, u32[]{:S(2)}) collective-permute-start(f32[2,2,512]{2,1,0:T(2,128)S(1)} %add_add_fusion), channel_id=1, source_target_pairs={{0,3},{1,2},{2,1},{3,0},{4,7},{5,6},{6,5},{7,4},{8,11},{9,10},{10,... | collective-permute-start | bytes 24584 | tf_op jit(solution)/shard_map/ppermute | solution.py:85
  212.0 4.1 %collective-permute-start.12 = (f32[2,2,512]{2,1,0:T(2,128)S(1)}, f32[2,2,512]{2,1,0:T(2,128)S(1)}, u32[]{:S(2)}, u32[]{:S(2)}) collective-permute-start(f32[2,2,512]{2,1,0:T(2,128)S(1)} %add_add_fusion), channel_id=1, source_target_pairs={{0,1},{1,0},{2,3},{3,2},{4,5},{5,4},{6,7},{7,6},{8,9},{9,8},{10,11... | collective-permute-start | bytes 24584 | tf_op jit(solution)/shard_map/ppermute | solution.py:85
Sparse Core Ops, SparseCore 0:
  56.6 81.0 all-gather.1

commit v2 on v0

v2 whole, which is shorter than its diff:
```python
import functools

import jax
import jax.numpy as jnp
from jax import lax
from jax.experimental import pallas as pl
from jax.experimental.pallas import tpu as pltpu
from jax.sharding import PartitionSpec as P

WEIGHTS = (8, 8, 6, 3, 3)
GROUPS = (2, 2, 1)
HELPER_VMEM = 1024 * 1024


def tile_of(length, most):
    size = min(length, most)
    while length % size:
        size -= 128
    return size


def project_kernel(parts, begin, query, fresh, keep, passes, tile, *refs):
    g_refs, q_ref = refs[:parts], refs[parts]
    if keep:
        sum_ref, mark_ref, x_ref, sems = refs[-4:]
    elif parts == 1:
        x_ref, (sum_ref, mark_ref) = g_refs[0], refs[-2:]
    else:
        sum_ref, mark_ref, x_ref, sems = refs[-4:]
    depth = x_ref.shape[1]
    queries, total, width = sum_ref.shape
    copies = []
    if parts > 1:
        rows = g_refs[0].shape[0]
        together = total // rows
        for at, g_ref in enumerate(g_refs):
            row, column = at % together, sum(ref.shape[1] for ref in g_refs[:at // together * together:together])
            where = x_ref.at[pl.ds(row * rows, rows), pl.ds(column, g_ref.shape[1])]
            copies.append(pltpu.make_async_copy(g_ref, where, sems.at[at]))
    for copy in copies:
        copy.start()
    mark_ref[...] = jnp.zeros_like(mark_ref)
    part = depth // passes

    def step(block_ref):
        number, at, turn = pl.program_id(0), pl.program_id(1), pl.program_id(2)

        if copies:

            @pl.when((number == 0) & (at == 0) & (turn == 0))
            def _():
                for copy in copies:
                    copy.wait()

        columns = pl.ds(pl.multiple_of(turn * part, part), part)
        product = jnp.dot(x_ref[:, columns], block_ref[0], preferred_element_type=jnp.float32)
        where = (number, slice(None), pl.ds(pl.multiple_of(at * tile, tile), tile))
        if not fresh:
            sum_ref[where] += product
        elif passes == 1:
            sum_ref[where] = product
        else:

            @pl.when(turn == 0)
            def _():
                sum_ref[where] = product

            @pl.when(turn > 0)
            def _():
                sum_ref[where] += product

    pltpu.emit_pipeline(
        step,
        grid=(queries, width // tile, passes),
        in_specs=[pl.BlockSpec((1, part, tile), lambda q, i, k: (q, k, i))],
    )(q_ref.at[pl.ds(query, queries), pl.ds(begin, depth), :])


def project(spans, query_grads, begin, query, queries, running, passes, tile, others=(), keep=False):
    parts = [part for span in spans for part in span]
    rows = parts[0].shape[0]
    depth = sum(span[0].shape[1] for span in spans)
    width = query_grads.shape[2]
    total = rows * len(spans[0])
    fresh = running is None
    laid = len(parts) == 1
    any_spec = pl.BlockSpec(memory_space=pl.ANY)
    vmem_spec = pl.BlockSpec(memory_space=pltpu.VMEM)
    out_shape = [
        jax.ShapeDtypeStruct((queries, total, width), jnp.float32),
        jax.ShapeDtypeStruct((8, 128), jnp.float32),
    ]
    if keep:
        out_shape.append(jax.ShapeDtypeStruct((total, depth), jnp.bfloat16))
    scratch = [] if laid or keep else [pltpu.VMEM((total, depth), jnp.bfloat16)]
    if not laid:
        scratch.append(pltpu.SemaphoreType.DMA((len(parts),)))
    return pl.pallas_call(
        functools.partial(project_kernel, len(parts), begin, query, fresh, keep, passes, tile_of(width, tile)),
        in_specs=[vmem_spec if laid else any_spec] * len(parts)
        + [any_spec, any_spec if fresh else vmem_spec]
        + [any_spec] * len(others),
        out_specs=[vmem_spec] * len(out_shape),
        out_shape=out_shape,
        scratch_shapes=scratch,
        input_output_aliases={} if fresh else {len(parts) + 1: 0},
        cost_estimate=pl.CostEstimate(flops=1024, bytes_accessed=1024, transcendentals=0),
        compiler_params=pltpu.CompilerParams(vmem_limit_bytes=26 * 1024 * 1024),
        name="project",
    )(*parts, query_grads, query_grads if fresh else running, *others)


def score_kernel(inp_size, pair, queries, ring, *refs):
    near_refs, refs = refs[:queries], refs[queries:]
    if inp_size > pair:
        far_ref, refs = refs[0], refs[1:]
    *a_refs, out_ref, held, sems = refs
    blocks, shard, width = held.shape[1:]
    me, here = lax.axis_index("inp"), lax.axis_index("out")
    sources = []
    for number in range(inp_size):
        by, other = divmod(number, pair)
        source = lax.rem(me - pair * by + inp_size, inp_size)
        sources.append(jnp.bitwise_xor(source, other) if pair == 2 else source)
    for number, source in enumerate(sources):
        if len(a_refs) == 1:
            begin = pl.multiple_of(source * shard, shard)
            pltpu.make_async_copy(
                a_refs[0].at[:, pl.ds(begin, shard), :], held.at[number], sems.at[number]
            ).start()
            continue
        for at, a_ref in enumerate(a_refs):
            for place, spot in enumerate(ring):

                @pl.when((here == spot) & (source == ring[place - at]))
                def _(a_ref=a_ref, number=number):
                    pltpu.make_async_copy(a_ref, held.at[number], sems.at[number]).start()

    lanes = 128
    for number, source in enumerate(sources):
        pltpu.make_async_copy(held.at[number], held.at[number], sems.at[number]).wait()
        for query in range(queries):
            total = None
            for at in range(0, width, lanes):
                block = held[number, :, :, at:at + lanes].reshape(blocks * shard, lanes).astype(jnp.float32)
                begin = (number if number < pair else number - pair) * blocks * shard
                where = (query, slice(begin, begin + blocks * shard), slice(at, at + lanes))
                rows = near_refs[query][(0, *where[1:])] if number < pair else far_ref[where]
                term = rows * block
                total = term if total is None else total + term
            out_ref[source, query, :] = jnp.sum(total.T, axis=0)


def score(sums, slots, ring, inp_size, pair, queries, blocks, shard):
    width = sums[0].shape[2]
    return pl.pallas_call(
        functools.partial(score_kernel, inp_size, pair, queries, ring),
        in_specs=[pl.BlockSpec(memory_space=pltpu.VMEM)] * len(sums)
        + [pl.BlockSpec(memory_space=pl.ANY)] * len(slots),
        out_specs=pl.BlockSpec(memory_space=pltpu.VMEM),
        out_shape=jax.ShapeDtypeStruct((inp_size, queries, blocks * shard), jnp.float32),
        scratch_shapes=[
            pltpu.VMEM((inp_size, blocks, shard, width), jnp.bfloat16),
            pltpu.SemaphoreType.DMA((inp_size,)),
        ],
        compiler_params=pltpu.CompilerParams(vmem_limit_bytes=10 * 1024 * 1024),
        name="score",
    )(*sums, *slots)


def xor_sum(value, axis, size):
    if size & (size - 1):
        return lax.psum(value, axis)
    terms = [value]
    for other in range(1, size):
        terms.append(lax.ppermute(value, axis, [(at, at ^ other) for at in range(size)]))
    while len(terms) > 1:
        terms = [terms[at] + terms[at + 1] for at in range(0, len(terms), 2)]
    return terms[0]


def after(value, *others):
    any_spec = pl.BlockSpec(memory_space=pl.ANY)
    return pl.pallas_call(
        lambda *refs: None,
        in_specs=[any_spec] * (1 + len(others)),
        out_specs=any_spec,
        out_shape=jax.ShapeDtypeStruct(value.shape, value.dtype),
        input_output_aliases={0: 0},
        compiler_params=pltpu.CompilerParams(vmem_limit_bytes=HELPER_VMEM),
        name="after",
    )(pltpu.with_memory_space_constraint(value, pltpu.VMEM), *others)


def in_hbm(value):
    return pltpu.with_memory_space_constraint(value, pltpu.HBM)


def cut_kernel(spans, source_ref, *refs):
    copies = []
    for at, (begin, length) in enumerate(spans):
        copies.append(pltpu.make_async_copy(source_ref.at[:, pl.ds(begin, length)], refs[at], refs[-1].at[at]))
    for copy in copies:
        copy.start()
    for copy in copies:
        copy.wait()


def cut(source, spans):
    return pl.pallas_call(
        functools.partial(cut_kernel, spans),
        in_specs=[pl.BlockSpec(memory_space=pl.ANY)],
        out_specs=[pl.BlockSpec(memory_space=pltpu.VMEM)] * len(spans),
        out_shape=[jax.ShapeDtypeStruct((source.shape[0], length), source.dtype) for _, length in spans],
        scratch_shapes=[pltpu.SemaphoreType.DMA((len(spans),))],
        compiler_params=pltpu.CompilerParams(vmem_limit_bytes=HELPER_VMEM),
        name="cut",
    )(source)


def shards(inp_size, out_size, activations, out_grads, query_grads, token_ids, loss_mask):
    blocks, shard, depth = out_grads.shape
    queries, _, width = query_grads.shape
    tokens = token_ids.shape[1]
    pair = 2 if inp_size % 2 == 0 else 1
    chips = inp_size // pair
    rows = blocks * shard

    unit = 256 if depth % 256 == 0 else depth
    units = depth // unit
    edges = [0]
    for at in range(len(WEIGHTS)):
        edges.append(units * sum(WEIGHTS[:at + 1]) // sum(WEIGHTS) * unit)
    spans = [(begin, end - begin) for begin, end in zip(edges, edges[1:]) if end > begin]
    chunks = len(spans)

    def flip(value):
        return lax.ppermute(value, "inp", [(at, at ^ 1) for at in range(inp_size)])

    def shift(value, by):
        return lax.ppermute(value, "inp", [(at, (at + pair * by) % inp_size) for at in range(inp_size)])

    own = in_hbm(out_grads.reshape(rows, depth))
    near = [own] + ([pltpu.with_memory_space_constraint(flip(own), pltpu.VMEM)] if pair == 2 else [])
    query_grads = in_hbm(query_grads)
    activations = in_hbm(activations)
    line = inp_size == out_size and activations.shape[1] == shard
    ring = list(range(0, out_size, 2)) + list(range(1, out_size, 2))[::-1]
    turn = [(ring[at - 1], ring[at]) for at in range(out_size)]
    slots = [activations]
    if not line:
        slots = [lax.all_gather(activations, "out", axis=1, tiled=True)]
    elif out_size > 1:
        slots.append(lax.ppermute(activations, "out", turn))

    pieces_out = cut(own, spans) if chips > 1 else []

    def send(chunk):
        return [shift(pieces_out[chunk], by) for by in range(1, chips)]

    settled = [1]

    def step_along(mark):
        if not line or settled[0] == out_size:
            return []
        settled[0] += 1
        slots[-1] = after(slots[-1], mark)
        if len(slots) < out_size:
            slots.append(lax.ppermute(slots[-1], "out", turn))
            return [slots[-2]]
        return [slots[-1]]

    coming = [send(chunk) for chunk in range(chunks)] if chips > 1 else []
    waiting = []

    def receive(mark, count=1):
        pieces = []
        for _ in range(min(count, len(coming))):
            arrived = [after(piece, mark) for piece in coming.pop(0)]
            waiting.append(sum([[piece, flip(piece)] if pair == 2 else [piece] for piece in arrived], []))
            pieces += arrived
        return pieces

    sums = []
    held = near
    for query in range(queries):
        others = []
        if query > 0:
            others = receive(mark) + (step_along(mark) if query == 1 else [])
        near_sum, mark, *kept = project([held], query_grads, 0, query, 1, None, 1, 512, others, len(held) > 1)
        held = kept or [after(held[0], mark)]
        sums.append(near_sum)
    running = None
    done = 0
    counts = list(GROUPS)
    while coming or waiting:
        count = counts.pop(0) if counts else len(coming)
        others = receive(mark, count - len(waiting)) + step_along(mark)
        depth_now = sum(length for _, length in spans[done:done + len(waiting)])
        running, mark = project(
            waiting, query_grads, spans[done][0], 0, queries, running, 1, 2048 if depth_now <= 1024 else 1024, others
        )
        done += len(waiting)
        waiting.clear()
    if running is not None:
        sums.append(running)
    raw = score(sums, slots, ring, inp_size, pair, queries, blocks, shard)
    raw = raw.reshape(inp_size, queries, blocks, shard).transpose(1, 2, 0, 3).reshape(queries, blocks, tokens)
    raw = xor_sum(xor_sum(raw, "inp", inp_size), "out", out_size)
    equal = token_ids[:, :, None] == token_ids[:, None, :]
    counts = jnp.sum(equal.astype(jnp.int32), axis=2)
    weight = loss_mask.astype(jnp.float32) / counts.astype(jnp.float32)
    return raw * weight[None]


def solution(mesh):
    in_specs = (
        P("grp", "out", "inp"),
        P("grp", "inp", "out"),
        P(None, "out", "inp"),
        P("grp", None),
        P("grp", None),
    )
    out_specs = P(None, "grp", None)
    body = functools.partial(shards, mesh.shape["inp"], mesh.shape["out"])
    return jax.shard_map(body, mesh=mesh, in_specs=in_specs, out_specs=out_specs, check_vma=False)
```

time: 290 us -> 121 us (0.42)
  waiting for transfers between devices: 150 us -> 13 us
  Pallas kernels: 0 us -> 85.7 us
  matrix products: 77.8 us -> 0 us
  blocking collectives: 33.8 us -> 0 us
  starting transfers between devices: 0.12 us -> 20.9 us
  between operations: 13.2 us -> 0.16 us
  other arithmetic: 9.25 us -> 1.03 us
  local copies, waits for them, and re-layouts: 6.45 us -> 0.04 us
    all_gather x4 -> x0, waiting for transfers between devices: 148 us -> none  [the longest x2 85 us: shards(): gathered = lax.all_gather(activations[number], 'out', axis=0, tiled=True)]
    pallas_call x0 -> x15, Pallas kernels: none -> 85.7 us  [the longest x5 80.2 us: project(): pl.pallas_call(functools.partial(project_kernel, len(parts), begin, query...]
    dot_general x2 -> x0, matrix products: 77.8 us -> none  [shards(): jnp.einsum('to,qoi->tqi', lax.all_gather(out_grads[number], 'inp', axis=0...]
    psum x1 -> x0, blocking collectives: 33.8 us -> none  [shards(): partial_value = lax.psum(partial_value, ('inp', 'out'))]
    ppermute x0 -> x20, starting transfers between devices: none -> 20.9 us  [the longest x5 6.66 us: shift(): lax.ppermute(value, 'inp', [(at, (at + pair * by) % inp_size) for at in r...]
    ppermute x0 -> x20, waiting for transfers between devices: none -> 13 us  [the longest x5 5.66 us: shift(): lax.ppermute(value, 'inp', [(at, (at + pair * by) % inp_size) for at in r...]
    convert_element_type x2 -> x0, other arithmetic: 8.22 us -> none  [shards(): gathered.astype(jnp.float32)[:, None, :]]
    slice x2 -> x0, local copies, waits for them, and re-layouts: 6.44 us -> none  [the longest x1 4.12 us: shards(): out_grads[number]]
  transfers between devices with their start and end apart: 4 -> 20, of which waited for: 4 -> 9; matrix products, arithmetic and copies ran while one was open for 18% -> 0% of each run, Pallas kernels for 0% -> 63%
where the time goes in v2:
time: 121 us
  Pallas kernels  85.7 us (71%)
  starting transfers between devices  20.9 us (17%)
  waiting for transfers between devices  13 us (11%)
    pallas_call x5, Pallas kernels, project(): pl.pallas_call(functools.partial(project_kernel, len(parts), begin, query...  80.2 us
    ppermute x5, starting transfers between devices, shift(): lax.ppermute(value, 'inp', [(at, (at + pair * by) % inp_size) for at in r...  6.66 us
    ppermute x6, starting transfers between devices, xor_sum(): lax.ppermute(value, axis, [(at, at ^ other) for at in range(size)])  5.76 us
    ppermute x5, waiting for transfers between devices, shift(): lax.ppermute(value, 'inp', [(at, (at + pair * by) % inp_size) for at in r...  5.66 us
    ppermute x6, waiting for transfers between devices, xor_sum(): lax.ppermute(value, axis, [(at, at ^ other) for at in range(size)])  5.58 us
    ppermute x2, starting transfers between devices, step_along(): slots.append(lax.ppermute(slots[-1], 'out', turn))  4.14 us
    ppermute x1, starting transfers between devices, shards(): slots.append(lax.ppermute(activations, 'out', turn))  3.59 us
    pallas_call x1, Pallas kernels, score(): pl.pallas_call(functools.partial(score_kernel, inp_size, pair, queries, r...  3.46 us
  transfers between devices with their start and end apart: 20, of which 9 were waited for; matrix products, arithmetic and copies ran while one was open for 0% of the time, Pallas kernels for 63%

profile of v2, /device:TPU:0, one launch (start us, length us, event | category | flops | bytes accessed | tf_op | source)
XLA Modules:
  0.0 120.8 jit_solution(10823198834010393716)
XLA Ops:
  0.0 0.5 collective-permute-start
  0.5 3.6 %collective-permute-start.2 = (bf16[2,128,2048]{2,1,0:T(8,128)(2,1)}, bf16[2,128,2048]{2,1,0:T(8,128)(2,1)S(1)}, u32[]{:S(2)}, u32[]{:S(2)}) collective-permute-start(bf16[2,128,2048]{2,1,0:T(8,128)(2,1)} %refs_3_.3), channel_id=1, source_target_pairs={{1,0},{0,2},{2,3},{3,1},{5,4},{4,6},{6,7},{7,5},{9,8},{8,10},{10,1... | collective-permute-start | bytes 3145736 | tf_op jit(solution)/shard_map/ppermute | solution.py:254
  4.0 2.0 %cut.1 = (bf16[256,2048]{1,0:T(8,128)(2,1)S(1)}, bf16[256,2048]{1,0:T(8,128)(2,1)S(1)}, bf16[256,1536]{1,0:T(8,128)(2,1)S(1)}, bf16[256,768]{1,0:T(8,128)(2,1)S(1)}, bf16[256,768]{1,0:T(8,128)(2,1)S(1)}) custom-call(bf16[256,7168]{1,0:T(8,128)(2,1)} %bitcast.12), custom_call_target="tpu_custom_call" | custom-call | tf_op jit(solution)/shard_map/cut/pallas_call | solution.py:210
  6.1 1.6 %collective-permute-start.1 = (bf16[256,2048]{1,0:T(8,128)(2,1)S(1)}, bf16[256,2048]{1,0:T(8,128)(2,1)S(1)}, u32[]{:S(2)}, u32[]{:S(2)}) collective-permute-start(bf16[256,2048]{1,0:T(8,128)(2,1)S(1)} %get-tuple-element.22), channel_id=1, source_target_pairs={{0,8},{4,12},{8,0},{12,4},{1,9},{5,13},{9,1},{13,5},{2,10},{6,14},... | collective-permute-start | bytes 3145736 | tf_op jit(solution)/shard_map/ppermute | solution.py:241
  7.7 0.5 collective-permute-start.6
  8.2 0.0 collective-permute-done.refs_1_
  8.2 20.2 %project.5 = (f32[1,512,2048]{2,1,0:T(8,128)S(1)}, f32[8,128]{1,0:T(8,128)S(1)}, bf16[512,7168]{1,0:T(8,128)(2,1)S(1)}) custom-call(bf16[256,7168]{1,0:T(8,128)(2,1)} %bitcast.13, bf16[256,7168]{1,0:T(8,128)(2,1)S(1)} %collective-permute-done.refs_1_, bf16[2,7168,2048]{2,1,0:T(8,128)(2,1)} %refs_2_.5, bf16[2,7168,2048]{2,1,0:T(8,128)(2,1)} %refs_2_.5), custom_call_target="tpu_custom_call" | custom-call | flops 1024 | bytes 1024 | tf_op jit(solution)/shard_map/project/pallas_call | solution.py:98
  28.4 0.0 collective-permute-done.2.refs_0_
  28.4 2.5 %collective-permute-start.8 = (bf16[2,128,2048]{2,1,0:T(8,128)(2,1)S(1)}, bf16[2,128,2048]{2,1,0:T(8,128)(2,1)S(1)}, u32[]{:S(2)}, u32[]{:S(2)}) collective-permute-start(bf16[2,128,2048]{2,1,0:T(8,128)(2,1)S(1)} %after.9.refs_4_), channel_id=1, source_target_pairs={{1,0},{0,2},{2,3},{3,1},{5,4},{4,6},{6,7},{7,5},{9,8},{8,10},{10,1... | collective-permute-start | bytes 3145736 | tf_op jit(solution)/shard_map/ppermute | solution.py:269
  31.0 1.2 collective-permute-done.1.refs_0_
  32.1 0.0 collective-permute-start.5
  32.1 19.0 %project.6 = (f32[1,512,2048]{2,1,0:T(8,128)S(1)}, f32[8,128]{1,0:T(8,128)S(1)}) custom-call(bf16[512,7168]{1,0:T(8,128)(2,1)S(1)} %get-tuple-element.21.refs_0_, bf16[2,7168,2048]{2,1,0:T(8,128)(2,1)} %refs_2_.5, bf16[2,7168,2048]{2,1,0:T(8,128)(2,1)} %refs_2_.5, bf16[256,2048]{1,0:T(8,128)(2,1)S(1)} %after.8.refs_3_.refs_0_, ...), custom_call_target="tpu_custom_call" | custom-call | flops 1024 | bytes 1024 | tf_op jit(solution)/shard_map/project/pallas_call | solution.py:98
  51.2 2.8 %collective-permute-done.6.refs_0_ = bf16[256,2048]{1,0:T(8,128)(2,1)S(1)} collective-permute-done((bf16[256,2048]{1,0:T(8,128)(2,1)S(1)}, bf16[256,2048]{1,0:T(8,128)(2,1)S(1)}, u32[]{:S(2)}, u32[]{:S(2)}) %collective-permute-start.6) | collective-permute-done | bytes 1048608 | tf_op jit(solution)/shard_map/ppermute | solution.py:241
  53.9 0.0 collective-permute-start.7
  53.9 1.5 %collective-permute-start.4 = (bf16[256,1536]{1,0:T(8,128)(2,1)S(1)}, bf16[256,1536]{1,0:T(8,128)(2,1)S(1)}, u32[]{:S(2)}, u32[]{:S(2)}) collective-permute-start(bf16[256,1536]{1,0:T(8,128)(2,1)S(1)} %get-tuple-element.26), channel_id=1, source_target_pairs={{0,8},{4,12},{8,0},{12,4},{1,9},{5,13},{9,1},{13,5},{2,10},{6,14},... | collective-permute-start | bytes 2359304 | tf_op jit(solution)/shard_map/ppermute | solution.py:241
  55.4 0.0 collective-permute-done.8.refs_0_
  55.4 1.6 %collective-permute-start.12 = (bf16[2,128,2048]{2,1,0:T(8,128)(2,1)S(1)}, bf16[2,128,2048]{2,1,0:T(8,128)(2,1)S(1)}, u32[]{:S(2)}, u32[]{:S(2)}) collective-permute-start(bf16[2,128,2048]{2,1,0:T(8,128)(2,1)S(1)} %after.11.refs_7_.refs_5_), channel_id=1, source_target_pairs={{1,0},{0,2},{2,3},{3,1},{5,4},{4,6},{6,7},{7,5},{9,8},{8,10},{10,1... | collective-permute-start | bytes 3145736 | tf_op jit(solution)/shard_map/ppermute | solution.py:269
  57.1 1.5 %collective-permute-start.10 = (bf16[256,768]{1,0:T(8,128)(2,1)S(1)}, bf16[256,768]{1,0:T(8,128)(2,1)S(1)}, u32[]{:S(2)}, u32[]{:S(2)}) collective-permute-start(bf16[256,768]{1,0:T(8,128)(2,1)S(1)} %get-tuple-element.30), channel_id=1, source_target_pairs={{0,8},{4,12},{8,0},{12,4},{1,9},{5,13},{9,1},{13,5},{2,10},{6,14},... | collective-permute-start | bytes 1179656 | tf_op jit(solution)/shard_map/ppermute | solution.py:241
  58.6 0.0 collective-permute-done.5.refs_1_
  58.6 0.0 collective-permute-done.7.refs_3_
  58.6 21.9 %project.7 = (f32[2,512,2048]{2,1,0:T(8,128)S(1)}, f32[8,128]{1,0:T(8,128)S(1)}) custom-call(bf16[256,2048]{1,0:T(8,128)(2,1)S(1)} %after.8.refs_3_.refs_0_, bf16[256,2048]{1,0:T(8,128)(2,1)S(1)} %collective-permute-done.5.refs_1_, bf16[256,2048]{1,0:T(8,128)(2,1)S(1)} %after.10.refs_2_.refs_6_, bf16[256,2048]{1,0:T(8,128)(2,1)S(1)} %collective-permute-done.7.refs_3_, ...), custom_call_target="tpu_custom_call" | custom-call | flops 1024 | bytes 1024 | tf_op jit(solution)/shard_map/project/pallas_call | solution.py:98
  80.5 0.0 collective-permute-done.4.refs_0_
  80.5 0.1 collective-permute-start.9
  80.6 1.7 %collective-permute-done.10.refs_0_ = bf16[256,768]{1,0:T(8,128)(2,1)S(1)} collective-permute-done((bf16[256,768]{1,0:T(8,128)(2,1)S(1)}, bf16[256,768]{1,0:T(8,128)(2,1)S(1)}, u32[]{:S(2)}, u32[]{:S(2)}) %collective-permute-start.10) | collective-permute-done | bytes 393248 | tf_op jit(solution)/shard_map/ppermute | solution.py:241
  82.3 0.0 collective-permute-start.11
  82.3 1.5 %collective-permute-start.3 = (bf16[256,768]{1,0:T(8,128)(2,1)S(1)}, bf16[256,768]{1,0:T(8,128)(2,1)S(1)}, u32[]{:S(2)}, u32[]{:S(2)}) collective-permute-start(bf16[256,768]{1,0:T(8,128)(2,1)S(1)} %get-tuple-element.25), channel_id=1, source_target_pairs={{0,8},{4,12},{8,0},{12,4},{1,9},{5,13},{9,1},{13,5},{2,10},{6,14},... | collective-permute-start | bytes 1179656 | tf_op jit(solution)/shard_map/ppermute | solution.py:241
  83.8 0.0 collective-permute-done.12.refs_0_
  83.8 0.2 collective-permute-done.11.refs_3_
  84.0 0.0 collective-permute-done.9.refs_1_
  84.0 13.1 %project.8 = (f32[2,512,2048]{2,1,0:T(8,128)S(1)}, f32[8,128]{1,0:T(8,128)S(1)}) custom-call(bf16[256,1536]{1,0:T(8,128)(2,1)S(1)} %after.12.refs_0_.refs_6_, bf16[256,1536]{1,0:T(8,128)(2,1)S(1)} %collective-permute-done.9.refs_1_, bf16[256,768]{1,0:T(8,128)(2,1)S(1)} %after.13.refs_2_.refs_7_, ...), custom_call_target="tpu_custom_call", output_to_operand_aliasing={{0}: (5, {})} | custom-call | flops 1024 | bytes 1024 | tf_op jit(solution)/shard_map/project/pallas_call | solution.py:98
  97.1 0.2 collective-permute-start.13
  97.3 1.6 %collective-permute-done.13.refs_1_ = bf16[256,768]{1,0:T(8,128)(2,1)S(1)} collective-permute-done((bf16[256,768]{1,0:T(8,128)(2,1)S(1)}, bf16[256,768]{1,0:T(8,128)(2,1)S(1)}, u32[]{:S(2)}, u32[]{:S(2)}) %collective-permute-start.13) | collective-permute-done | bytes 393248 | tf_op jit(solution)/shard_map/ppermute | solution.py:238
  98.9 6.0 %project.9 = (f32[2,512,2048]{2,1,0:T(8,128)S(1)}, f32[8,128]{1,0:T(8,128)}) custom-call(bf16[256,768]{1,0:T(8,128)(2,1)S(1)} %after.15.refs_0_.refs_4_, bf16[256,768]{1,0:T(8,128)(2,1)S(1)} %collective-permute-done.13.refs_1_, bf16[2,7168,2048]{2,1,0:T(8,128)(2,1)} %refs_2_.5, ...), custom_call_target="tpu_custom_call", output_to_operand_aliasing={{0}: (3, {})} | custom-call | flops 1024 | bytes 1024 | tf_op jit(solution)/shard_map/project/pallas_call | solution.py:98
  104.9 0.0 copy-start
  104.9 0.0 copy-start.1
  104.9 3.5 %score.1 = f32[4,2,256]{2,1,0:T(2,128)S(1)} custom-call(f32[1,512,2048]{2,1,0:T(8,128)S(1)} %get-tuple-element.20.refs_0_, f32[1,512,2048]{2,1,0:T(8,128)S(1)} %get-tuple-element.24.refs_1_, f32[2,512,2048]{2,1,0:T(8,128)S(1)} %get-tuple-element.34.refs_2_, bf16[2,128,2048]{2,1,0:T(8,128)(2,1)} %refs_3_.3, bf16[2,128,2048]{2,1,0:T(8,128)(2,1)S(1)} %after.9.refs_4_, ...), custom_call_target="tpu_custom_call" | custom-call | tf_op jit(solution)/shard_map/score/pallas_call | solution.py:156
  108.4 1.0 collective-permute-start.15
  109.4 0.1 collective-permute-start.16
  109.6 1.1 collective-permute-start.14
  110.6 0.4 convert_reduce_fusion
  111.1 1.1 collective-permute-done.15
  112.2 0.4 collective-permute-done.16
  112.6 2.2 %collective-permute-start.18 = (f32[2,2,512]{2,1,0:T(2,128)S(1)}, f32[2,2,512]{2,1,0:T(2,128)S(1)}, u32[]{:S(2)}, u32[]{:S(2)}) collective-permute-start(f32[2,2,512]{2,1,0:T(2,128)S(1)} %add_add_fusion), channel_id=1, source_target_pairs={{0,2},{1,3},{2,0},{3,1},{4,6},{5,7},{6,4},{7,5},{8,10},{9,11},{10,... | collective-permute-start | bytes 24584 | tf_op jit(solution)/shard_map/ppermute | solution.py:176
  114.8 1.4 %collective-permute-start.17 = (f32[2,2,512]{2,1,0:T(2,128)S(1)}, f32[2,2,512]{2,1,0:T(2,128)S(1)}, u32[]{:S(2)}, u32[]{:S(2)}) collective-permute-start(f32[2,2,512]{2,1,0:T(2,128)S(1)} %add_add_fusion), channel_id=1, source_target_pairs={{0,1},{1,0},{2,3},{3,2},{4,5},{5,4},{6,7},{7,6},{8,9},{9,8},{10,11... | collective-permute-start | bytes 24584 | tf_op jit(solution)/shard_map/ppermute | solution.py:176
  116.2 1.0 collective-permute-done.18
  117.2 3.0 %collective-permute-done.19 = f32[2,2,512]{2,1,0:T(2,128)S(1)} collective-permute-done((f32[2,2,512]{2,1,0:T(2,128)S(1)}, f32[2,2,512]{2,1,0:T(2,128)S(1)}, u32[]{:S(2)}, u32[]{:S(2)}) %collective-permute-start.19) | collective-permute-done | bytes 8224 | tf_op jit(solution)/shard_map/ppermute | solution.py:176
  120.2 0.0 collective-permute-done.17
  120.2 0.6 add_multiply_fusion
  (17 shorter events, 0.1 us)
Async XLA Ops:
  0.0 8.2 %collective-permute-start = (bf16[256,7168]{1,0:T(8,128)(2,1)}, bf16[256,7168]{1,0:T(8,128)(2,1)S(1)}, u32[]{:S(2)}, u32[]{:S(2)}) collective-permute-start(bf16[256,7168]{1,0:T(8,128)(2,1)} %bitcast.11), channel_id=1, source_target_pairs={{0,4},{4,0},{8,12},{12,8},{1,5},{5,1},{9,13},{13,9},{2,6},{6,2},{1... | collective-permute-start | bytes 11010056 | tf_op jit(solution)/shard_map/ppermute | solution.py:238
  0.5 28.0 %collective-permute-start.2 = (bf16[2,128,2048]{2,1,0:T(8,128)(2,1)}, bf16[2,128,2048]{2,1,0:T(8,128)(2,1)S(1)}, u32[]{:S(2)}, u32[]{:S(2)}) collective-permute-start(bf16[2,128,2048]{2,1,0:T(8,128)(2,1)} %refs_3_.3), channel_id=1, source_target_pairs={{1,0},{0,2},{2,3},{3,1},{5,4},{4,6},{6,7},{7,5},{9,8},{8,10},{10,1... | collective-permute-start | bytes 3145736 | tf_op jit(solution)/shard_map/ppermute | solution.py:254
  6.1 26.1 %collective-permute-start.1 = (bf16[256,2048]{1,0:T(8,128)(2,1)S(1)}, bf16[256,2048]{1,0:T(8,128)(2,1)S(1)}, u32[]{:S(2)}, u32[]{:S(2)}) collective-permute-start(bf16[256,2048]{1,0:T(8,128)(2,1)S(1)} %get-tuple-element.22), channel_id=1, source_target_pairs={{0,8},{4,12},{8,0},{12,4},{1,9},{5,13},{9,1},{13,5},{2,10},{6,14},... | collective-permute-start | bytes 3145736 | tf_op jit(solution)/shard_map/ppermute | solution.py:241
  7.7 46.2 %collective-permute-start.6 = (bf16[256,2048]{1,0:T(8,128)(2,1)S(1)}, bf16[256,2048]{1,0:T(8,128)(2,1)S(1)}, u32[]{:S(2)}, u32[]{:S(2)}) collective-permute-start(bf16[256,2048]{1,0:T(8,128)(2,1)S(1)} %get-tuple-element.27), channel_id=1, source_target_pairs={{0,8},{4,12},{8,0},{12,4},{1,9},{5,13},{9,1},{13,5},{2,10},{6,14},... | collective-permute-start | bytes 3145736 | tf_op jit(solution)/shard_map/ppermute | solution.py:241
  28.4 27.0 %collective-permute-start.8 = (bf16[2,128,2048]{2,1,0:T(8,128)(2,1)S(1)}, bf16[2,128,2048]{2,1,0:T(8,128)(2,1)S(1)}, u32[]{:S(2)}, u32[]{:S(2)}) collective-permute-start(bf16[2,128,2048]{2,1,0:T(8,128)(2,1)S(1)} %after.9.refs_4_), channel_id=1, source_target_pairs={{1,0},{0,2},{2,3},{3,1},{5,4},{4,6},{6,7},{7,5},{9,8},{8,10},{10,1... | collective-permute-start | bytes 3145736 | tf_op jit(solution)/shard_map/ppermute | solution.py:269
  32.1 26.4 %collective-permute-start.5 = (bf16[256,2048]{1,0:T(8,128)(2,1)S(1)}, bf16[256,2048]{1,0:T(8,128)(2,1)S(1)}, u32[]{:S(2)}, u32[]{:S(2)}) collective-permute-start(bf16[256,2048]{1,0:T(8,128)(2,1)S(1)} %after.8.refs_3_.refs_0_), channel_id=1, source_target_pairs={{0,4},{4,0},{8,12},{12,8},{1,5},{5,1},{9,13},{13,9},{2,6},{6,2},{1... | collective-permute-start | bytes 3145736 | tf_op jit(solution)/shard_map/ppermute | solution.py:238
  53.9 4.7 %collective-permute-start.7 = (bf16[256,2048]{1,0:T(8,128)(2,1)S(1)}, bf16[256,2048]{1,0:T(8,128)(2,1)S(1)}, u32[]{:S(2)}, u32[]{:S(2)}) collective-permute-start(bf16[256,2048]{1,0:T(8,128)(2,1)S(1)} %after.10.refs_2_.refs_6_), channel_id=1, source_target_pairs={{0,4},{4,0},{8,12},{12,8},{1,5},{5,1},{9,13},{13,9},{2,6},{6,2},{1... | collective-permute-start | bytes 3145736 | tf_op jit(solution)/shard_map/ppermute | solution.py:238
  53.9 26.6 %collective-permute-start.4 = (bf16[256,1536]{1,0:T(8,128)(2,1)S(1)}, bf16[256,1536]{1,0:T(8,128)(2,1)S(1)}, u32[]{:S(2)}, u32[]{:S(2)}) collective-permute-start(bf16[256,1536]{1,0:T(8,128)(2,1)S(1)} %get-tuple-element.26), channel_id=1, source_target_pairs={{0,8},{4,12},{8,0},{12,4},{1,9},{5,13},{9,1},{13,5},{2,10},{6,14},... | collective-permute-start | bytes 2359304 | tf_op jit(solution)/shard_map/ppermute | solution.py:241
  55.4 28.4 %collective-permute-start.12 = (bf16[2,128,2048]{2,1,0:T(8,128)(2,1)S(1)}, bf16[2,128,2048]{2,1,0:T(8,128)(2,1)S(1)}, u32[]{:S(2)}, u32[]{:S(2)}) collective-permute-start(bf16[2,128,2048]{2,1,0:T(8,128)(2,1)S(1)} %after.11.refs_7_.refs_5_), channel_id=1, source_target_pairs={{1,0},{0,2},{2,3},{3,1},{5,4},{4,6},{6,7},{7,5},{9,8},{8,10},{10,1... | collective-permute-start | bytes 3145736 | tf_op jit(solution)/shard_map/ppermute | solution.py:269
  57.1 25.2 %collective-permute-start.10 = (bf16[256,768]{1,0:T(8,128)(2,1)S(1)}, bf16[256,768]{1,0:T(8,128)(2,1)S(1)}, u32[]{:S(2)}, u32[]{:S(2)}) collective-permute-start(bf16[256,768]{1,0:T(8,128)(2,1)S(1)} %get-tuple-element.30), channel_id=1, source_target_pairs={{0,8},{4,12},{8,0},{12,4},{1,9},{5,13},{9,1},{13,5},{2,10},{6,14},... | collective-permute-start | bytes 1179656 | tf_op jit(solution)/shard_map/ppermute | solution.py:241
  80.5 3.5 %collective-permute-start.9 = (bf16[256,1536]{1,0:T(8,128)(2,1)S(1)}, bf16[256,1536]{1,0:T(8,128)(2,1)S(1)}, u32[]{:S(2)}, u32[]{:S(2)}) collective-permute-start(bf16[256,1536]{1,0:T(8,128)(2,1)S(1)} %after.12.refs_0_.refs_6_), channel_id=1, source_target_pairs={{0,4},{4,0},{8,12},{12,8},{1,5},{5,1},{9,13},{13,9},{2,6},{6,2},{1... | collective-permute-start | bytes 2359304 | tf_op jit(solution)/shard_map/ppermute | solution.py:238
  82.3 1.7 %collective-permute-start.11 = (bf16[256,768]{1,0:T(8,128)(2,1)S(1)}, bf16[256,768]{1,0:T(8,128)(2,1)S(1)}, u32[]{:S(2)}, u32[]{:S(2)}) collective-permute-start(bf16[256,768]{1,0:T(8,128)(2,1)S(1)} %after.13.refs_2_.refs_7_), channel_id=1, source_target_pairs={{0,4},{4,0},{8,12},{12,8},{1,5},{5,1},{9,13},{13,9},{2,6},{6,2},{1... | collective-permute-start | bytes 1179656 | tf_op jit(solution)/shard_map/ppermute | solution.py:238
  82.3 14.8 %collective-permute-start.3 = (bf16[256,768]{1,0:T(8,128)(2,1)S(1)}, bf16[256,768]{1,0:T(8,128)(2,1)S(1)}, u32[]{:S(2)}, u32[]{:S(2)}) collective-permute-start(bf16[256,768]{1,0:T(8,128)(2,1)S(1)} %get-tuple-element.25), channel_id=1, source_target_pairs={{0,8},{4,12},{8,0},{12,4},{1,9},{5,13},{9,1},{13,5},{2,10},{6,14},... | collective-permute-start | bytes 1179656 | tf_op jit(solution)/shard_map/ppermute | solution.py:241
  97.1 1.8 %collective-permute-start.13 = (bf16[256,768]{1,0:T(8,128)(2,1)S(1)}, bf16[256,768]{1,0:T(8,128)(2,1)S(1)}, u32[]{:S(2)}, u32[]{:S(2)}) collective-permute-start(bf16[256,768]{1,0:T(8,128)(2,1)S(1)} %after.15.refs_0_.refs_4_), channel_id=1, source_target_pairs={{0,4},{4,0},{8,12},{12,8},{1,5},{5,1},{9,13},{13,9},{2,6},{6,2},{1... | collective-permute-start | bytes 1179656 | tf_op jit(solution)/shard_map/ppermute | solution.py:238
  104.9 5.7 %copy-start = (s32[2,512]{1,0:T(2,128)S(1)}, s32[2,512]{1,0:T(2,128)}, u32[]{:S(2)}) copy-start(s32[2,512]{1,0:T(2,128)} %param.8) | copy-start | bytes 12292
  104.9 11.2 %copy-start.1 = (s32[2,512]{1,0:T(2,128)S(1)}, s32[2,512]{1,0:T(2,128)}, u32[]{:S(2)}) copy-start(s32[2,512]{1,0:T(2,128)} %param.9) | copy-start | bytes 12292
  108.4 3.7 %collective-permute-start.15 = (f32[2,2,512]{2,1,0:T(2,128)S(1)}, f32[2,2,512]{2,1,0:T(2,128)S(1)}, u32[]{:S(2)}, u32[]{:S(2)}) collective-permute-start(f32[2,2,512]{2,1,0:T(2,128)S(1)} %copy_bitcast_fusion), channel_id=1, source_target_pairs={{0,8},{4,12},{8,0},{12,4},{1,9},{5,13},{9,1},{13,5},{2,10},{6,14},... | collective-permute-start | bytes 24584 | tf_op jit(solution)/shard_map/ppermute | solution.py:176
  109.4 3.1 %collective-permute-start.16 = (f32[2,2,512]{2,1,0:T(2,128)S(1)}, f32[2,2,512]{2,1,0:T(2,128)S(1)}, u32[]{:S(2)}, u32[]{:S(2)}) collective-permute-start(f32[2,2,512]{2,1,0:T(2,128)S(1)} %copy_bitcast_fusion), channel_id=1, source_target_pairs={{0,12},{4,8},{8,4},{12,0},{1,13},{5,9},{9,5},{13,1},{2,14},{6,10},... | collective-permute-start | bytes 24584 | tf_op jit(solution)/shard_map/ppermute | solution.py:176
  109.6 3.0 %collective-permute-start.14 = (f32[2,2,512]{2,1,0:T(2,128)S(1)}, f32[2,2,512]{2,1,0:T(2,128)S(1)}, u32[]{:S(2)}, u32[]{:S(2)}) collective-permute-start(f32[2,2,512]{2,1,0:T(2,128)S(1)} %copy_bitcast_fusion), channel_id=1, source_target_pairs={{0,4},{4,0},{8,12},{12,8},{1,5},{5,1},{9,13},{13,9},{2,6},{6,2},{1... | collective-permute-start | bytes 24584 | tf_op jit(solution)/shard_map/ppermute | solution.py:176
  112.6 4.6 %collective-permute-start.18 = (f32[2,2,512]{2,1,0:T(2,128)S(1)}, f32[2,2,512]{2,1,0:T(2,128)S(1)}, u32[]{:S(2)}, u32[]{:S(2)}) collective-permute-start(f32[2,2,512]{2,1,0:T(2,128)S(1)} %add_add_fusion), channel_id=1, source_target_pairs={{0,2},{1,3},{2,0},{3,1},{4,6},{5,7},{6,4},{7,5},{8,10},{9,11},{10,... | collective-permute-start | bytes 24584 | tf_op jit(solution)/shard_map/ppermute | solution.py:176
  114.8 5.4 %collective-permute-start.19 = (f32[2,2,512]{2,1,0:T(2,128)S(1)}, f32[2,2,512]{2,1,0:T(2,128)S(1)}, u32[]{:S(2)}, u32[]{:S(2)}) collective-permute-start(f32[2,2,512]{2,1,0:T(2,128)S(1)} %add_add_fusion), channel_id=1, source_target_pairs={{0,3},{1,2},{2,1},{3,0},{4,7},{5,6},{6,5},{7,4},{8,11},{9,10},{10,... | collective-permute-start | bytes 24584 | tf_op jit(solution)/shard_map/ppermute | solution.py:176
  114.8 5.4 %collective-permute-start.17 = (f32[2,2,512]{2,1,0:T(2,128)S(1)}, f32[2,2,512]{2,1,0:T(2,128)S(1)}, u32[]{:S(2)}, u32[]{:S(2)}) collective-permute-start(f32[2,2,512]{2,1,0:T(2,128)S(1)} %add_add_fusion), channel_id=1, source_target_pairs={{0,1},{1,0},{2,3},{3,2},{4,5},{5,4},{6,7},{7,6},{8,9},{9,8},{10,11... | collective-permute-start | bytes 24584 | tf_op jit(solution)/shard_map/ppermute | solution.py:176

commit v3 on v2

v3 whole, which is shorter than its diff:
```python
import functools
import typing

import jax
import jax.numpy as jnp
from jax import lax
from jax.experimental import pallas as pl
from jax.experimental.pallas import tpu as pltpu
from jax.sharding import PartitionSpec as P

WEIGHTS = (8, 7, 8, 5)
GROUPS = (2, 1, 1)
HELPER_VMEM = 1024 * 1024
TILE = 512
STRIP_ROWS = 8192


def tile_of(length, most):
    size = min(length, most)
    while length % size:
        size -= 128
    return size


class Plan(typing.NamedTuple):
    query: int
    queries: int
    begin: int
    depth: int
    tile: int
    strips: int
    turns: int

    @property
    def steps(self):
        return self.queries * self.turns


def plan_of(query, queries, begin, depth, width, room):
    tile = tile_of(width, TILE)
    strips = 1
    while strips * 2 * depth <= room and width // tile % (strips * 2) == 0:
        strips *= 2
    return Plan(query, queries, begin, depth, tile, strips, width // tile // strips)


def fetches(plan, step, q_ref, slot_ref, sems):
    number, turn = plan.query + step // plan.turns, step % plan.turns
    copies = []
    for strip in range(plan.strips):
        column = (turn * plan.strips + strip) * plan.tile
        if not isinstance(column, int):
            column = pl.multiple_of(column, plan.tile)
        source = q_ref.at[number, pl.ds(plan.begin, plan.depth), pl.ds(column, plan.tile)]
        target = slot_ref.at[pl.ds(strip * plan.depth, plan.depth)]
        copies.append(pltpu.make_async_copy(source, target, sems.at[strip]))
    return copies


def run(copies, start):
    for copy in copies:
        if start:
            copy.start()
        else:
            copy.wait()


def load_kernel(plan, source_ref, q_ref, slot_ref, x_ref, sem, sems):
    first = fetches(plan, 0, q_ref, slot_ref, sems)
    rows = pltpu.make_async_copy(source_ref, x_ref.at[pl.ds(0, source_ref.shape[0])], sem)
    run(first, True)
    rows.start()
    run(first, False)
    rows.wait()


def load(own, total, query_grads, plan, room):
    vmem_spec = pl.BlockSpec(memory_space=pltpu.VMEM)
    return pl.pallas_call(
        functools.partial(load_kernel, plan),
        in_specs=[pl.BlockSpec(memory_space=pl.ANY)] * 2,
        out_specs=[vmem_spec] * 2,
        out_shape=[
            jax.ShapeDtypeStruct((room, plan.tile), jnp.bfloat16),
            jax.ShapeDtypeStruct((total, own.shape[1]), jnp.bfloat16),
        ],
        scratch_shapes=[pltpu.SemaphoreType.DMA, pltpu.SemaphoreType.DMA((plan.strips,))],
        cost_estimate=pl.CostEstimate(flops=1024, bytes_accessed=1024, transcendentals=0),
        compiler_params=pltpu.CompilerParams(vmem_limit_bytes=HELPER_VMEM),
        name="load",
    )(own, query_grads)


def project_kernel(parts, plan, later, fresh, laid, *refs):
    g_refs, q_ref = refs[:parts], refs[parts]
    sum_ref, mark_ref, slot_a, x_ref, slot_b, sems, sems_a, sems_b = refs[-8:]
    total = x_ref.shape[0]
    copies = []
    together = total // g_refs[0].shape[0] if parts and not laid else 1
    column = 0
    for at, g_ref in enumerate(g_refs):
        rows = g_ref.shape[0]
        row = total - rows if laid else at % together * rows
        where = x_ref.at[pl.ds(row, rows), pl.ds(column, g_ref.shape[1])]
        copies.append(pltpu.make_async_copy(g_ref, where, sems.at[at]))
        if not laid and at % together == together - 1:
            column += g_ref.shape[1]
    steps = plan.steps
    run(copies, True)
    if steps > 1:
        run(fetches(plan, 1, q_ref, slot_b, sems_b), True)
    mark_ref[...] = jnp.zeros_like(mark_ref)
    run(copies, False)

    def multiply(step, slot_ref):
        number, turn = step // plan.turns, step % plan.turns
        for strip in range(plan.strips):
            product = jnp.dot(
                x_ref[...],
                slot_ref[strip * plan.depth:(strip + 1) * plan.depth, :],
                preferred_element_type=jnp.float32,
            )
            begin = (turn * plan.strips + strip) * plan.tile
            if not isinstance(begin, int):
                begin = pl.multiple_of(begin, plan.tile)
            where = (number, slice(None), pl.ds(begin, plan.tile))
            if fresh:
                sum_ref[where] = product
            else:
                sum_ref[where] += product

    def both(pair):
        step = pair * 2

        @pl.when(pair > 0)
        def _():
            run(fetches(plan, step + 1, q_ref, slot_b, sems_b), True)
            run(fetches(plan, step, q_ref, slot_a, sems_a), False)

        multiply(step, slot_a)

        @pl.when(step + 2 < steps)
        def _():
            run(fetches(plan, step + 2, q_ref, slot_a, sems_a), True)

        if later is not None:

            @pl.when(step + 2 >= steps)
            def _():
                run(fetches(later, 0, q_ref, slot_a, sems_a), True)

        run(fetches(plan, step + 1, q_ref, slot_b, sems_b), False)
        multiply(step + 1, slot_b)

    if steps % 2 == 0:

        @pl.loop(0, steps // 2)
        def _(pair):
            both(pair)
    else:
        for step in range(steps):
            slot_ref, slot_sems = (slot_a, sems_a) if step % 2 == 0 else (slot_b, sems_b)
            if step > 0:
                run(fetches(plan, step, q_ref, slot_ref, slot_sems), step > 1)
                if step > 1:
                    run(fetches(plan, step, q_ref, slot_ref, slot_sems), False)
            multiply(step, slot_ref)
        if later is not None:
            run(fetches(later, 0, q_ref, slot_a, sems_a), True)
    if later is not None:
        run(fetches(later, 0, q_ref, slot_a, sems_a), False)


def project(parts, rows, query_grads, plan, later, slot, running, others=(), laid=None):
    width = query_grads.shape[2]
    fresh = running is None
    any_spec = pl.BlockSpec(memory_space=pl.ANY)
    vmem_spec = pl.BlockSpec(memory_space=pltpu.VMEM)
    operands = [*parts, query_grads, slot]
    in_specs = [any_spec] * (len(parts) + 1) + [vmem_spec]
    aliases = {len(parts) + 1: 2}
    if not fresh:
        aliases[len(operands)] = 0
        operands.append(running)
        in_specs.append(vmem_spec)
    out_shape = [
        jax.ShapeDtypeStruct((plan.queries, rows, width), jnp.float32),
        jax.ShapeDtypeStruct((8, 128), jnp.float32),
        jax.ShapeDtypeStruct(slot.shape, slot.dtype),
    ]
    scratch = []
    if laid is not None:
        aliases[len(operands)] = 3
        operands.append(laid)
        in_specs.append(vmem_spec)
        out_shape.append(jax.ShapeDtypeStruct(laid.shape, laid.dtype))
    else:
        scratch.append(pltpu.VMEM((rows, plan.depth), jnp.bfloat16))
    scratch += [
        pltpu.VMEM(slot.shape, slot.dtype),
        pltpu.SemaphoreType.DMA((max(len(parts), 1),)),
        pltpu.SemaphoreType.DMA((max(plan.strips, later.strips if later else 1),)),
        pltpu.SemaphoreType.DMA((plan.strips,)),
    ]
    limit = 2 * slot.size + (2 * rows * plan.depth if laid is None else 0) + 4 * 1024 * 1024
    return pl.pallas_call(
        functools.partial(project_kernel, len(parts), plan, later, fresh, laid is not None),
        in_specs=in_specs + [any_spec] * len(others),
        out_specs=[vmem_spec] * len(out_shape),
        out_shape=out_shape,
        scratch_shapes=scratch,
        input_output_aliases=aliases,
        cost_estimate=pl.CostEstimate(flops=1024, bytes_accessed=1024, transcendentals=0),
        compiler_params=pltpu.CompilerParams(vmem_limit_bytes=limit),
        name="project",
    )(*operands, *others)


def score_kernel(inp_size, pair, queries, ring, *refs):
    near_refs, refs = refs[:queries], refs[queries:]
    if inp_size > pair:
        far_ref, refs = refs[0], refs[1:]
    *a_refs, out_ref, held, sems = refs
    blocks, shard, width = held.shape[1:]
    me, here = lax.axis_index("inp"), lax.axis_index("out")
    sources = []
    for number in range(inp_size):
        by, other = divmod(number, pair)
        source = lax.rem(me - pair * by + inp_size, inp_size)
        sources.append(jnp.bitwise_xor(source, other) if pair == 2 else source)
    for number, source in enumerate(sources):
        if len(a_refs) == 1:
            begin = pl.multiple_of(source * shard, shard)
            pltpu.make_async_copy(
                a_refs[0].at[:, pl.ds(begin, shard), :], held.at[number], sems.at[number]
            ).start()
            continue
        for at, a_ref in enumerate(a_refs):
            for place, spot in enumerate(ring):

                @pl.when((here == spot) & (source == ring[place - at]))
                def _(a_ref=a_ref, number=number):
                    pltpu.make_async_copy(a_ref, held.at[number], sems.at[number]).start()

    lanes = 128
    for number, source in enumerate(sources):
        pltpu.make_async_copy(held.at[number], held.at[number], sems.at[number]).wait()
        for query in range(queries):
            total = None
            for at in range(0, width, lanes):
                block = held[number, :, :, at:at + lanes].reshape(blocks * shard, lanes).astype(jnp.float32)
                begin = (number if number < pair else number - pair) * blocks * shard
                where = (query, slice(begin, begin + blocks * shard), slice(at, at + lanes))
                rows = near_refs[query][(0, *where[1:])] if number < pair else far_ref[where]
                term = rows * block
                total = term if total is None else total + term
            out_ref[source, query, :] = jnp.sum(total.T, axis=0)


def score(sums, slots, ring, inp_size, pair, queries, blocks, shard):
    width = sums[0].shape[2]
    return pl.pallas_call(
        functools.partial(score_kernel, inp_size, pair, queries, ring),
        in_specs=[pl.BlockSpec(memory_space=pltpu.VMEM)] * len(sums)
        + [pl.BlockSpec(memory_space=pl.ANY)] * len(slots),
        out_specs=pl.BlockSpec(memory_space=pltpu.VMEM),
        out_shape=jax.ShapeDtypeStruct((inp_size, queries, blocks * shard), jnp.float32),
        scratch_shapes=[
            pltpu.VMEM((inp_size, blocks, shard, width), jnp.bfloat16),
            pltpu.SemaphoreType.DMA((inp_size,)),
        ],
        compiler_params=pltpu.CompilerParams(vmem_limit_bytes=6 * 1024 * 1024),
        name="score",
    )(*sums, *slots)


def xor_sum(value, axis, size):
    if size & (size - 1):
        return lax.psum(value, axis)
    terms = [value]
    for other in range(1, size):
        terms.append(lax.ppermute(value, axis, [(at, at ^ other) for at in range(size)]))
    while len(terms) > 1:
        terms = [terms[at] + terms[at + 1] for at in range(0, len(terms), 2)]
    return terms[0]


def after(value, *others):
    any_spec = pl.BlockSpec(memory_space=pl.ANY)
    return pl.pallas_call(
        lambda *refs: None,
        in_specs=[any_spec] * (1 + len(others)),
        out_specs=any_spec,
        out_shape=jax.ShapeDtypeStruct(value.shape, value.dtype),
        input_output_aliases={0: 0},
        compiler_params=pltpu.CompilerParams(vmem_limit_bytes=HELPER_VMEM),
        name="after",
    )(pltpu.with_memory_space_constraint(value, pltpu.VMEM), *others)


def in_hbm(value):
    return pltpu.with_memory_space_constraint(value, pltpu.HBM)


def cut_kernel(spans, source_ref, *refs):
    outs, sems = refs[:-1], refs[-1]
    copies = []
    for at, (span, out_ref) in enumerate(zip(spans, outs)):
        copies.append(pltpu.make_async_copy(source_ref.at[:, pl.ds(*span)], out_ref, sems.at[at]))
    run(copies, True)
    run(copies, False)


def cut(source, spans):
    return pl.pallas_call(
        functools.partial(cut_kernel, spans),
        in_specs=[pl.BlockSpec(memory_space=pl.ANY)],
        out_specs=[pl.BlockSpec(memory_space=pltpu.VMEM)] * len(spans),
        out_shape=[jax.ShapeDtypeStruct((source.shape[0], length), source.dtype) for _, length in spans],
        scratch_shapes=[pltpu.SemaphoreType.DMA((len(spans),))],
        compiler_params=pltpu.CompilerParams(vmem_limit_bytes=HELPER_VMEM),
        name="cut",
    )(source)


def shards(inp_size, out_size, activations, out_grads, query_grads, token_ids, loss_mask):
    blocks, shard, depth = out_grads.shape
    queries, _, width = query_grads.shape
    tokens = token_ids.shape[1]
    pair = 2 if inp_size % 2 == 0 else 1
    chips = inp_size // pair
    rows = blocks * shard

    unit = 256 if depth % 256 == 0 else depth
    units = depth // unit
    edges = [0]
    for at in range(len(WEIGHTS)):
        edges.append(units * sum(WEIGHTS[:at + 1]) // sum(WEIGHTS) * unit)
    spans = [(begin, end - begin) for begin, end in zip(edges, edges[1:]) if end > begin]
    chunks = len(spans)

    def flip(value):
        return lax.ppermute(value, "inp", [(at, at ^ 1) for at in range(inp_size)])

    def shift(value, by):
        return lax.ppermute(value, "inp", [(at, (at + pair * by) % inp_size) for at in range(inp_size)])

    own = in_hbm(out_grads.reshape(rows, depth))
    near = [pltpu.with_memory_space_constraint(flip(own), pltpu.VMEM)] if pair == 2 else []
    query_grads = in_hbm(query_grads)
    activations = in_hbm(activations)
    line = inp_size == out_size and activations.shape[1] == shard and out_size > 1
    ring = list(range(0, out_size, 2)) + list(range(1, out_size, 2))[::-1]
    turn = [(ring[at - 1], ring[at]) for at in range(out_size)]
    pieces_out = cut(own, spans) if chips > 1 else []

    slots = [activations]
    if line:
        slots.append(lax.ppermute(activations, "out", turn))
    else:
        slots = [lax.all_gather(activations, "out", axis=1, tiled=True)]

    def step_along(mark):
        if not line or len(slots) == out_size:
            return []
        slots[-1] = ended = after(slots[-1], mark)
        slots.append(lax.ppermute(ended, "out", turn))
        return [ended]

    coming = []
    if chips > 1:
        coming = [[shift(piece, by) for by in range(1, chips)] for piece in pieces_out]
    waiting = []

    def receive(mark, count=1):
        pieces = []
        for _ in range(min(count, len(coming))):
            arrived = [after(piece, mark) for piece in coming.pop(0)]
            waiting.extend(sum([[piece, flip(piece)] if pair == 2 else [piece] for piece in arrived], []))
            pieces += arrived
        return pieces

    room = max(depth, STRIP_ROWS if depth >= STRIP_ROWS // 2 else 0)
    plans = [plan_of(query, 1, 0, depth, width, depth) for query in range(queries)]
    chosen = []
    for count in GROUPS + (1,) * chunks:
        group, spans = (spans[:count], spans[count:]) if chips > 1 else ([], [])
        if group:
            chosen.append(count)
            length = sum(length for _, length in group)
            plans.append(plan_of(0, queries, group[0][0], length, width, room))
    plans.append(None)

    slot, laid = load(own, pair * rows, query_grads, plans[0], room)
    sums = []
    mark = None
    for query in range(queries):
        others = []
        if query > 0:
            others = receive(mark) + step_along(mark)
        near_sum, mark, slot, laid = project(
            near if query == 0 else [], pair * rows, query_grads, plans[query], plans[query + 1], slot, None, others, laid
        )
        sums.append(near_sum)
    running = None
    got = min(queries - 1, len(coming))
    for at, count in enumerate(chosen):
        others = receive(mark, count - (got if at == 0 else 0)) + (step_along(mark) if at > 0 else [])
        running, mark, slot = project(
            waiting, (inp_size - pair) * rows, query_grads, plans[queries + at], plans[queries + at + 1], slot, running, others
        )
        waiting.clear()
    if running is not None:
        sums.append(running)
    raw = score(sums, slots, ring, inp_size, pair, queries, blocks, shard)
    raw = raw.reshape(inp_size, queries, blocks, shard).transpose(1, 2, 0, 3).reshape(queries, blocks, tokens)
    raw = xor_sum(xor_sum(raw, "inp", inp_size), "out", out_size)
    equal = token_ids[:, :, None] == token_ids[:, None, :]
    counts = jnp.sum(equal.astype(jnp.int32), axis=2)
    weight = loss_mask.astype(jnp.float32) / counts.astype(jnp.float32)
    return raw * weight[None]


def solution(mesh):
    in_specs = (
        P("grp", "out", "inp"),
        P("grp", "inp", "out"),
        P(None, "out", "inp"),
        P("grp", None),
        P("grp", None),
    )
    out_specs = P(None, "grp", None)
    body = functools.partial(shards, mesh.shape["inp"], mesh.shape["out"])
    return jax.shard_map(body, mesh=mesh, in_specs=in_specs, out_specs=out_specs, check_vma=False)
```

time: 121 us -> 118 us (0.975)
  Pallas kernels: 85.7 us -> 74.7 us
  waiting for transfers between devices: 13 us -> 19 us
  starting transfers between devices: 20.9 us -> 23.4 us
    pallas_call x5 -> x6, Pallas kernels: 80.2 us -> 69.2 us  [the longest x5 65 us: project(): pl.pallas_call(functools.partial(project_kernel, len(parts), plan, later,...]
    ppermute x2, waiting for transfers between devices: 0.01 us -> 6.01 us  [step_along(): slots.append(lax.ppermute(ended, 'out', turn))]
    ppermute x2, starting transfers between devices: 4.14 us -> 6.39 us  [step_along(): slots.append(lax.ppermute(ended, 'out', turn))]
    ppermute x6, starting transfers between devices: 5.76 us -> 7.17 us  [xor_sum(): lax.ppermute(value, axis, [(at, at ^ other) for at in range(size)])]
    ppermute x5 -> x4, waiting for transfers between devices: 5.66 us -> 4.9 us  [shift(): lax.ppermute(value, 'inp', [(at, (at + pair * by) % inp_size) for at in r...]
    ppermute x5 -> x4, starting transfers between devices: 6.66 us -> 6.77 us  [shift(): lax.ppermute(value, 'inp', [(at, (at + pair * by) % inp_size) for at in r...]
  transfers between devices with their start and end apart: 20 -> 18, of which waited for: 9 -> 11; matrix products, arithmetic and copies ran while one was open for 0% -> 0% of each run, Pallas kernels for 63% -> 60%
where the time goes in v3:
time: 118 us
  Pallas kernels  74.7 us (63%)
  starting transfers between devices  23.4 us (20%)
  waiting for transfers between devices  19 us (16%)
    pallas_call x5, Pallas kernels, project(): pl.pallas_call(functools.partial(project_kernel, len(parts), plan, later,...  65 us
    ppermute x6, starting transfers between devices, xor_sum(): lax.ppermute(value, axis, [(at, at ^ other) for at in range(size)])  7.17 us
    ppermute x4, starting transfers between devices, shift(): lax.ppermute(value, 'inp', [(at, (at + pair * by) % inp_size) for at in r...  6.77 us
    ppermute x2, starting transfers between devices, step_along(): slots.append(lax.ppermute(ended, 'out', turn))  6.39 us
    ppermute x2, waiting for transfers between devices, step_along(): slots.append(lax.ppermute(ended, 'out', turn))  6.01 us
    ppermute x6, waiting for transfers between devices, xor_sum(): lax.ppermute(value, axis, [(at, at ^ other) for at in range(size)])  5.97 us
    ppermute x4, waiting for transfers between devices, shift(): lax.ppermute(value, 'inp', [(at, (at + pair * by) % inp_size) for at in r...  4.9 us
    pallas_call x1, Pallas kernels, load(): pl.pallas_call(functools.partial(load_kernel, plan), in_specs=[pl.BlockSp...  4.16 us
  transfers between devices with their start and end apart: 18, of which 11 were waited for; matrix products, arithmetic and copies ran while one was open for 0% of the time, Pallas kernels for 60%

profile of v3, /device:TPU:0, one launch (start us, length us, event | category | flops | bytes accessed | tf_op | source)
XLA Modules:
  0.0 118.3 jit_solution(6667015706118545646)
XLA Ops:
  0.0 0.5 collective-permute-start
  0.5 2.0 %cut.1 = (bf16[256,2048]{1,0:T(8,128)(2,1)S(1)}, bf16[256,1792]{1,0:T(8,128)(2,1)S(1)}, bf16[256,2048]{1,0:T(8,128)(2,1)S(1)}, bf16[256,1280]{1,0:T(8,128)(2,1)S(1)}) custom-call(bf16[256,7168]{1,0:T(8,128)(2,1)} %bitcast.12), custom_call_target="tpu_custom_call" | custom-call | tf_op jit(solution)/shard_map/cut/pallas_call | solution.py:315
  2.5 2.6 %collective-permute-start.1 = (bf16[256,2048]{1,0:T(8,128)(2,1)S(1)}, bf16[256,2048]{1,0:T(8,128)(2,1)S(1)}, u32[]{:S(2)}, u32[]{:S(2)}) collective-permute-start(bf16[256,2048]{1,0:T(8,128)(2,1)S(1)} %get-tuple-element.30), channel_id=1, source_target_pairs={{0,8},{4,12},{8,0},{12,4},{1,9},{5,13},{9,1},{13,5},{2,10},{6,14},... | collective-permute-start | bytes 3145736 | tf_op jit(solution)/shard_map/ppermute | solution.py:346
  5.1 2.6 %collective-permute-start.2 = (bf16[2,128,2048]{2,1,0:T(8,128)(2,1)}, bf16[2,128,2048]{2,1,0:T(8,128)(2,1)S(1)}, u32[]{:S(2)}, u32[]{:S(2)}) collective-permute-start(bf16[2,128,2048]{2,1,0:T(8,128)(2,1)} %refs_3_.1), channel_id=1, source_target_pairs={{1,0},{0,2},{2,3},{3,1},{5,4},{4,6},{6,7},{7,5},{9,8},{8,10},{10,1... | collective-permute-start | bytes 3145736 | tf_op jit(solution)/shard_map/ppermute | solution.py:359
  7.7 0.5 collective-permute-start.6
  8.2 4.2 %load.1 = (bf16[8192,512]{1,0:T(8,128)(2,1)S(1)}, bf16[512,7168]{1,0:T(8,128)(2,1)S(1)}) custom-call(bf16[256,7168]{1,0:T(8,128)(2,1)} %bitcast.13, bf16[2,7168,2048]{2,1,0:T(8,128)(2,1)} %refs_2_.3), custom_call_target="tpu_custom_call" | custom-call | flops 1024 | bytes 1024 | tf_op jit(solution)/shard_map/load/pallas_call | solution.py:79
  12.3 0.0 collective-permute-done.refs_0_
  12.4 16.2 %project.5 = (f32[1,512,2048]{2,1,0:T(8,128)S(1)}, f32[8,128]{1,0:T(8,128)S(1)}, bf16[8192,512]{1,0:T(8,128)(2,1)S(1)}, bf16[512,7168]{1,0:T(8,128)(2,1)S(1)}) custom-call(bf16[256,7168]{1,0:T(8,128)(2,1)S(1)} %collective-permute-done.refs_0_, bf16[2,7168,2048]{2,1,0:T(8,128)(2,1)} %refs_2_.3, ...), custom_call_target="tpu_custom_call", output_to_operand_aliasing={{2}: (2, {}), {3}: (3, {})} | custom-call | flops 1024 | bytes 1024 | tf_op jit(solution)/shard_map/project/pallas_call | solution.py:206
  28.5 0.5 collective-permute-done.1.refs_0_
  29.1 0.0 collective-permute-start.5
  29.1 1.9 %collective-permute-start.4 = (bf16[256,2048]{1,0:T(8,128)(2,1)S(1)}, bf16[256,2048]{1,0:T(8,128)(2,1)S(1)}, u32[]{:S(2)}, u32[]{:S(2)}) collective-permute-start(bf16[256,2048]{1,0:T(8,128)(2,1)S(1)} %get-tuple-element.34), channel_id=1, source_target_pairs={{0,8},{4,12},{8,0},{12,4},{1,9},{5,13},{9,1},{13,5},{2,10},{6,14},... | collective-permute-start | bytes 3145736 | tf_op jit(solution)/shard_map/ppermute | solution.py:346
  31.0 0.0 collective-permute-done.2.refs_0_
  31.0 15.9 %project.6 = (f32[1,512,2048]{2,1,0:T(8,128)S(1)}, f32[8,128]{1,0:T(8,128)S(1)}, bf16[8192,512]{1,0:T(8,128)(2,1)S(1)}, bf16[512,7168]{1,0:T(8,128)(2,1)S(1)}) custom-call(bf16[2,7168,2048]{2,1,0:T(8,128)(2,1)} %refs_2_.3, bf16[8192,512]{1,0:T(8,128)(2,1)S(1)} %get-tuple-element.28.refs_1_, ...), custom_call_target="tpu_custom_call", output_to_operand_aliasing={{2}: (1, {}), {3}: (2, {})} | custom-call | flops 1024 | bytes 1024 | tf_op jit(solution)/shard_map/project/pallas_call | solution.py:206
  47.0 1.8 %collective-permute-done.6.refs_0_ = bf16[256,1792]{1,0:T(8,128)(2,1)S(1)} collective-permute-done((bf16[256,1792]{1,0:T(8,128)(2,1)S(1)}, bf16[256,1792]{1,0:T(8,128)(2,1)S(1)}, u32[]{:S(2)}, u32[]{:S(2)}) %collective-permute-start.6) | collective-permute-done | bytes 917536 | tf_op jit(solution)/shard_map/ppermute | solution.py:346
  48.8 0.0 collective-permute-start.7
  48.8 3.0 %collective-permute-start.9 = (bf16[2,128,2048]{2,1,0:T(8,128)(2,1)S(1)}, bf16[2,128,2048]{2,1,0:T(8,128)(2,1)S(1)}, u32[]{:S(2)}, u32[]{:S(2)}) collective-permute-start(bf16[2,128,2048]{2,1,0:T(8,128)(2,1)S(1)} %after.7.refs_4_), channel_id=1, source_target_pairs={{1,0},{0,2},{2,3},{3,1},{5,4},{4,6},{6,7},{7,5},{9,8},{8,10},{10,1... | collective-permute-start | bytes 3145736 | tf_op jit(solution)/shard_map/ppermute | solution.py:367
  51.8 0.0 collective-permute-done.7.refs_3_
  51.8 0.0 collective-permute-done.5.refs_1_
  51.8 17.3 %project.7 = (f32[2,512,2048]{2,1,0:T(8,128)S(1)}, f32[8,128]{1,0:T(8,128)S(1)}, bf16[8192,512]{1,0:T(8,128)(2,1)S(1)}) custom-call(bf16[256,2048]{1,0:T(8,128)(2,1)S(1)} %after.6.refs_3_.refs_0_, bf16[256,2048]{1,0:T(8,128)(2,1)S(1)} %collective-permute-done.5.refs_1_, bf16[256,1792]{1,0:T(8,128)(2,1)S(1)} %after.8.refs_2_.refs_6_, ...), custom_call_target="tpu_custom_call", output_to_operand_aliasing={{2}: (5, {})} | custom-call | flops 1024 | bytes 1024 | tf_op jit(solution)/shard_map/project/pallas_call | solution.py:206
  69.1 2.0 %collective-permute-done.4.refs_0_ = bf16[256,2048]{1,0:T(8,128)(2,1)S(1)} collective-permute-done((bf16[256,2048]{1,0:T(8,128)(2,1)S(1)}, bf16[256,2048]{1,0:T(8,128)(2,1)S(1)}, u32[]{:S(2)}, u32[]{:S(2)}) %collective-permute-start.4) | collective-permute-done | bytes 1048608 | tf_op jit(solution)/shard_map/ppermute | solution.py:346
  71.0 0.0 collective-permute-start.8
  71.0 1.7 %collective-permute-start.3 = (bf16[256,1280]{1,0:T(8,128)(2,1)S(1)}, bf16[256,1280]{1,0:T(8,128)(2,1)S(1)}, u32[]{:S(2)}, u32[]{:S(2)}) collective-permute-start(bf16[256,1280]{1,0:T(8,128)(2,1)S(1)} %get-tuple-element.33), channel_id=1, source_target_pairs={{0,8},{4,12},{8,0},{12,4},{1,9},{5,13},{9,1},{13,5},{2,10},{6,14},... | collective-permute-start | bytes 1966088 | tf_op jit(solution)/shard_map/ppermute | solution.py:346
  72.8 2.1 %collective-permute-done.9.refs_0_ = bf16[2,128,2048]{2,1,0:T(8,128)(2,1)S(1)} collective-permute-done((bf16[2,128,2048]{2,1,0:T(8,128)(2,1)S(1)}, bf16[2,128,2048]{2,1,0:T(8,128)(2,1)S(1)}, u32[]{:S(2)}, u32[]{:S(2)}) %collective-permute-start.9) | collective-permute-done | bytes 1048608 | tf_op jit(solution)/shard_map/ppermute | solution.py:367
  74.9 3.4 %collective-permute-start.11 = (bf16[2,128,2048]{2,1,0:T(8,128)(2,1)S(1)}, bf16[2,128,2048]{2,1,0:T(8,128)(2,1)S(1)}, u32[]{:S(2)}, u32[]{:S(2)}) collective-permute-start(bf16[2,128,2048]{2,1,0:T(8,128)(2,1)S(1)} %after.10.refs_6_.refs_5_), channel_id=1, source_target_pairs={{1,0},{0,2},{2,3},{3,1},{5,4},{4,6},{6,7},{7,5},{9,8},{8,10},{10,1... | collective-permute-start | bytes 3145736 | tf_op jit(solution)/shard_map/ppermute | solution.py:367
  78.2 0.0 collective-permute-done.8.refs_1_
  78.2 9.3 %project.8 = (f32[2,512,2048]{2,1,0:T(8,128)S(1)}, f32[8,128]{1,0:T(8,128)S(1)}, bf16[8192,512]{1,0:T(8,128)(2,1)S(1)}) custom-call(bf16[256,2048]{1,0:T(8,128)(2,1)S(1)} %after.9.refs_0_.refs_5_, bf16[256,2048]{1,0:T(8,128)(2,1)S(1)} %collective-permute-done.8.refs_1_, ...), custom_call_target="tpu_custom_call", output_to_operand_aliasing={{2}: (3, {}), {0}: (4, {})} | custom-call | flops 1024 | bytes 1024 | tf_op jit(solution)/shard_map/project/pallas_call | solution.py:206
  87.6 0.6 collective-permute-done.3.refs_0_
  88.2 0.0 collective-permute-start.10
  88.2 2.1 %collective-permute-done.10.refs_1_ = bf16[256,1280]{1,0:T(8,128)(2,1)S(1)} collective-permute-done((bf16[256,1280]{1,0:T(8,128)(2,1)S(1)}, bf16[256,1280]{1,0:T(8,128)(2,1)S(1)}, u32[]{:S(2)}, u32[]{:S(2)}) %collective-permute-start.10) | collective-permute-done | bytes 655392 | tf_op jit(solution)/shard_map/ppermute | solution.py:343
  90.3 6.3 %project.9 = (f32[2,512,2048]{2,1,0:T(8,128)S(1)}, f32[8,128]{1,0:T(8,128)}, bf16[8192,512]{1,0:T(8,128)(2,1)S(1)}) custom-call(bf16[256,1280]{1,0:T(8,128)(2,1)S(1)} %after.11.refs_0_.refs_5_, bf16[256,1280]{1,0:T(8,128)(2,1)S(1)} %collective-permute-done.10.refs_1_, bf16[2,7168,2048]{2,1,0:T(8,128)(2,1)} %refs_2_.3, ...), custom_call_target="tpu_custom_call", output_to_operand_aliasing={{2}: (3, {}), {0}: (4, {})} | custom-call | flops 1024 | bytes 1024 | tf_op jit(solution)/shard_map/project/pallas_call | solution.py:206
  96.6 3.9 %collective-permute-done.11.refs_6_ = bf16[2,128,2048]{2,1,0:T(8,128)(2,1)S(1)} collective-permute-done((bf16[2,128,2048]{2,1,0:T(8,128)(2,1)S(1)}, bf16[2,128,2048]{2,1,0:T(8,128)(2,1)S(1)}, u32[]{:S(2)}, u32[]{:S(2)}) %collective-permute-start.11) | collective-permute-done | bytes 1048608 | tf_op jit(solution)/shard_map/ppermute | solution.py:367
  100.6 3.5 %score.1 = f32[4,2,256]{2,1,0:T(2,128)S(1)} custom-call(f32[1,512,2048]{2,1,0:T(8,128)S(1)} %get-tuple-element.27.refs_0_, f32[1,512,2048]{2,1,0:T(8,128)S(1)} %get-tuple-element.32.refs_1_, f32[2,512,2048]{2,1,0:T(8,128)S(1)} %get-tuple-element.44.refs_2_, bf16[2,128,2048]{2,1,0:T(8,128)(2,1)} %refs_3_.1, bf16[2,128,2048]{2,1,0:T(8,128)(2,1)S(1)} %after.7.refs_4_, ...), custom_call_target="tpu_custom_call" | custom-call | tf_op jit(solution)/shard_map/score/pallas_call | solution.py:262
  104.1 0.8 collective-permute-start.13
  104.8 0.0 collective-permute-start.14
  104.8 1.4 %collective-permute-start.12 = (f32[2,2,512]{2,1,0:T(2,128)S(1)}, f32[2,2,512]{2,1,0:T(2,128)S(1)}, u32[]{:S(2)}, u32[]{:S(2)}) collective-permute-start(f32[2,2,512]{2,1,0:T(2,128)S(1)} %copy_bitcast_fusion), channel_id=1, source_target_pairs={{0,4},{4,0},{8,12},{12,8},{1,5},{5,1},{9,13},{13,9},{2,6},{6,2},{1... | collective-permute-start | bytes 24584 | tf_op jit(solution)/shard_map/ppermute | solution.py:282
  106.3 0.0 copy-done
  106.3 0.4 convert_reduce_fusion
  106.7 1.1 collective-permute-done.13
  107.8 0.2 collective-permute-done.14
  108.0 0.0 collective-permute-done.12
  108.0 4.2 %collective-permute-start.16 = (f32[2,2,512]{2,1,0:T(2,128)S(1)}, f32[2,2,512]{2,1,0:T(2,128)S(1)}, u32[]{:S(2)}, u32[]{:S(2)}) collective-permute-start(f32[2,2,512]{2,1,0:T(2,128)S(1)} %add_add_fusion), channel_id=1, source_target_pairs={{0,2},{1,3},{2,0},{3,1},{4,6},{5,7},{6,4},{7,5},{8,10},{9,11},{10,... | collective-permute-start | bytes 24584 | tf_op jit(solution)/shard_map/ppermute | solution.py:282
  112.2 0.7 collective-permute-start.17
  112.9 0.0 collective-permute-start.15
  112.9 0.0 copy-done.1
  113.0 0.9 collective-permute-done.16
  113.8 3.8 %collective-permute-done.17 = f32[2,2,512]{2,1,0:T(2,128)S(1)} collective-permute-done((f32[2,2,512]{2,1,0:T(2,128)S(1)}, f32[2,2,512]{2,1,0:T(2,128)S(1)}, u32[]{:S(2)}, u32[]{:S(2)}) %collective-permute-start.17) | collective-permute-done | bytes 8224 | tf_op jit(solution)/shard_map/ppermute | solution.py:282
  117.6 0.0 collective-permute-done.15
  117.6 0.6 add_multiply_fusion
  (12 shorter events, 0.0 us)
Async XLA Ops:
  0.0 12.3 %collective-permute-start = (bf16[256,7168]{1,0:T(8,128)(2,1)}, bf16[256,7168]{1,0:T(8,128)(2,1)S(1)}, u32[]{:S(2)}, u32[]{:S(2)}) collective-permute-start(bf16[256,7168]{1,0:T(8,128)(2,1)} %bitcast.11), channel_id=1, source_target_pairs={{0,4},{4,0},{8,12},{12,8},{1,5},{5,1},{9,13},{13,9},{2,6},{6,2},{1... | collective-permute-start | bytes 11010056 | tf_op jit(solution)/shard_map/ppermute | solution.py:343
  2.5 26.6 %collective-permute-start.1 = (bf16[256,2048]{1,0:T(8,128)(2,1)S(1)}, bf16[256,2048]{1,0:T(8,128)(2,1)S(1)}, u32[]{:S(2)}, u32[]{:S(2)}) collective-permute-start(bf16[256,2048]{1,0:T(8,128)(2,1)S(1)} %get-tuple-element.30), channel_id=1, source_target_pairs={{0,8},{4,12},{8,0},{12,4},{1,9},{5,13},{9,1},{13,5},{2,10},{6,14},... | collective-permute-start | bytes 3145736 | tf_op jit(solution)/shard_map/ppermute | solution.py:346
  5.1 26.0 %collective-permute-start.2 = (bf16[2,128,2048]{2,1,0:T(8,128)(2,1)}, bf16[2,128,2048]{2,1,0:T(8,128)(2,1)S(1)}, u32[]{:S(2)}, u32[]{:S(2)}) collective-permute-start(bf16[2,128,2048]{2,1,0:T(8,128)(2,1)} %refs_3_.1), channel_id=1, source_target_pairs={{1,0},{0,2},{2,3},{3,1},{5,4},{4,6},{6,7},{7,5},{9,8},{8,10},{10,1... | collective-permute-start | bytes 3145736 | tf_op jit(solution)/shard_map/ppermute | solution.py:359
  7.7 41.1 %collective-permute-start.6 = (bf16[256,1792]{1,0:T(8,128)(2,1)S(1)}, bf16[256,1792]{1,0:T(8,128)(2,1)S(1)}, u32[]{:S(2)}, u32[]{:S(2)}) collective-permute-start(bf16[256,1792]{1,0:T(8,128)(2,1)S(1)} %get-tuple-element.35), channel_id=1, source_target_pairs={{0,8},{4,12},{8,0},{12,4},{1,9},{5,13},{9,1},{13,5},{2,10},{6,14},... | collective-permute-start | bytes 2752520 | tf_op jit(solution)/shard_map/ppermute | solution.py:346
  29.1 22.7 %collective-permute-start.5 = (bf16[256,2048]{1,0:T(8,128)(2,1)S(1)}, bf16[256,2048]{1,0:T(8,128)(2,1)S(1)}, u32[]{:S(2)}, u32[]{:S(2)}) collective-permute-start(bf16[256,2048]{1,0:T(8,128)(2,1)S(1)} %after.6.refs_3_.refs_0_), channel_id=1, source_target_pairs={{0,4},{4,0},{8,12},{12,8},{1,5},{5,1},{9,13},{13,9},{2,6},{6,2},{1... | collective-permute-start | bytes 3145736 | tf_op jit(solution)/shard_map/ppermute | solution.py:343
  29.1 41.9 %collective-permute-start.4 = (bf16[256,2048]{1,0:T(8,128)(2,1)S(1)}, bf16[256,2048]{1,0:T(8,128)(2,1)S(1)}, u32[]{:S(2)}, u32[]{:S(2)}) collective-permute-start(bf16[256,2048]{1,0:T(8,128)(2,1)S(1)} %get-tuple-element.34), channel_id=1, source_target_pairs={{0,8},{4,12},{8,0},{12,4},{1,9},{5,13},{9,1},{13,5},{2,10},{6,14},... | collective-permute-start | bytes 3145736 | tf_op jit(solution)/shard_map/ppermute | solution.py:346
  48.8 3.0 %collective-permute-start.7 = (bf16[256,1792]{1,0:T(8,128)(2,1)S(1)}, bf16[256,1792]{1,0:T(8,128)(2,1)S(1)}, u32[]{:S(2)}, u32[]{:S(2)}) collective-permute-start(bf16[256,1792]{1,0:T(8,128)(2,1)S(1)} %after.8.refs_2_.refs_6_), channel_id=1, source_target_pairs={{0,4},{4,0},{8,12},{12,8},{1,5},{5,1},{9,13},{13,9},{2,6},{6,2},{1... | collective-permute-start | bytes 2752520 | tf_op jit(solution)/shard_map/ppermute | solution.py:343
  48.8 26.1 %collective-permute-start.9 = (bf16[2,128,2048]{2,1,0:T(8,128)(2,1)S(1)}, bf16[2,128,2048]{2,1,0:T(8,128)(2,1)S(1)}, u32[]{:S(2)}, u32[]{:S(2)}) collective-permute-start(bf16[2,128,2048]{2,1,0:T(8,128)(2,1)S(1)} %after.7.refs_4_), channel_id=1, source_target_pairs={{1,0},{0,2},{2,3},{3,1},{5,4},{4,6},{6,7},{7,5},{9,8},{8,10},{10,1... | collective-permute-start | bytes 3145736 | tf_op jit(solution)/shard_map/ppermute | solution.py:367
  71.0 7.2 %collective-permute-start.8 = (bf16[256,2048]{1,0:T(8,128)(2,1)S(1)}, bf16[256,2048]{1,0:T(8,128)(2,1)S(1)}, u32[]{:S(2)}, u32[]{:S(2)}) collective-permute-start(bf16[256,2048]{1,0:T(8,128)(2,1)S(1)} %after.9.refs_0_.refs_5_), channel_id=1, source_target_pairs={{0,4},{4,0},{8,12},{12,8},{1,5},{5,1},{9,13},{13,9},{2,6},{6,2},{1... | collective-permute-start | bytes 3145736 | tf_op jit(solution)/shard_map/ppermute | solution.py:343
  71.0 17.1 %collective-permute-start.3 = (bf16[256,1280]{1,0:T(8,128)(2,1)S(1)}, bf16[256,1280]{1,0:T(8,128)(2,1)S(1)}, u32[]{:S(2)}, u32[]{:S(2)}) collective-permute-start(bf16[256,1280]{1,0:T(8,128)(2,1)S(1)} %get-tuple-element.33), channel_id=1, source_target_pairs={{0,8},{4,12},{8,0},{12,4},{1,9},{5,13},{9,1},{13,5},{2,10},{6,14},... | collective-permute-start | bytes 1966088 | tf_op jit(solution)/shard_map/ppermute | solution.py:346
  74.9 25.7 %collective-permute-start.11 = (bf16[2,128,2048]{2,1,0:T(8,128)(2,1)S(1)}, bf16[2,128,2048]{2,1,0:T(8,128)(2,1)S(1)}, u32[]{:S(2)}, u32[]{:S(2)}) collective-permute-start(bf16[2,128,2048]{2,1,0:T(8,128)(2,1)S(1)} %after.10.refs_6_.refs_5_), channel_id=1, source_target_pairs={{1,0},{0,2},{2,3},{3,1},{5,4},{4,6},{6,7},{7,5},{9,8},{8,10},{10,1... | collective-permute-start | bytes 3145736 | tf_op jit(solution)/shard_map/ppermute | solution.py:367
  88.2 2.1 %collective-permute-start.10 = (bf16[256,1280]{1,0:T(8,128)(2,1)S(1)}, bf16[256,1280]{1,0:T(8,128)(2,1)S(1)}, u32[]{:S(2)}, u32[]{:S(2)}) collective-permute-start(bf16[256,1280]{1,0:T(8,128)(2,1)S(1)} %after.11.refs_0_.refs_5_), channel_id=1, source_target_pairs={{0,4},{4,0},{8,12},{12,8},{1,5},{5,1},{9,13},{13,9},{2,6},{6,2},{1... | collective-permute-start | bytes 1966088 | tf_op jit(solution)/shard_map/ppermute | solution.py:343
  100.6 5.7 %copy-start = (s32[2,512]{1,0:T(2,128)S(1)}, s32[2,512]{1,0:T(2,128)}, u32[]{:S(2)}) copy-start(s32[2,512]{1,0:T(2,128)} %param.8) | copy-start | bytes 12292
  100.6 12.4 %copy-start.1 = (s32[2,512]{1,0:T(2,128)S(1)}, s32[2,512]{1,0:T(2,128)}, u32[]{:S(2)}) copy-start(s32[2,512]{1,0:T(2,128)} %param.9) | copy-start | bytes 12292
  104.1 3.7 %collective-permute-start.13 = (f32[2,2,512]{2,1,0:T(2,128)S(1)}, f32[2,2,512]{2,1,0:T(2,128)S(1)}, u32[]{:S(2)}, u32[]{:S(2)}) collective-permute-start(f32[2,2,512]{2,1,0:T(2,128)S(1)} %copy_bitcast_fusion), channel_id=1, source_target_pairs={{0,8},{4,12},{8,0},{12,4},{1,9},{5,13},{9,1},{13,5},{2,10},{6,14},... | collective-permute-start | bytes 24584 | tf_op jit(solution)/shard_map/ppermute | solution.py:282
  104.8 3.1 %collective-permute-start.14 = (f32[2,2,512]{2,1,0:T(2,128)S(1)}, f32[2,2,512]{2,1,0:T(2,128)S(1)}, u32[]{:S(2)}, u32[]{:S(2)}) collective-permute-start(f32[2,2,512]{2,1,0:T(2,128)S(1)} %copy_bitcast_fusion), channel_id=1, source_target_pairs={{0,12},{4,8},{8,4},{12,0},{1,13},{5,9},{9,5},{13,1},{2,14},{6,10},... | collective-permute-start | bytes 24584 | tf_op jit(solution)/shard_map/ppermute | solution.py:282
  104.8 3.1 %collective-permute-start.12 = (f32[2,2,512]{2,1,0:T(2,128)S(1)}, f32[2,2,512]{2,1,0:T(2,128)S(1)}, u32[]{:S(2)}, u32[]{:S(2)}) collective-permute-start(f32[2,2,512]{2,1,0:T(2,128)S(1)} %copy_bitcast_fusion), channel_id=1, source_target_pairs={{0,4},{4,0},{8,12},{12,8},{1,5},{5,1},{9,13},{13,9},{2,6},{6,2},{1... | collective-permute-start | bytes 24584 | tf_op jit(solution)/shard_map/ppermute | solution.py:282
  108.0 5.8 %collective-permute-start.16 = (f32[2,2,512]{2,1,0:T(2,128)S(1)}, f32[2,2,512]{2,1,0:T(2,128)S(1)}, u32[]{:S(2)}, u32[]{:S(2)}) collective-permute-start(f32[2,2,512]{2,1,0:T(2,128)S(1)} %add_add_fusion), channel_id=1, source_target_pairs={{0,2},{1,3},{2,0},{3,1},{4,6},{5,7},{6,4},{7,5},{8,10},{9,11},{10,... | collective-permute-start | bytes 24584 | tf_op jit(solution)/shard_map/ppermute | solution.py:282
  112.2 5.4 %collective-permute-start.17 = (f32[2,2,512]{2,1,0:T(2,128)S(1)}, f32[2,2,512]{2,1,0:T(2,128)S(1)}, u32[]{:S(2)}, u32[]{:S(2)}) collective-permute-start(f32[2,2,512]{2,1,0:T(2,128)S(1)} %add_add_fusion), channel_id=1, source_target_pairs={{0,3},{1,2},{2,1},{3,0},{4,7},{5,6},{6,5},{7,4},{8,11},{9,10},{10,... | collective-permute-start | bytes 24584 | tf_op jit(solution)/shard_map/ppermute | solution.py:282
  112.9 4.7 %collective-permute-start.15 = (f32[2,2,512]{2,1,0:T(2,128)S(1)}, f32[2,2,512]{2,1,0:T(2,128)S(1)}, u32[]{:S(2)}, u32[]{:S(2)}) collective-permute-start(f32[2,2,512]{2,1,0:T(2,128)S(1)} %add_add_fusion), channel_id=1, source_target_pairs={{0,1},{1,0},{2,3},{3,2},{4,5},{5,4},{6,7},{7,6},{8,9},{9,8},{10,11... | collective-permute-start | bytes 24584 | tf_op jit(solution)/shard_map/ppermute | solution.py:282

commit v4 on v3

--- a/solution.py
+++ b/solution.py
@@ -8,7 +8,7 @@
 from jax.experimental.pallas import tpu as pltpu
 from jax.sharding import PartitionSpec as P
 
-WEIGHTS = (8, 7, 8, 5)
+WEIGHTS = (8, 6, 8, 6)
 GROUPS = (2, 1, 1)
 HELPER_VMEM = 1024 * 1024
 TILE = 512
@@ -65,30 +65,35 @@
             copy.wait()
 
 
-def load_kernel(plan, source_ref, q_ref, slot_ref, x_ref, sem, sems):
-    first = fetches(plan, 0, q_ref, slot_ref, sems)
-    rows = pltpu.make_async_copy(source_ref, x_ref.at[pl.ds(0, source_ref.shape[0])], sem)
-    run(first, True)
-    rows.start()
-    run(first, False)
-    rows.wait()
+def load_kernel(plan, parts, *refs):
+    g_refs, (q_ref, slot_ref, x_ref, sems, slot_sems) = refs[:parts], refs[parts:]
+    copies = fetches(plan, 0, q_ref, slot_ref, slot_sems)
+    column = 0
+    for at, g_ref in enumerate(g_refs):
+        rows, columns = g_ref.shape
+        where = x_ref.at[pl.ds(0, rows), pl.ds(column, columns)]
+        copies.append(pltpu.make_async_copy(g_ref, where, sems.at[at]))
+        column += columns
+    run(copies, True)
+    run(copies, False)
 
 
 def load(own, total, query_grads, plan, room):
     vmem_spec = pl.BlockSpec(memory_space=pltpu.VMEM)
-    return pl.pallas_call(
-        functools.partial(load_kernel, plan),
-        in_specs=[pl.BlockSpec(memory_space=pl.ANY)] * 2,
+    depth = sum(part.shape[1] for part in own)
+    return pl.pallas_call(
+        functools.partial(load_kernel, plan, len(own)),
+        in_specs=[pl.BlockSpec(memory_space=pl.ANY)] * (len(own) + 1),
         out_specs=[vmem_spec] * 2,
         out_shape=[
             jax.ShapeDtypeStruct((room, plan.tile), jnp.bfloat16),
-            jax.ShapeDtypeStruct((total, own.shape[1]), jnp.bfloat16),
+            jax.ShapeDtypeStruct((total, depth), jnp.bfloat16),
         ],
-        scratch_shapes=[pltpu.SemaphoreType.DMA, pltpu.SemaphoreType.DMA((plan.strips,))],
+        scratch_shapes=[pltpu.SemaphoreType.DMA((len(own),)), pltpu.SemaphoreType.DMA((plan.strips,))],
         cost_estimate=pl.CostEstimate(flops=1024, bytes_accessed=1024, transcendentals=0),
         compiler_params=pltpu.CompilerParams(vmem_limit_bytes=HELPER_VMEM),
         name="load",
-    )(own, query_grads)
+    )(*own, query_grads)
 
 
 def project_kernel(parts, plan, later, fresh, laid, *refs):
@@ -245,16 +250,17 @@
     lanes = 128
     for number, source in enumerate(sources):
         pltpu.make_async_copy(held.at[number], held.at[number], sems.at[number]).wait()
+        totals = [None] * queries
+        begin = (number if number < pair else number - pair) * blocks * shard
+        for at in range(0, width, lanes):
+            block = held[number, :, :, at:at + lanes].reshape(blocks * shard, lanes).astype(jnp.float32)
+            for query in range(queries):
+                where = (slice(begin, begin + blocks * shard), slice(at, at + lanes))
+                rows = near_refs[query][(0, *where)] if number < pair else far_ref[(query, *where)]
+                term = rows * block
+                totals[query] = term if totals[query] is None else totals[query] + term
         for query in range(queries):
-            total = None
-            for at in range(0, width, lanes):
-                block = held[number, :, :, at:at + lanes].reshape(blocks * shard, lanes).astype(jnp.float32)
-                begin = (number if number < pair else number - pair) * blocks * shard
-                where = (query, slice(begin, begin + blocks * shard), slice(at, at + lanes))
-                rows = near_refs[query][(0, *where[1:])] if number < pair else far_ref[where]
-                term = rows * block
-                total = term if total is None else total + term
-            out_ref[source, query, :] = jnp.sum(total.T, axis=0)
+            out_ref[source, query, :] = jnp.sum(totals[query].T, axis=0)
 
 
 def score(sums, slots, ring, inp_size, pair, queries, blocks, shard):
@@ -298,6 +304,34 @@
     )(pltpu.with_memory_space_constraint(value, pltpu.VMEM), *others)
 
 
+def halve_kernel(source_ref, *refs):
+    *outs, sems = refs[-3:]
+    begin, copies = 0, []
+    for at, out_ref in enumerate(outs):
+        where = source_ref.at[:, pl.ds(begin, out_ref.shape[1])]
+        copies.append(pltpu.make_async_copy(where, out_ref, sems.at[at]))
+        begin += out_ref.shape[1]
+    run(copies, True)
+    run(copies, False)
+
+
+def halve(value, *others):
+    rows, columns = value.shape
+    first = columns // 256 * 128 or columns
+    if first == columns:
+        return [after(value, *others)]
+    return pl.pallas_call(
+        halve_kernel,
+        in_specs=[pl.BlockSpec(memory_space=pl.ANY)] * (1 + len(others)),
+        out_specs=[pl.BlockSpec(memory_space=pltpu.VMEM)] * 2,
+        out_shape=[jax.ShapeDtypeStruct((rows, part), value.dtype) for part in (first, columns - first)],
+        scratch_shapes=[pltpu.SemaphoreType.DMA((2,))],
+        cost_estimate=pl.CostEstimate(flops=1024, bytes_accessed=1024, transcendentals=0),
+        compiler_params=pltpu.CompilerParams(vmem_limit_bytes=HELPER_VMEM),
+        name="halve",
+    )(pltpu.with_memory_space_constraint(value, pltpu.VMEM), *others)
+
+
 def in_hbm(value):
     return pltpu.with_memory_space_constraint(value, pltpu.HBM)
 
@@ -373,12 +407,14 @@
     waiting = []
 
     def receive(mark, count=1):
-        pieces = []
+        ended = []
         for _ in range(min(count, len(coming))):
-            arrived = [after(piece, mark) for piece in coming.pop(0)]
-            waiting.extend(sum([[piece, flip(piece)] if pair == 2 else [piece] for piece in arrived], []))
-            pieces += arrived
-        return pieces
+            pieces = [halve(piece, mark, *waiting) for piece in coming.pop(0)]
+            for halves in zip(*pieces):
+                for half in halves:
+                    waiting.extend([half, flip(half)] if pair == 2 else [half])
+            ended += [halves[0] for halves in pieces]
+        return ended
 
     room = max(depth, STRIP_ROWS if depth >= STRIP_ROWS // 2 else 0)
     plans = [plan_of(query, 1, 0, depth, width, depth) for query in range(queries)]
@@ -391,7 +427,7 @@
             plans.append(plan_of(0, queries, group[0][0], length, width, room))
     plans.append(None)
 
-    slot, laid = load(own, pair * rows, query_grads, plans[0], room)
+    slot, laid = load(pieces_out or [own], pair * rows, query_grads, plans[0], room)
     sums = []
     mark = None
     for query in range(queries):

time: 118 us -> 113 us (0.958)
  waiting for transfers between devices: 19 us -> 15.7 us
  starting transfers between devices: 23.4 us -> 22.2 us
    ppermute x2, waiting for transfers between devices: 6.01 us -> 0.01 us  [step_along(): slots.append(lax.ppermute(ended, 'out', turn))]
    ppermute x5 -> x9, starting transfers between devices: 0.46 us -> 2.72 us  [flip(): return lax.ppermute(value, 'inp', [(at, at ^ 1) for at in range(inp_size)])]
    ppermute x5 -> x9, waiting for transfers between devices: 2.11 us -> 4.19 us  [flip(): return lax.ppermute(value, 'inp', [(at, at ^ 1) for at in range(inp_size)])]
    ppermute x4, starting transfers between devices: 6.77 us -> 5.13 us  [shift(): lax.ppermute(value, 'inp', [(at, (at + pair * by) % inp_size) for at in r...]
    ppermute x6, starting transfers between devices: 7.17 us -> 5.76 us  [xor_sum(): lax.ppermute(value, axis, [(at, at ^ other) for at in range(size)])]
    ppermute x2, starting transfers between devices: 6.39 us -> 5.03 us  [step_along(): slots.append(lax.ppermute(ended, 'out', turn))]
    pallas_call x1 -> x5, Pallas kernels: 4.16 us -> 3.52 us  [the longest x1 3.13 us: load(): pl.pallas_call(functools.partial(load_kernel, plan, len(own)), in_specs=[...]
  transfers between devices with their start and end apart: 18 -> 22, of which waited for: 11 -> 12; matrix products, arithmetic and copies ran while one was open for 0% -> 0% of each run, Pallas kernels for 60% -> 62%
where the time goes in v4:
time: 113 us
  Pallas kernels  73.9 us (65%)
  starting transfers between devices  22.2 us (20%)
  waiting for transfers between devices  15.7 us (14%)
    pallas_call x5, Pallas kernels, project(): pl.pallas_call(functools.partial(project_kernel, len(parts), plan, later,...  64.8 us
    ppermute x4, waiting for transfers between devices, shift(): lax.ppermute(value, 'inp', [(at, (at + pair * by) % inp_size) for at in r...  5.95 us
    ppermute x6, starting transfers between devices, xor_sum(): lax.ppermute(value, axis, [(at, at ^ other) for at in range(size)])  5.76 us
    ppermute x6, waiting for transfers between devices, xor_sum(): lax.ppermute(value, axis, [(at, at ^ other) for at in range(size)])  5.57 us
    ppermute x4, starting transfers between devices, shift(): lax.ppermute(value, 'inp', [(at, (at + pair * by) % inp_size) for at in r...  5.13 us
    ppermute x2, starting transfers between devices, step_along(): slots.append(lax.ppermute(ended, 'out', turn))  5.03 us
    ppermute x9, waiting for transfers between devices, flip(): return lax.ppermute(value, 'inp', [(at, at ^ 1) for at in range(inp_size)])  4.19 us
    ppermute x1, starting transfers between devices, shards(): slots.append(lax.ppermute(activations, 'out', turn))  3.59 us
  transfers between devices with their start and end apart: 22, of which 12 were waited for; matrix products, arithmetic and copies ran while one was open for 0% of the time, Pallas kernels for 62%

profile of v4, /device:TPU:0, one launch (start us, length us, event | category | flops | bytes accessed | tf_op | source)
XLA Modules:
  0.0 113.2 jit_solution(6885686374580096809)
XLA Ops:
  0.0 0.5 collective-permute-start
  0.5 3.6 %collective-permute-start.2 = (bf16[2,128,2048]{2,1,0:T(8,128)(2,1)}, bf16[2,128,2048]{2,1,0:T(8,128)(2,1)S(1)}, u32[]{:S(2)}, u32[]{:S(2)}) collective-permute-start(bf16[2,128,2048]{2,1,0:T(8,128)(2,1)} %refs_3_.1), channel_id=1, source_target_pairs={{1,0},{0,2},{2,3},{3,1},{5,4},{4,6},{6,7},{7,5},{9,8},{8,10},{10,1... | collective-permute-start | bytes 3145736 | tf_op jit(solution)/shard_map/ppermute | solution.py:393
  4.0 2.0 %cut.1 = (bf16[256,2048]{1,0:T(8,128)(2,1)S(1)}, bf16[256,1536]{1,0:T(8,128)(2,1)S(1)}, bf16[256,2048]{1,0:T(8,128)(2,1)S(1)}, bf16[256,1536]{1,0:T(8,128)(2,1)S(1)}) custom-call(bf16[256,7168]{1,0:T(8,128)(2,1)} %bitcast.12), custom_call_target="tpu_custom_call" | custom-call | tf_op jit(solution)/shard_map/cut/pallas_call | solution.py:349
  6.1 1.6 %collective-permute-start.1 = (bf16[256,2048]{1,0:T(8,128)(2,1)S(1)}, bf16[256,2048]{1,0:T(8,128)(2,1)S(1)}, u32[]{:S(2)}, u32[]{:S(2)}) collective-permute-start(bf16[256,2048]{1,0:T(8,128)(2,1)S(1)} %get-tuple-element.33.refs_0_), channel_id=1, source_target_pairs={{0,8},{4,12},{8,0},{12,4},{1,9},{5,13},{9,1},{13,5},{2,10},{6,14},... | collective-permute-start | bytes 3145736 | tf_op jit(solution)/shard_map/ppermute | solution.py:380
  7.7 0.5 collective-permute-start.7
  8.2 3.1 %load.1 = (bf16[8192,512]{1,0:T(8,128)(2,1)S(1)}, bf16[512,7168]{1,0:T(8,128)(2,1)S(1)}) custom-call(bf16[256,2048]{1,0:T(8,128)(2,1)S(1)} %get-tuple-element.33.refs_0_, bf16[256,1536]{1,0:T(8,128)(2,1)S(1)} %get-tuple-element.34.refs_1_, bf16[256,2048]{1,0:T(8,128)(2,1)S(1)} %get-tuple-element.35.refs_2_, bf16[256,1536]{1,0:T(8,128)(2,1)S(1)} %get-tuple-element.36.refs_3_, ...), custom_call_target="tpu_custom_call" | custom-call | flops 1024 | bytes 1024 | tf_op jit(solution)/shard_map/load/pallas_call | solution.py:84
  11.3 16.2 %project.5 = (f32[1,512,2048]{2,1,0:T(8,128)S(1)}, f32[8,128]{1,0:T(8,128)S(1)}, bf16[8192,512]{1,0:T(8,128)(2,1)S(1)}, bf16[512,7168]{1,0:T(8,128)(2,1)S(1)}) custom-call(bf16[256,7168]{1,0:T(8,128)(2,1)S(1)} %collective-permute-done.refs_0_, bf16[2,7168,2048]{2,1,0:T(8,128)(2,1)} %refs_4_.5, ...), custom_call_target="tpu_custom_call", output_to_operand_aliasing={{2}: (2, {}), {3}: (3, {})} | custom-call | flops 1024 | bytes 1024 | tf_op jit(solution)/shard_map/project/pallas_call | solution.py:211
  27.5 3.2 %collective-permute-start.12 = (bf16[2,128,2048]{2,1,0:T(8,128)(2,1)S(1)}, bf16[2,128,2048]{2,1,0:T(8,128)(2,1)S(1)}, u32[]{:S(2)}, u32[]{:S(2)}) collective-permute-start(bf16[2,128,2048]{2,1,0:T(8,128)(2,1)S(1)} %after.2.refs_4_), channel_id=1, source_target_pairs={{1,0},{0,2},{2,3},{3,1},{5,4},{4,6},{6,7},{7,5},{9,8},{8,10},{10,1... | collective-permute-start | bytes 3145736 | tf_op jit(solution)/shard_map/ppermute | solution.py:401
  30.7 1.5 %collective-permute-start.4 = (bf16[256,2048]{1,0:T(8,128)(2,1)S(1)}, bf16[256,2048]{1,0:T(8,128)(2,1)S(1)}, u32[]{:S(2)}, u32[]{:S(2)}) collective-permute-start(bf16[256,2048]{1,0:T(8,128)(2,1)S(1)} %get-tuple-element.35.refs_2_), channel_id=1, source_target_pairs={{0,8},{4,12},{8,0},{12,4},{1,9},{5,13},{9,1},{13,5},{2,10},{6,14},... | collective-permute-start | bytes 3145736 | tf_op jit(solution)/shard_map/ppermute | solution.py:380
  32.2 0.1 halve.4
  32.4 0.1 collective-permute-start.5
  32.4 0.5 collective-permute-start.6
  32.9 15.9 %project.6 = (f32[1,512,2048]{2,1,0:T(8,128)S(1)}, f32[8,128]{1,0:T(8,128)S(1)}, bf16[8192,512]{1,0:T(8,128)(2,1)S(1)}, bf16[512,7168]{1,0:T(8,128)(2,1)S(1)}) custom-call(bf16[2,7168,2048]{2,1,0:T(8,128)(2,1)} %refs_4_.5, bf16[8192,512]{1,0:T(8,128)(2,1)S(1)} %get-tuple-element.40.refs_1_, ...), custom_call_target="tpu_custom_call", output_to_operand_aliasing={{2}: (1, {}), {3}: (2, {})} | custom-call | flops 1024 | bytes 1024 | tf_op jit(solution)/shard_map/project/pallas_call | solution.py:211
  48.9 0.1 collective-permute-done.7.source_ref
  49.0 0.1 halve.5
  49.1 0.1 collective-permute-start.8
  49.2 0.5 collective-permute-start.9
  49.7 1.5 %collective-permute-start.3 = (bf16[256,1536]{1,0:T(8,128)(2,1)S(1)}, bf16[256,1536]{1,0:T(8,128)(2,1)S(1)}, u32[]{:S(2)}, u32[]{:S(2)}) collective-permute-start(bf16[256,1536]{1,0:T(8,128)(2,1)S(1)} %get-tuple-element.36.refs_3_), channel_id=1, source_target_pairs={{0,8},{4,12},{8,0},{12,4},{1,9},{5,13},{9,1},{13,5},{2,10},{6,14},... | collective-permute-start | bytes 2359304 | tf_op jit(solution)/shard_map/ppermute | solution.py:380
  51.2 0.3 collective-permute-done.9.refs_7_
  51.4 16.2 %project.7 = (f32[2,512,2048]{2,1,0:T(8,128)S(1)}, f32[8,128]{1,0:T(8,128)S(1)}, bf16[8192,512]{1,0:T(8,128)(2,1)S(1)}) custom-call(bf16[256,1024]{1,0:T(8,128)(2,1)S(1)} %get-tuple-element.43.refs_3_.refs_1_.refs_0_, bf16[256,1024]{1,0:T(8,128)(2,1)S(1)} %collective-permute-done.5.refs_2_.refs_1_, ...), custom_call_target="tpu_custom_call", output_to_operand_aliasing={{2}: (9, {})} | custom-call | flops 1024 | bytes 1024 | tf_op jit(solution)/shard_map/project/pallas_call | solution.py:211
  67.7 1.8 %collective-permute-start.15 = (bf16[2,128,2048]{2,1,0:T(8,128)(2,1)S(1)}, bf16[2,128,2048]{2,1,0:T(8,128)(2,1)S(1)}, u32[]{:S(2)}, u32[]{:S(2)}) collective-permute-start(bf16[2,128,2048]{2,1,0:T(8,128)(2,1)S(1)} %after.3.refs_8_.refs_5_), channel_id=1, source_target_pairs={{1,0},{0,2},{2,3},{3,1},{5,4},{4,6},{6,7},{7,5},{9,8},{8,10},{10,1... | collective-permute-start | bytes 3145736 | tf_op jit(solution)/shard_map/ppermute | solution.py:401
  69.5 1.9 %collective-permute-done.4.source_ref = bf16[256,2048]{1,0:T(8,128)(2,1)S(1)} collective-permute-done((bf16[256,2048]{1,0:T(8,128)(2,1)S(1)}, bf16[256,2048]{1,0:T(8,128)(2,1)S(1)}, u32[]{:S(2)}, u32[]{:S(2)}) %collective-permute-start.4) | collective-permute-done | bytes 1048608 | tf_op jit(solution)/shard_map/ppermute | solution.py:380
  71.5 0.1 halve.6
  71.6 0.1 collective-permute-start.10
  71.7 0.5 collective-permute-start.11
  72.2 1.4 %collective-permute-done.10.refs_1_ = bf16[256,1024]{1,0:T(8,128)(2,1)S(1)} collective-permute-done((bf16[256,1024]{1,0:T(8,128)(2,1)S(1)}, bf16[256,1024]{1,0:T(8,128)(2,1)S(1)}, u32[]{:S(2)}, u32[]{:S(2)}) %collective-permute-start.10) | collective-permute-done | bytes 524320 | tf_op jit(solution)/shard_map/ppermute | solution.py:377
  73.6 0.7 collective-permute-done.11.refs_3_
  74.3 9.4 %project.8 = (f32[2,512,2048]{2,1,0:T(8,128)S(1)}, f32[8,128]{1,0:T(8,128)S(1)}, bf16[8192,512]{1,0:T(8,128)(2,1)S(1)}) custom-call(bf16[256,1024]{1,0:T(8,128)(2,1)S(1)} %get-tuple-element.51.refs_0_.refs_7_, bf16[256,1024]{1,0:T(8,128)(2,1)S(1)} %collective-permute-done.10.refs_1_, ...), custom_call_target="tpu_custom_call", output_to_operand_aliasing={{2}: (5, {}), {0}: (6, {})} | custom-call | flops 1024 | bytes 1024 | tf_op jit(solution)/shard_map/project/pallas_call | solution.py:211
  83.7 3.9 %collective-permute-done.3.source_ref = bf16[256,1536]{1,0:T(8,128)(2,1)S(1)} collective-permute-done((bf16[256,1536]{1,0:T(8,128)(2,1)S(1)}, bf16[256,1536]{1,0:T(8,128)(2,1)S(1)}, u32[]{:S(2)}, u32[]{:S(2)}) %collective-permute-start.3) | collective-permute-done | bytes 786464 | tf_op jit(solution)/shard_map/ppermute | solution.py:380
  87.6 0.1 halve.7
  87.7 0.1 collective-permute-start.13
  87.8 0.5 collective-permute-start.14
  88.3 1.2 %collective-permute-done.13.refs_1_ = bf16[256,768]{1,0:T(8,128)(2,1)S(1)} collective-permute-done((bf16[256,768]{1,0:T(8,128)(2,1)S(1)}, bf16[256,768]{1,0:T(8,128)(2,1)S(1)}, u32[]{:S(2)}, u32[]{:S(2)}) %collective-permute-start.13) | collective-permute-done | bytes 393248 | tf_op jit(solution)/shard_map/ppermute | solution.py:377
  89.5 0.6 collective-permute-done.14.refs_3_
  90.1 7.1 %project.9 = (f32[2,512,2048]{2,1,0:T(8,128)S(1)}, f32[8,128]{1,0:T(8,128)}, bf16[8192,512]{1,0:T(8,128)(2,1)S(1)}) custom-call(bf16[256,768]{1,0:T(8,128)(2,1)S(1)} %get-tuple-element.56.refs_0_.refs_7_, bf16[256,768]{1,0:T(8,128)(2,1)S(1)} %collective-permute-done.13.refs_1_, ...), custom_call_target="tpu_custom_call", output_to_operand_aliasing={{2}: (5, {}), {0}: (6, {})} | custom-call | flops 1024 | bytes 1024 | tf_op jit(solution)/shard_map/project/pallas_call | solution.py:211
  97.2 0.0 copy-start.1
  97.2 3.5 %score.1 = f32[4,2,256]{2,1,0:T(2,128)S(1)} custom-call(f32[1,512,2048]{2,1,0:T(8,128)S(1)} %get-tuple-element.39.refs_0_, f32[1,512,2048]{2,1,0:T(8,128)S(1)} %get-tuple-element.44.refs_1_, f32[2,512,2048]{2,1,0:T(8,128)S(1)} %get-tuple-element.60.refs_2_, bf16[2,128,2048]{2,1,0:T(8,128)(2,1)} %refs_3_.1, bf16[2,128,2048]{2,1,0:T(8,128)(2,1)S(1)} %after.2.refs_4_, ...), custom_call_target="tpu_custom_call" | custom-call | tf_op jit(solution)/shard_map/score/pallas_call | solution.py:268
  100.8 1.1 collective-permute-start.17
  101.9 0.0 collective-permute-start.18
  101.9 1.1 collective-permute-start.16
  103.0 0.4 convert_reduce_fusion
  103.4 1.1 collective-permute-done.17
  104.5 0.5 collective-permute-done.18
  105.0 2.1 %collective-permute-start.20 = (f32[2,2,512]{2,1,0:T(2,128)S(1)}, f32[2,2,512]{2,1,0:T(2,128)S(1)}, u32[]{:S(2)}, u32[]{:S(2)}) collective-permute-start(f32[2,2,512]{2,1,0:T(2,128)S(1)} %add_add_fusion), channel_id=1, source_target_pairs={{0,2},{1,3},{2,0},{3,1},{4,6},{5,7},{6,4},{7,5},{8,10},{9,11},{10,... | collective-permute-start | bytes 24584 | tf_op jit(solution)/shard_map/ppermute | solution.py:288
  107.1 1.5 %collective-permute-start.19 = (f32[2,2,512]{2,1,0:T(2,128)S(1)}, f32[2,2,512]{2,1,0:T(2,128)S(1)}, u32[]{:S(2)}, u32[]{:S(2)}) collective-permute-start(f32[2,2,512]{2,1,0:T(2,128)S(1)} %add_add_fusion), channel_id=1, source_target_pairs={{0,1},{1,0},{2,3},{3,2},{4,5},{5,4},{6,7},{7,6},{8,9},{9,8},{10,11... | collective-permute-start | bytes 24584 | tf_op jit(solution)/shard_map/ppermute | solution.py:288
  108.6 1.0 collective-permute-done.20
  109.6 2.9 %collective-permute-done.21 = f32[2,2,512]{2,1,0:T(2,128)S(1)} collective-permute-done((f32[2,2,512]{2,1,0:T(2,128)S(1)}, f32[2,2,512]{2,1,0:T(2,128)S(1)}, u32[]{:S(2)}, u32[]{:S(2)}) %collective-permute-start.21) | collective-permute-done | bytes 8224 | tf_op jit(solution)/shard_map/ppermute | solution.py:288
  112.6 0.6 add_multiply_fusion
  (20 shorter events, 0.1 us)
Async XLA Ops:
  0.0 11.3 %collective-permute-start = (bf16[256,7168]{1,0:T(8,128)(2,1)}, bf16[256,7168]{1,0:T(8,128)(2,1)S(1)}, u32[]{:S(2)}, u32[]{:S(2)}) collective-permute-start(bf16[256,7168]{1,0:T(8,128)(2,1)} %bitcast.11), channel_id=1, source_target_pairs={{0,4},{4,0},{8,12},{12,8},{1,5},{5,1},{9,13},{13,9},{2,6},{6,2},{1... | collective-permute-start | bytes 11010056 | tf_op jit(solution)/shard_map/ppermute | solution.py:377
  0.5 27.1 %collective-permute-start.2 = (bf16[2,128,2048]{2,1,0:T(8,128)(2,1)}, bf16[2,128,2048]{2,1,0:T(8,128)(2,1)S(1)}, u32[]{:S(2)}, u32[]{:S(2)}) collective-permute-start(bf16[2,128,2048]{2,1,0:T(8,128)(2,1)} %refs_3_.1), channel_id=1, source_target_pairs={{1,0},{0,2},{2,3},{3,1},{5,4},{4,6},{6,7},{7,5},{9,8},{8,10},{10,1... | collective-permute-start | bytes 3145736 | tf_op jit(solution)/shard_map/ppermute | solution.py:393
  6.1 26.2 %collective-permute-start.1 = (bf16[256,2048]{1,0:T(8,128)(2,1)S(1)}, bf16[256,2048]{1,0:T(8,128)(2,1)S(1)}, u32[]{:S(2)}, u32[]{:S(2)}) collective-permute-start(bf16[256,2048]{1,0:T(8,128)(2,1)S(1)} %get-tuple-element.33.refs_0_), channel_id=1, source_target_pairs={{0,8},{4,12},{8,0},{12,4},{1,9},{5,13},{9,1},{13,5},{2,10},{6,14},... | collective-permute-start | bytes 3145736 | tf_op jit(solution)/shard_map/ppermute | solution.py:380
  7.7 41.3 %collective-permute-start.7 = (bf16[256,1536]{1,0:T(8,128)(2,1)S(1)}, bf16[256,1536]{1,0:T(8,128)(2,1)S(1)}, u32[]{:S(2)}, u32[]{:S(2)}) collective-permute-start(bf16[256,1536]{1,0:T(8,128)(2,1)S(1)} %get-tuple-element.34.refs_1_), channel_id=1, source_target_pairs={{0,8},{4,12},{8,0},{12,4},{1,9},{5,13},{9,1},{13,5},{2,10},{6,14},... | collective-permute-start | bytes 2359304 | tf_op jit(solution)/shard_map/ppermute | solution.py:380
  27.5 40.1 %collective-permute-start.12 = (bf16[2,128,2048]{2,1,0:T(8,128)(2,1)S(1)}, bf16[2,128,2048]{2,1,0:T(8,128)(2,1)S(1)}, u32[]{:S(2)}, u32[]{:S(2)}) collective-permute-start(bf16[2,128,2048]{2,1,0:T(8,128)(2,1)S(1)} %after.2.refs_4_), channel_id=1, source_target_pairs={{1,0},{0,2},{2,3},{3,1},{5,4},{4,6},{6,7},{7,5},{9,8},{8,10},{10,1... | collective-permute-start | bytes 3145736 | tf_op jit(solution)/shard_map/ppermute | solution.py:401
  30.7 40.7 %collective-permute-start.4 = (bf16[256,2048]{1,0:T(8,128)(2,1)S(1)}, bf16[256,2048]{1,0:T(8,128)(2,1)S(1)}, u32[]{:S(2)}, u32[]{:S(2)}) collective-permute-start(bf16[256,2048]{1,0:T(8,128)(2,1)S(1)} %get-tuple-element.35.refs_2_), channel_id=1, source_target_pairs={{0,8},{4,12},{8,0},{12,4},{1,9},{5,13},{9,1},{13,5},{2,10},{6,14},... | collective-permute-start | bytes 3145736 | tf_op jit(solution)/shard_map/ppermute | solution.py:380
  32.4 16.6 %collective-permute-start.5 = (bf16[256,1024]{1,0:T(8,128)(2,1)S(1)}, bf16[256,1024]{1,0:T(8,128)(2,1)S(1)}, u32[]{:S(2)}, u32[]{:S(2)}) collective-permute-start(bf16[256,1024]{1,0:T(8,128)(2,1)S(1)} %get-tuple-element.43.refs_3_.refs_1_.refs_0_), channel_id=1, source_target_pairs={{0,4},{4,0},{8,12},{12,8},{1,5},{5,1},{9,13},{13,9},{2,6},{6,2},{1... | collective-permute-start | bytes 1572872 | tf_op jit(solution)/shard_map/ppermute | solution.py:377
  32.4 16.6 %collective-permute-start.6 = (bf16[256,1024]{1,0:T(8,128)(2,1)S(1)}, bf16[256,1024]{1,0:T(8,128)(2,1)S(1)}, u32[]{:S(2)}, u32[]{:S(2)}) collective-permute-start(bf16[256,1024]{1,0:T(8,128)(2,1)S(1)} %get-tuple-element.45.refs_3_.refs_2_), channel_id=1, source_target_pairs={{0,4},{4,0},{8,12},{12,8},{1,5},{5,1},{9,13},{13,9},{2,6},{6,2},{1... | collective-permute-start | bytes 1572872 | tf_op jit(solution)/shard_map/ppermute | solution.py:377
  49.1 2.1 %collective-permute-start.8 = (bf16[256,768]{1,0:T(8,128)(2,1)S(1)}, bf16[256,768]{1,0:T(8,128)(2,1)S(1)}, u32[]{:S(2)}, u32[]{:S(2)}) collective-permute-start(bf16[256,768]{1,0:T(8,128)(2,1)S(1)} %get-tuple-element.47.refs_4_.refs_10_), channel_id=1, source_target_pairs={{0,4},{4,0},{8,12},{12,8},{1,5},{5,1},{9,13},{13,9},{2,6},{6,2},{1... | collective-permute-start | bytes 1179656 | tf_op jit(solution)/shard_map/ppermute | solution.py:377
  49.2 2.3 %collective-permute-start.9 = (bf16[256,768]{1,0:T(8,128)(2,1)S(1)}, bf16[256,768]{1,0:T(8,128)(2,1)S(1)}, u32[]{:S(2)}, u32[]{:S(2)}) collective-permute-start(bf16[256,768]{1,0:T(8,128)(2,1)S(1)} %get-tuple-element.48.refs_6_), channel_id=1, source_target_pairs={{0,4},{4,0},{8,12},{12,8},{1,5},{5,1},{9,13},{13,9},{2,6},{6,2},{1... | collective-permute-start | bytes 1179656 | tf_op jit(solution)/shard_map/ppermute | solution.py:377
  49.7 38.0 %collective-permute-start.3 = (bf16[256,1536]{1,0:T(8,128)(2,1)S(1)}, bf16[256,1536]{1,0:T(8,128)(2,1)S(1)}, u32[]{:S(2)}, u32[]{:S(2)}) collective-permute-start(bf16[256,1536]{1,0:T(8,128)(2,1)S(1)} %get-tuple-element.36.refs_3_), channel_id=1, source_target_pairs={{0,8},{4,12},{8,0},{12,4},{1,9},{5,13},{9,1},{13,5},{2,10},{6,14},... | collective-permute-start | bytes 2359304 | tf_op jit(solution)/shard_map/ppermute | solution.py:380
  67.7 29.5 %collective-permute-start.15 = (bf16[2,128,2048]{2,1,0:T(8,128)(2,1)S(1)}, bf16[2,128,2048]{2,1,0:T(8,128)(2,1)S(1)}, u32[]{:S(2)}, u32[]{:S(2)}) collective-permute-start(bf16[2,128,2048]{2,1,0:T(8,128)(2,1)S(1)} %after.3.refs_8_.refs_5_), channel_id=1, source_target_pairs={{1,0},{0,2},{2,3},{3,1},{5,4},{4,6},{6,7},{7,5},{9,8},{8,10},{10,1... | collective-permute-start | bytes 3145736 | tf_op jit(solution)/shard_map/ppermute | solution.py:401
  71.6 2.0 %collective-permute-start.10 = (bf16[256,1024]{1,0:T(8,128)(2,1)S(1)}, bf16[256,1024]{1,0:T(8,128)(2,1)S(1)}, u32[]{:S(2)}, u32[]{:S(2)}) collective-permute-start(bf16[256,1024]{1,0:T(8,128)(2,1)S(1)} %get-tuple-element.51.refs_0_.refs_7_), channel_id=1, source_target_pairs={{0,4},{4,0},{8,12},{12,8},{1,5},{5,1},{9,13},{13,9},{2,6},{6,2},{1... | collective-permute-start | bytes 1572872 | tf_op jit(solution)/shard_map/ppermute | solution.py:377
  71.7 2.6 %collective-permute-start.11 = (bf16[256,1024]{1,0:T(8,128)(2,1)S(1)}, bf16[256,1024]{1,0:T(8,128)(2,1)S(1)}, u32[]{:S(2)}, u32[]{:S(2)}) collective-permute-start(bf16[256,1024]{1,0:T(8,128)(2,1)S(1)} %get-tuple-element.52.refs_2_), channel_id=1, source_target_pairs={{0,4},{4,0},{8,12},{12,8},{1,5},{5,1},{9,13},{13,9},{2,6},{6,2},{1... | collective-permute-start | bytes 1572872 | tf_op jit(solution)/shard_map/ppermute | solution.py:377
  87.7 1.8 %collective-permute-start.13 = (bf16[256,768]{1,0:T(8,128)(2,1)S(1)}, bf16[256,768]{1,0:T(8,128)(2,1)S(1)}, u32[]{:S(2)}, u32[]{:S(2)}) collective-permute-start(bf16[256,768]{1,0:T(8,128)(2,1)S(1)} %get-tuple-element.56.refs_0_.refs_7_), channel_id=1, source_target_pairs={{0,4},{4,0},{8,12},{12,8},{1,5},{5,1},{9,13},{13,9},{2,6},{6,2},{1... | collective-permute-start | bytes 1179656 | tf_op jit(solution)/shard_map/ppermute | solution.py:377
  87.8 2.3 %collective-permute-start.14 = (bf16[256,768]{1,0:T(8,128)(2,1)S(1)}, bf16[256,768]{1,0:T(8,128)(2,1)S(1)}, u32[]{:S(2)}, u32[]{:S(2)}) collective-permute-start(bf16[256,768]{1,0:T(8,128)(2,1)S(1)} %get-tuple-element.57.refs_2_), channel_id=1, source_target_pairs={{0,4},{4,0},{8,12},{12,8},{1,5},{5,1},{9,13},{13,9},{2,6},{6,2},{1... | collective-permute-start | bytes 1179656 | tf_op jit(solution)/shard_map/ppermute | solution.py:377
  97.2 5.8 %copy-start = (s32[2,512]{1,0:T(2,128)S(1)}, s32[2,512]{1,0:T(2,128)}, u32[]{:S(2)}) copy-start(s32[2,512]{1,0:T(2,128)} %param.8) | copy-start | bytes 12292
  97.2 11.4 %copy-start.1 = (s32[2,512]{1,0:T(2,128)S(1)}, s32[2,512]{1,0:T(2,128)}, u32[]{:S(2)}) copy-start(s32[2,512]{1,0:T(2,128)} %param.9) | copy-start | bytes 12292
  100.8 3.7 %collective-permute-start.17 = (f32[2,2,512]{2,1,0:T(2,128)S(1)}, f32[2,2,512]{2,1,0:T(2,128)S(1)}, u32[]{:S(2)}, u32[]{:S(2)}) collective-permute-start(f32[2,2,512]{2,1,0:T(2,128)S(1)} %copy_bitcast_fusion), channel_id=1, source_target_pairs={{0,8},{4,12},{8,0},{12,4},{1,9},{5,13},{9,1},{13,5},{2,10},{6,14},... | collective-permute-start | bytes 24584 | tf_op jit(solution)/shard_map/ppermute | solution.py:288
  101.9 3.1 %collective-permute-start.18 = (f32[2,2,512]{2,1,0:T(2,128)S(1)}, f32[2,2,512]{2,1,0:T(2,128)S(1)}, u32[]{:S(2)}, u32[]{:S(2)}) collective-permute-start(f32[2,2,512]{2,1,0:T(2,128)S(1)} %copy_bitcast_fusion), channel_id=1, source_target_pairs={{0,12},{4,8},{8,4},{12,0},{1,13},{5,9},{9,5},{13,1},{2,14},{6,10},... | collective-permute-start | bytes 24584 | tf_op jit(solution)/shard_map/ppermute | solution.py:288
  101.9 3.1 %collective-permute-start.16 = (f32[2,2,512]{2,1,0:T(2,128)S(1)}, f32[2,2,512]{2,1,0:T(2,128)S(1)}, u32[]{:S(2)}, u32[]{:S(2)}) collective-permute-start(f32[2,2,512]{2,1,0:T(2,128)S(1)} %copy_bitcast_fusion), channel_id=1, source_target_pairs={{0,4},{4,0},{8,12},{12,8},{1,5},{5,1},{9,13},{13,9},{2,6},{6,2},{1... | collective-permute-start | bytes 24584 | tf_op jit(solution)/shard_map/ppermute | solution.py:288
  105.0 4.6 %collective-permute-start.20 = (f32[2,2,512]{2,1,0:T(2,128)S(1)}, f32[2,2,512]{2,1,0:T(2,128)S(1)}, u32[]{:S(2)}, u32[]{:S(2)}) collective-permute-start(f32[2,2,512]{2,1,0:T(2,128)S(1)} %add_add_fusion), channel_id=1, source_target_pairs={{0,2},{1,3},{2,0},{3,1},{4,6},{5,7},{6,4},{7,5},{8,10},{9,11},{10,... | collective-permute-start | bytes 24584 | tf_op jit(solution)/shard_map/ppermute | solution.py:288
  107.1 5.4 %collective-permute-start.21 = (f32[2,2,512]{2,1,0:T(2,128)S(1)}, f32[2,2,512]{2,1,0:T(2,128)S(1)}, u32[]{:S(2)}, u32[]{:S(2)}) collective-permute-start(f32[2,2,512]{2,1,0:T(2,128)S(1)} %add_add_fusion), channel_id=1, source_target_pairs={{0,3},{1,2},{2,1},{3,0},{4,7},{5,6},{6,5},{7,4},{8,11},{9,10},{10,... | collective-permute-start | bytes 24584 | tf_op jit(solution)/shard_map/ppermute | solution.py:288
  107.1 5.4 %collective-permute-start.19 = (f32[2,2,512]{2,1,0:T(2,128)S(1)}, f32[2,2,512]{2,1,0:T(2,128)S(1)}, u32[]{:S(2)}, u32[]{:S(2)}) collective-permute-start(f32[2,2,512]{2,1,0:T(2,128)S(1)} %add_add_fusion), channel_id=1, source_target_pairs={{0,1},{1,0},{2,3},{3,2},{4,5},{5,4},{6,7},{7,6},{8,9},{9,8},{10,11... | collective-permute-start | bytes 24584 | tf_op jit(solution)/shard_map/ppermute | solution.py:288

commit v5 on v4

--- a/solution.py
+++ b/solution.py
@@ -8,7 +8,7 @@
 from jax.experimental.pallas import tpu as pltpu
 from jax.sharding import PartitionSpec as P
 
-WEIGHTS = (8, 6, 8, 6)
+WEIGHTS = (8, 7, 8, 5)
 GROUPS = (2, 1, 1)
 HELPER_VMEM = 1024 * 1024
 TILE = 512
@@ -233,22 +233,27 @@
         by, other = divmod(number, pair)
         source = lax.rem(me - pair * by + inp_size, inp_size)
         sources.append(jnp.bitwise_xor(source, other) if pair == 2 else source)
-    for number, source in enumerate(sources):
+
+    def bring(number):
+        source = sources[number]
         if len(a_refs) == 1:
             begin = pl.multiple_of(source * shard, shard)
             pltpu.make_async_copy(
                 a_refs[0].at[:, pl.ds(begin, shard), :], held.at[number], sems.at[number]
             ).start()
-            continue
+            return
         for at, a_ref in enumerate(a_refs):
             for place, spot in enumerate(ring):
 
                 @pl.when((here == spot) & (source == ring[place - at]))
-                def _(a_ref=a_ref, number=number):
+                def _(a_ref=a_ref):
                     pltpu.make_async_copy(a_ref, held.at[number], sems.at[number]).start()
 
     lanes = 128
+    bring(0)
     for number, source in enumerate(sources):
+        if number + 1 < inp_size:
+            bring(number + 1)
         pltpu.make_async_copy(held.at[number], held.at[number], sems.at[number]).wait()
         totals = [None] * queries
         begin = (number if number < pair else number - pair) * blocks * shard
@@ -386,7 +391,9 @@
     line = inp_size == out_size and activations.shape[1] == shard and out_size > 1
     ring = list(range(0, out_size, 2)) + list(range(1, out_size, 2))[::-1]
     turn = [(ring[at - 1], ring[at]) for at in range(out_size)]
-    pieces_out = cut(own, spans) if chips > 1 else []
+    pieces_out = []
+    if chips > 1:
+        pieces_out = cut(own, spans[:1]) + (cut(own, spans[1:]) if chunks > 1 else [])
 
     slots = [activations]
     if line:

time: 113 us -> 114 us (level)
  Pallas kernels: 73.9 us -> 75.1 us
    ppermute x9, waiting for transfers between devices: 4.19 us -> 5.7 us  [flip(): return lax.ppermute(value, 'inp', [(at, at ^ 1) for at in range(inp_size)])]
    pallas_call x1 -> x2, Pallas kernels: 2.04 us -> 2.94 us  [cut(): pl.pallas_call(functools.partial(cut_kernel, spans), in_specs=[pl.BlockSp...]
  transfers between devices with their start and end apart: 22 -> 22, of which waited for: 12 -> 13; matrix products, arithmetic and copies ran while one was open for 0% -> 0% of each run, Pallas kernels for 62% -> 63%
where the time goes in v5:
time: 114 us
  Pallas kernels  75.1 us (66%)
  starting transfers between devices  21.3 us (19%)
  waiting for transfers between devices  15.8 us (14%)
    pallas_call x5, Pallas kernels, project(): pl.pallas_call(functools.partial(project_kernel, len(parts), plan, later,...  64.9 us
    ppermute x6, starting transfers between devices, xor_sum(): lax.ppermute(value, axis, [(at, at ^ other) for at in range(size)])  5.76 us
    ppermute x9, waiting for transfers between devices, flip(): return lax.ppermute(value, 'inp', [(at, at ^ 1) for at in range(inp_size)])  5.7 us
    ppermute x6, waiting for transfers between devices, xor_sum(): lax.ppermute(value, axis, [(at, at ^ other) for at in range(size)])  5.28 us
    ppermute x4, starting transfers between devices, shift(): lax.ppermute(value, 'inp', [(at, (at + pair * by) % inp_size) for at in r...  5.19 us
    ppermute x4, waiting for transfers between devices, shift(): lax.ppermute(value, 'inp', [(at, (at + pair * by) % inp_size) for at in r...  4.83 us
    ppermute x2, starting transfers between devices, step_along(): slots.append(lax.ppermute(ended, 'out', turn))  4.06 us
    pallas_call x1, Pallas kernels, score(): pl.pallas_call(functools.partial(score_kernel, inp_size, pair, queries, r...  3.76 us
  transfers between devices with their start and end apart: 22, of which 13 were waited for; matrix products, arithmetic and copies ran while one was open for 0% of the time, Pallas kernels for 63%

profile of v5, /device:TPU:0, one launch (start us, length us, event | category | flops | bytes accessed | tf_op | source)
XLA Modules:
  0.0 113.6 jit_solution(8711990608864097187)
XLA Ops:
  0.0 0.5 collective-permute-start
  0.5 3.6 %collective-permute-start.2 = (bf16[2,128,2048]{2,1,0:T(8,128)(2,1)}, bf16[2,128,2048]{2,1,0:T(8,128)(2,1)S(1)}, u32[]{:S(2)}, u32[]{:S(2)}) collective-permute-start(bf16[2,128,2048]{2,1,0:T(8,128)(2,1)} %refs_3_.1), channel_id=1, source_target_pairs={{1,0},{0,2},{2,3},{3,1},{5,4},{4,6},{6,7},{7,5},{9,8},{8,10},{10,1... | collective-permute-start | bytes 3145736 | tf_op jit(solution)/shard_map/ppermute | solution.py:400
  4.0 1.2 %cut.2.refs_0_ = bf16[256,2048]{1,0:T(8,128)(2,1)S(1)} custom-call(bf16[256,7168]{1,0:T(8,128)(2,1)} %bitcast.12), custom_call_target="tpu_custom_call" | custom-call | tf_op jit(solution)/shard_map/cut/pallas_call | solution.py:354
  5.3 1.6 %collective-permute-start.1 = (bf16[256,2048]{1,0:T(8,128)(2,1)S(1)}, bf16[256,2048]{1,0:T(8,128)(2,1)S(1)}, u32[]{:S(2)}, u32[]{:S(2)}) collective-permute-start(bf16[256,2048]{1,0:T(8,128)(2,1)S(1)} %cut.2.refs_0_), channel_id=1, source_target_pairs={{0,8},{4,12},{8,0},{12,4},{1,9},{5,13},{9,1},{13,5},{2,10},{6,14},... | collective-permute-start | bytes 3145736 | tf_op jit(solution)/shard_map/ppermute | solution.py:385
  6.9 1.7 %cut.3 = (bf16[256,1792]{1,0:T(8,128)(2,1)S(1)}, bf16[256,2048]{1,0:T(8,128)(2,1)S(1)}, bf16[256,1280]{1,0:T(8,128)(2,1)S(1)}) custom-call(bf16[256,7168]{1,0:T(8,128)(2,1)} %bitcast.13), custom_call_target="tpu_custom_call" | custom-call | tf_op jit(solution)/shard_map/cut/pallas_call | solution.py:354
  8.6 0.6 collective-permute-start.7
  9.2 3.1 %load.1 = (bf16[8192,512]{1,0:T(8,128)(2,1)S(1)}, bf16[512,7168]{1,0:T(8,128)(2,1)S(1)}) custom-call(bf16[256,2048]{1,0:T(8,128)(2,1)S(1)} %cut.2.refs_0_, bf16[256,1792]{1,0:T(8,128)(2,1)S(1)} %get-tuple-element.32.refs_1_, bf16[256,2048]{1,0:T(8,128)(2,1)S(1)} %get-tuple-element.33.refs_2_, bf16[256,1280]{1,0:T(8,128)(2,1)S(1)} %get-tuple-element.34.refs_3_, ...), custom_call_target="tpu_custom_call" | custom-call | flops 1024 | bytes 1024 | tf_op jit(solution)/shard_map/load/pallas_call | solution.py:84
  12.3 16.2 %project.5 = (f32[1,512,2048]{2,1,0:T(8,128)S(1)}, f32[8,128]{1,0:T(8,128)S(1)}, bf16[8192,512]{1,0:T(8,128)(2,1)S(1)}, bf16[512,7168]{1,0:T(8,128)(2,1)S(1)}) custom-call(bf16[256,7168]{1,0:T(8,128)(2,1)S(1)} %collective-permute-done.refs_0_, bf16[2,7168,2048]{2,1,0:T(8,128)(2,1)} %refs_4_.5, ...), custom_call_target="tpu_custom_call", output_to_operand_aliasing={{2}: (2, {}), {3}: (3, {})} | custom-call | flops 1024 | bytes 1024 | tf_op jit(solution)/shard_map/project/pallas_call | solution.py:211
  28.5 2.2 %collective-permute-start.12 = (bf16[2,128,2048]{2,1,0:T(8,128)(2,1)S(1)}, bf16[2,128,2048]{2,1,0:T(8,128)(2,1)S(1)}, u32[]{:S(2)}, u32[]{:S(2)}) collective-permute-start(bf16[2,128,2048]{2,1,0:T(8,128)(2,1)S(1)} %after.2.refs_4_), channel_id=1, source_target_pairs={{1,0},{0,2},{2,3},{3,1},{5,4},{4,6},{6,7},{7,5},{9,8},{8,10},{10,1... | collective-permute-start | bytes 3145736 | tf_op jit(solution)/shard_map/ppermute | solution.py:408
  30.7 0.6 collective-permute-done.1.source_ref
  31.3 0.1 halve.4
  31.5 0.1 collective-permute-start.5
  31.5 0.5 collective-permute-start.6
  32.0 1.5 %collective-permute-start.4 = (bf16[256,2048]{1,0:T(8,128)(2,1)S(1)}, bf16[256,2048]{1,0:T(8,128)(2,1)S(1)}, u32[]{:S(2)}, u32[]{:S(2)}) collective-permute-start(bf16[256,2048]{1,0:T(8,128)(2,1)S(1)} %get-tuple-element.33.refs_2_), channel_id=1, source_target_pairs={{0,8},{4,12},{8,0},{12,4},{1,9},{5,13},{9,1},{13,5},{2,10},{6,14},... | collective-permute-start | bytes 3145736 | tf_op jit(solution)/shard_map/ppermute | solution.py:385
  33.6 15.9 %project.6 = (f32[1,512,2048]{2,1,0:T(8,128)S(1)}, f32[8,128]{1,0:T(8,128)S(1)}, bf16[8192,512]{1,0:T(8,128)(2,1)S(1)}, bf16[512,7168]{1,0:T(8,128)(2,1)S(1)}) custom-call(bf16[2,7168,2048]{2,1,0:T(8,128)(2,1)} %refs_4_.5, bf16[8192,512]{1,0:T(8,128)(2,1)S(1)} %get-tuple-element.38.refs_1_, ...), custom_call_target="tpu_custom_call", output_to_operand_aliasing={{2}: (1, {}), {3}: (2, {})} | custom-call | flops 1024 | bytes 1024 | tf_op jit(solution)/shard_map/project/pallas_call | solution.py:211
  49.5 1.5 %collective-permute-done.7.source_ref = bf16[256,1792]{1,0:T(8,128)(2,1)S(1)} collective-permute-done((bf16[256,1792]{1,0:T(8,128)(2,1)S(1)}, bf16[256,1792]{1,0:T(8,128)(2,1)S(1)}, u32[]{:S(2)}, u32[]{:S(2)}) %collective-permute-start.7) | collective-permute-done | bytes 917536 | tf_op jit(solution)/shard_map/ppermute | solution.py:385
  51.0 0.1 halve.5
  51.2 0.5 collective-permute-start.9
  51.7 1.3 %collective-permute-done.8.refs_5_ = bf16[256,896]{1,0:T(8,128)(2,1)S(1)} collective-permute-done((bf16[256,896]{1,0:T(8,128)(2,1)S(1)}, bf16[256,896]{1,0:T(8,128)(2,1)S(1)}, u32[]{:S(2)}, u32[]{:S(2)}) %collective-permute-start.8) | collective-permute-done | bytes 458784 | tf_op jit(solution)/shard_map/ppermute | solution.py:382
  53.0 0.7 collective-permute-done.9.refs_7_
  53.7 17.3 %project.7 = (f32[2,512,2048]{2,1,0:T(8,128)S(1)}, f32[8,128]{1,0:T(8,128)S(1)}, bf16[8192,512]{1,0:T(8,128)(2,1)S(1)}) custom-call(bf16[256,1024]{1,0:T(8,128)(2,1)S(1)} %get-tuple-element.41.refs_3_.refs_1_.refs_0_, bf16[256,1024]{1,0:T(8,128)(2,1)S(1)} %collective-permute-done.5.refs_2_.refs_1_, ...), custom_call_target="tpu_custom_call", output_to_operand_aliasing={{2}: (9, {})} | custom-call | flops 1024 | bytes 1024 | tf_op jit(solution)/shard_map/project/pallas_call | solution.py:211
  71.0 1.9 %collective-permute-start.15 = (bf16[2,128,2048]{2,1,0:T(8,128)(2,1)S(1)}, bf16[2,128,2048]{2,1,0:T(8,128)(2,1)S(1)}, u32[]{:S(2)}, u32[]{:S(2)}) collective-permute-start(bf16[2,128,2048]{2,1,0:T(8,128)(2,1)S(1)} %after.3.refs_8_.refs_5_), channel_id=1, source_target_pairs={{1,0},{0,2},{2,3},{3,1},{5,4},{4,6},{6,7},{7,5},{9,8},{8,10},{10,1... | collective-permute-start | bytes 3145736 | tf_op jit(solution)/shard_map/ppermute | solution.py:408
  72.8 1.5 %collective-permute-start.3 = (bf16[256,1280]{1,0:T(8,128)(2,1)S(1)}, bf16[256,1280]{1,0:T(8,128)(2,1)S(1)}, u32[]{:S(2)}, u32[]{:S(2)}) collective-permute-start(bf16[256,1280]{1,0:T(8,128)(2,1)S(1)} %get-tuple-element.34.refs_3_), channel_id=1, source_target_pairs={{0,8},{4,12},{8,0},{12,4},{1,9},{5,13},{9,1},{13,5},{2,10},{6,14},... | collective-permute-start | bytes 1966088 | tf_op jit(solution)/shard_map/ppermute | solution.py:385
  74.4 0.1 halve.6
  74.5 0.1 collective-permute-start.10
  74.6 0.5 collective-permute-start.11
  75.1 1.4 %collective-permute-done.10.refs_1_ = bf16[256,1024]{1,0:T(8,128)(2,1)S(1)} collective-permute-done((bf16[256,1024]{1,0:T(8,128)(2,1)S(1)}, bf16[256,1024]{1,0:T(8,128)(2,1)S(1)}, u32[]{:S(2)}, u32[]{:S(2)}) %collective-permute-start.10) | collective-permute-done | bytes 524320 | tf_op jit(solution)/shard_map/ppermute | solution.py:382
  76.5 0.7 collective-permute-done.11.refs_3_
  77.2 9.4 %project.8 = (f32[2,512,2048]{2,1,0:T(8,128)S(1)}, f32[8,128]{1,0:T(8,128)S(1)}, bf16[8192,512]{1,0:T(8,128)(2,1)S(1)}) custom-call(bf16[256,1024]{1,0:T(8,128)(2,1)S(1)} %get-tuple-element.49.refs_0_.refs_7_, bf16[256,1024]{1,0:T(8,128)(2,1)S(1)} %collective-permute-done.10.refs_1_, ...), custom_call_target="tpu_custom_call", output_to_operand_aliasing={{2}: (5, {}), {0}: (6, {})} | custom-call | flops 1024 | bytes 1024 | tf_op jit(solution)/shard_map/project/pallas_call | solution.py:211
  86.6 2.7 %collective-permute-done.3.source_ref = bf16[256,1280]{1,0:T(8,128)(2,1)S(1)} collective-permute-done((bf16[256,1280]{1,0:T(8,128)(2,1)S(1)}, bf16[256,1280]{1,0:T(8,128)(2,1)S(1)}, u32[]{:S(2)}, u32[]{:S(2)}) %collective-permute-start.3) | collective-permute-done | bytes 655392 | tf_op jit(solution)/shard_map/ppermute | solution.py:385
  89.3 0.1 halve.7
  89.4 0.1 collective-permute-start.13
  89.5 0.5 collective-permute-start.14
  90.0 1.1 collective-permute-done.13.refs_1_
  91.1 0.5 collective-permute-done.14.refs_3_
  91.6 6.0 %project.9 = (f32[2,512,2048]{2,1,0:T(8,128)S(1)}, f32[8,128]{1,0:T(8,128)}, bf16[8192,512]{1,0:T(8,128)(2,1)S(1)}) custom-call(bf16[256,640]{1,0:T(8,128)(2,1)S(1)} %get-tuple-element.54.refs_0_.refs_7_, bf16[256,640]{1,0:T(8,128)(2,1)S(1)} %collective-permute-done.13.refs_1_, ...), custom_call_target="tpu_custom_call", output_to_operand_aliasing={{2}: (5, {}), {0}: (6, {})} | custom-call | flops 1024 | bytes 1024 | tf_op jit(solution)/shard_map/project/pallas_call | solution.py:211
  97.7 3.8 %score.1 = f32[4,2,256]{2,1,0:T(2,128)S(1)} custom-call(f32[1,512,2048]{2,1,0:T(8,128)S(1)} %get-tuple-element.37.refs_0_, f32[1,512,2048]{2,1,0:T(8,128)S(1)} %get-tuple-element.42.refs_1_, f32[2,512,2048]{2,1,0:T(8,128)S(1)} %get-tuple-element.58.refs_2_, bf16[2,128,2048]{2,1,0:T(8,128)(2,1)} %refs_3_.1, bf16[2,128,2048]{2,1,0:T(8,128)(2,1)S(1)} %after.2.refs_4_, ...), custom_call_target="tpu_custom_call" | custom-call | tf_op jit(solution)/shard_map/score/pallas_call | solution.py:273
  101.5 0.7 collective-permute-start.17
  102.2 0.3 collective-permute-start.18
  102.5 1.2 %collective-permute-start.16 = (f32[2,2,512]{2,1,0:T(2,128)S(1)}, f32[2,2,512]{2,1,0:T(2,128)S(1)}, u32[]{:S(2)}, u32[]{:S(2)}) collective-permute-start(f32[2,2,512]{2,1,0:T(2,128)S(1)} %copy_bitcast_fusion), channel_id=1, source_target_pairs={{0,4},{4,0},{8,12},{12,8},{1,5},{5,1},{9,13},{13,9},{2,6},{6,2},{1... | collective-permute-start | bytes 24584 | tf_op jit(solution)/shard_map/ppermute | solution.py:293
  103.7 0.4 convert_reduce_fusion
  104.1 1.1 collective-permute-done.17
  105.3 2.2 %collective-permute-start.20 = (f32[2,2,512]{2,1,0:T(2,128)S(1)}, f32[2,2,512]{2,1,0:T(2,128)S(1)}, u32[]{:S(2)}, u32[]{:S(2)}) collective-permute-start(f32[2,2,512]{2,1,0:T(2,128)S(1)} %add_add_fusion), channel_id=1, source_target_pairs={{0,2},{1,3},{2,0},{3,1},{4,6},{5,7},{6,4},{7,5},{8,10},{9,11},{10,... | collective-permute-start | bytes 24584 | tf_op jit(solution)/shard_map/ppermute | solution.py:293
  107.5 0.8 collective-permute-start.21
  108.3 0.6 collective-permute-start.19
  108.9 1.1 collective-permute-done.20
  110.0 3.0 %collective-permute-done.21 = f32[2,2,512]{2,1,0:T(2,128)S(1)} collective-permute-done((f32[2,2,512]{2,1,0:T(2,128)S(1)}, f32[2,2,512]{2,1,0:T(2,128)S(1)}, u32[]{:S(2)}, u32[]{:S(2)}) %collective-permute-start.21) | collective-permute-done | bytes 8224 | tf_op jit(solution)/shard_map/ppermute | solution.py:293
  113.0 0.6 add_multiply_fusion
  (21 shorter events, 0.2 us)
Async XLA Ops:
  0.0 12.3 %collective-permute-start = (bf16[256,7168]{1,0:T(8,128)(2,1)}, bf16[256,7168]{1,0:T(8,128)(2,1)S(1)}, u32[]{:S(2)}, u32[]{:S(2)}) collective-permute-start(bf16[256,7168]{1,0:T(8,128)(2,1)} %bitcast.11), channel_id=1, source_target_pairs={{0,4},{4,0},{8,12},{12,8},{1,5},{5,1},{9,13},{13,9},{2,6},{6,2},{1... | collective-permute-start | bytes 11010056 | tf_op jit(solution)/shard_map/ppermute | solution.py:382
  0.5 28.0 %collective-permute-start.2 = (bf16[2,128,2048]{2,1,0:T(8,128)(2,1)}, bf16[2,128,2048]{2,1,0:T(8,128)(2,1)S(1)}, u32[]{:S(2)}, u32[]{:S(2)}) collective-permute-start(bf16[2,128,2048]{2,1,0:T(8,128)(2,1)} %refs_3_.1), channel_id=1, source_target_pairs={{1,0},{0,2},{2,3},{3,1},{5,4},{4,6},{6,7},{7,5},{9,8},{8,10},{10,1... | collective-permute-start | bytes 3145736 | tf_op jit(solution)/shard_map/ppermute | solution.py:400
  5.3 26.1 %collective-permute-start.1 = (bf16[256,2048]{1,0:T(8,128)(2,1)S(1)}, bf16[256,2048]{1,0:T(8,128)(2,1)S(1)}, u32[]{:S(2)}, u32[]{:S(2)}) collective-permute-start(bf16[256,2048]{1,0:T(8,128)(2,1)S(1)} %cut.2.refs_0_), channel_id=1, source_target_pairs={{0,8},{4,12},{8,0},{12,4},{1,9},{5,13},{9,1},{13,5},{2,10},{6,14},... | collective-permute-start | bytes 3145736 | tf_op jit(solution)/shard_map/ppermute | solution.py:385
  8.6 42.4 %collective-permute-start.7 = (bf16[256,1792]{1,0:T(8,128)(2,1)S(1)}, bf16[256,1792]{1,0:T(8,128)(2,1)S(1)}, u32[]{:S(2)}, u32[]{:S(2)}) collective-permute-start(bf16[256,1792]{1,0:T(8,128)(2,1)S(1)} %get-tuple-element.32.refs_1_), channel_id=1, source_target_pairs={{0,8},{4,12},{8,0},{12,4},{1,9},{5,13},{9,1},{13,5},{2,10},{6,14},... | collective-permute-start | bytes 2752520 | tf_op jit(solution)/shard_map/ppermute | solution.py:385
  28.5 42.5 %collective-permute-start.12 = (bf16[2,128,2048]{2,1,0:T(8,128)(2,1)S(1)}, bf16[2,128,2048]{2,1,0:T(8,128)(2,1)S(1)}, u32[]{:S(2)}, u32[]{:S(2)}) collective-permute-start(bf16[2,128,2048]{2,1,0:T(8,128)(2,1)S(1)} %after.2.refs_4_), channel_id=1, source_target_pairs={{1,0},{0,2},{2,3},{3,1},{5,4},{4,6},{6,7},{7,5},{9,8},{8,10},{10,1... | collective-permute-start | bytes 3145736 | tf_op jit(solution)/shard_map/ppermute | solution.py:408
  31.5 19.5 %collective-permute-start.5 = (bf16[256,1024]{1,0:T(8,128)(2,1)S(1)}, bf16[256,1024]{1,0:T(8,128)(2,1)S(1)}, u32[]{:S(2)}, u32[]{:S(2)}) collective-permute-start(bf16[256,1024]{1,0:T(8,128)(2,1)S(1)} %get-tuple-element.41.refs_3_.refs_1_.refs_0_), channel_id=1, source_target_pairs={{0,4},{4,0},{8,12},{12,8},{1,5},{5,1},{9,13},{13,9},{2,6},{6,2},{1... | collective-permute-start | bytes 1572872 | tf_op jit(solution)/shard_map/ppermute | solution.py:382
  31.5 19.5 %collective-permute-start.6 = (bf16[256,1024]{1,0:T(8,128)(2,1)S(1)}, bf16[256,1024]{1,0:T(8,128)(2,1)S(1)}, u32[]{:S(2)}, u32[]{:S(2)}) collective-permute-start(bf16[256,1024]{1,0:T(8,128)(2,1)S(1)} %get-tuple-element.43.refs_3_.refs_2_), channel_id=1, source_target_pairs={{0,4},{4,0},{8,12},{12,8},{1,5},{5,1},{9,13},{13,9},{2,6},{6,2},{1... | collective-permute-start | bytes 1572872 | tf_op jit(solution)/shard_map/ppermute | solution.py:382
  32.0 42.3 %collective-permute-start.4 = (bf16[256,2048]{1,0:T(8,128)(2,1)S(1)}, bf16[256,2048]{1,0:T(8,128)(2,1)S(1)}, u32[]{:S(2)}, u32[]{:S(2)}) collective-permute-start(bf16[256,2048]{1,0:T(8,128)(2,1)S(1)} %get-tuple-element.33.refs_2_), channel_id=1, source_target_pairs={{0,8},{4,12},{8,0},{12,4},{1,9},{5,13},{9,1},{13,5},{2,10},{6,14},... | collective-permute-start | bytes 3145736 | tf_op jit(solution)/shard_map/ppermute | solution.py:385
  51.1 1.9 %collective-permute-start.8 = (bf16[256,896]{1,0:T(8,128)(2,1)S(1)}, bf16[256,896]{1,0:T(8,128)(2,1)S(1)}, u32[]{:S(2)}, u32[]{:S(2)}) collective-permute-start(bf16[256,896]{1,0:T(8,128)(2,1)S(1)} %get-tuple-element.45.refs_4_.refs_10_), channel_id=1, source_target_pairs={{0,4},{4,0},{8,12},{12,8},{1,5},{5,1},{9,13},{13,9},{2,6},{6,2},{1... | collective-permute-start | bytes 1376264 | tf_op jit(solution)/shard_map/ppermute | solution.py:382
  51.2 2.5 %collective-permute-start.9 = (bf16[256,896]{1,0:T(8,128)(2,1)S(1)}, bf16[256,896]{1,0:T(8,128)(2,1)S(1)}, u32[]{:S(2)}, u32[]{:S(2)}) collective-permute-start(bf16[256,896]{1,0:T(8,128)(2,1)S(1)} %get-tuple-element.46.refs_6_), channel_id=1, source_target_pairs={{0,4},{4,0},{8,12},{12,8},{1,5},{5,1},{9,13},{13,9},{2,6},{6,2},{1... | collective-permute-start | bytes 1376264 | tf_op jit(solution)/shard_map/ppermute | solution.py:382
  71.0 26.7 %collective-permute-start.15 = (bf16[2,128,2048]{2,1,0:T(8,128)(2,1)S(1)}, bf16[2,128,2048]{2,1,0:T(8,128)(2,1)S(1)}, u32[]{:S(2)}, u32[]{:S(2)}) collective-permute-start(bf16[2,128,2048]{2,1,0:T(8,128)(2,1)S(1)} %after.3.refs_8_.refs_5_), channel_id=1, source_target_pairs={{1,0},{0,2},{2,3},{3,1},{5,4},{4,6},{6,7},{7,5},{9,8},{8,10},{10,1... | collective-permute-start | bytes 3145736 | tf_op jit(solution)/shard_map/ppermute | solution.py:408
  72.8 16.5 %collective-permute-start.3 = (bf16[256,1280]{1,0:T(8,128)(2,1)S(1)}, bf16[256,1280]{1,0:T(8,128)(2,1)S(1)}, u32[]{:S(2)}, u32[]{:S(2)}) collective-permute-start(bf16[256,1280]{1,0:T(8,128)(2,1)S(1)} %get-tuple-element.34.refs_3_), channel_id=1, source_target_pairs={{0,8},{4,12},{8,0},{12,4},{1,9},{5,13},{9,1},{13,5},{2,10},{6,14},... | collective-permute-start | bytes 1966088 | tf_op jit(solution)/shard_map/ppermute | solution.py:385
  74.5 2.0 %collective-permute-start.10 = (bf16[256,1024]{1,0:T(8,128)(2,1)S(1)}, bf16[256,1024]{1,0:T(8,128)(2,1)S(1)}, u32[]{:S(2)}, u32[]{:S(2)}) collective-permute-start(bf16[256,1024]{1,0:T(8,128)(2,1)S(1)} %get-tuple-element.49.refs_0_.refs_7_), channel_id=1, source_target_pairs={{0,4},{4,0},{8,12},{12,8},{1,5},{5,1},{9,13},{13,9},{2,6},{6,2},{1... | collective-permute-start | bytes 1572872 | tf_op jit(solution)/shard_map/ppermute | solution.py:382
  74.6 2.6 %collective-permute-start.11 = (bf16[256,1024]{1,0:T(8,128)(2,1)S(1)}, bf16[256,1024]{1,0:T(8,128)(2,1)S(1)}, u32[]{:S(2)}, u32[]{:S(2)}) collective-permute-start(bf16[256,1024]{1,0:T(8,128)(2,1)S(1)} %get-tuple-element.50.refs_2_), channel_id=1, source_target_pairs={{0,4},{4,0},{8,12},{12,8},{1,5},{5,1},{9,13},{13,9},{2,6},{6,2},{1... | collective-permute-start | bytes 1572872 | tf_op jit(solution)/shard_map/ppermute | solution.py:382
  89.4 1.7 %collective-permute-start.13 = (bf16[256,640]{1,0:T(8,128)(2,1)S(1)}, bf16[256,640]{1,0:T(8,128)(2,1)S(1)}, u32[]{:S(2)}, u32[]{:S(2)}) collective-permute-start(bf16[256,640]{1,0:T(8,128)(2,1)S(1)} %get-tuple-element.54.refs_0_.refs_7_), channel_id=1, source_target_pairs={{0,4},{4,0},{8,12},{12,8},{1,5},{5,1},{9,13},{13,9},{2,6},{6,2},{1... | collective-permute-start | bytes 983048 | tf_op jit(solution)/shard_map/ppermute | solution.py:382
  89.5 2.1 %collective-permute-start.14 = (bf16[256,640]{1,0:T(8,128)(2,1)S(1)}, bf16[256,640]{1,0:T(8,128)(2,1)S(1)}, u32[]{:S(2)}, u32[]{:S(2)}) collective-permute-start(bf16[256,640]{1,0:T(8,128)(2,1)S(1)} %get-tuple-element.55.refs_2_), channel_id=1, source_target_pairs={{0,4},{4,0},{8,12},{12,8},{1,5},{5,1},{9,13},{13,9},{2,6},{6,2},{1... | collective-permute-start | bytes 983048 | tf_op jit(solution)/shard_map/ppermute | solution.py:382
  97.7 6.0 %copy-start = (s32[2,512]{1,0:T(2,128)S(1)}, s32[2,512]{1,0:T(2,128)}, u32[]{:S(2)}) copy-start(s32[2,512]{1,0:T(2,128)} %param.8) | copy-start | bytes 12292
  97.7 11.2 %copy-start.1 = (s32[2,512]{1,0:T(2,128)S(1)}, s32[2,512]{1,0:T(2,128)}, u32[]{:S(2)}) copy-start(s32[2,512]{1,0:T(2,128)} %param.9) | copy-start | bytes 12292
  101.5 3.7 %collective-permute-start.17 = (f32[2,2,512]{2,1,0:T(2,128)S(1)}, f32[2,2,512]{2,1,0:T(2,128)S(1)}, u32[]{:S(2)}, u32[]{:S(2)}) collective-permute-start(f32[2,2,512]{2,1,0:T(2,128)S(1)} %copy_bitcast_fusion), channel_id=1, source_target_pairs={{0,8},{4,12},{8,0},{12,4},{1,9},{5,13},{9,1},{13,5},{2,10},{6,14},... | collective-permute-start | bytes 24584 | tf_op jit(solution)/shard_map/ppermute | solution.py:293
  102.2 3.1 %collective-permute-start.18 = (f32[2,2,512]{2,1,0:T(2,128)S(1)}, f32[2,2,512]{2,1,0:T(2,128)S(1)}, u32[]{:S(2)}, u32[]{:S(2)}) collective-permute-start(f32[2,2,512]{2,1,0:T(2,128)S(1)} %copy_bitcast_fusion), channel_id=1, source_target_pairs={{0,12},{4,8},{8,4},{12,0},{1,13},{5,9},{9,5},{13,1},{2,14},{6,10},... | collective-permute-start | bytes 24584 | tf_op jit(solution)/shard_map/ppermute | solution.py:293
  102.5 2.8 %collective-permute-start.16 = (f32[2,2,512]{2,1,0:T(2,128)S(1)}, f32[2,2,512]{2,1,0:T(2,128)S(1)}, u32[]{:S(2)}, u32[]{:S(2)}) collective-permute-start(f32[2,2,512]{2,1,0:T(2,128)S(1)} %copy_bitcast_fusion), channel_id=1, source_target_pairs={{0,4},{4,0},{8,12},{12,8},{1,5},{5,1},{9,13},{13,9},{2,6},{6,2},{1... | collective-permute-start | bytes 24584 | tf_op jit(solution)/shard_map/ppermute | solution.py:293
  105.3 4.7 %collective-permute-start.20 = (f32[2,2,512]{2,1,0:T(2,128)S(1)}, f32[2,2,512]{2,1,0:T(2,128)S(1)}, u32[]{:S(2)}, u32[]{:S(2)}) collective-permute-start(f32[2,2,512]{2,1,0:T(2,128)S(1)} %add_add_fusion), channel_id=1, source_target_pairs={{0,2},{1,3},{2,0},{3,1},{4,6},{5,7},{6,4},{7,5},{8,10},{9,11},{10,... | collective-permute-start | bytes 24584 | tf_op jit(solution)/shard_map/ppermute | solution.py:293
  107.5 5.4 %collective-permute-start.21 = (f32[2,2,512]{2,1,0:T(2,128)S(1)}, f32[2,2,512]{2,1,0:T(2,128)S(1)}, u32[]{:S(2)}, u32[]{:S(2)}) collective-permute-start(f32[2,2,512]{2,1,0:T(2,128)S(1)} %add_add_fusion), channel_id=1, source_target_pairs={{0,3},{1,2},{2,1},{3,0},{4,7},{5,6},{6,5},{7,4},{8,11},{9,10},{10,... | collective-permute-start | bytes 24584 | tf_op jit(solution)/shard_map/ppermute | solution.py:293
  108.3 4.7 %collective-permute-start.19 = (f32[2,2,512]{2,1,0:T(2,128)S(1)}, f32[2,2,512]{2,1,0:T(2,128)S(1)}, u32[]{:S(2)}, u32[]{:S(2)}) collective-permute-start(f32[2,2,512]{2,1,0:T(2,128)S(1)} %add_add_fusion), channel_id=1, source_target_pairs={{0,1},{1,0},{2,3},{3,2},{4,5},{5,4},{6,7},{7,6},{8,9},{9,8},{10,11... | collective-permute-start | bytes 24584 | tf_op jit(solution)/shard_map/ppermute | solution.py:293

commit v6 on v5

--- a/solution.py
+++ b/solution.py
@@ -8,7 +8,7 @@
 from jax.experimental.pallas import tpu as pltpu
 from jax.sharding import PartitionSpec as P
 
-WEIGHTS = (8, 7, 8, 5)
+WEIGHTS = (9, 6, 7, 6)
 GROUPS = (2, 1, 1)
 HELPER_VMEM = 1024 * 1024
 TILE = 512
@@ -23,29 +23,26 @@
 
 
 class Plan(typing.NamedTuple):
-    query: int
-    queries: int
+    first: int
+    steps: int
     begin: int
     depth: int
     tile: int
     strips: int
     turns: int
 
-    @property
-    def steps(self):
-        return self.queries * self.turns
-
-
-def plan_of(query, queries, begin, depth, width, room):
+
+def plan_of(queries, begin, depth, width, room):
     tile = tile_of(width, TILE)
     strips = 1
     while strips * 2 * depth <= room and width // tile % (strips * 2) == 0:
         strips *= 2
-    return Plan(query, queries, begin, depth, tile, strips, width // tile // strips)
+    turns = width // tile // strips
+    return Plan(0, queries * turns, begin, depth, tile, strips, turns)
 
 
 def fetches(plan, step, q_ref, slot_ref, sems):
-    number, turn = plan.query + step // plan.turns, step % plan.turns
+    number, turn = (plan.first + step) // plan.turns, (plan.first + step) % plan.turns
     copies = []
     for strip in range(plan.strips):
         column = (turn * plan.strips + strip) * plan.tile
@@ -96,7 +93,7 @@
     )(*own, query_grads)
 
 
-def project_kernel(parts, plan, later, fresh, laid, *refs):
+def project_kernel(parts, plan, later, add, laid, *refs):
     g_refs, q_ref = refs[:parts], refs[parts]
     sum_ref, mark_ref, slot_a, x_ref, slot_b, sems, sems_a, sems_b = refs[-8:]
     total = x_ref.shape[0]
@@ -118,7 +115,7 @@
     run(copies, False)
 
     def multiply(step, slot_ref):
-        number, turn = step // plan.turns, step % plan.turns
+        number, turn = (plan.first + step) // plan.turns, (plan.first + step) % plan.turns
         for strip in range(plan.strips):
             product = jnp.dot(
                 x_ref[...],
@@ -129,10 +126,10 @@
             if not isinstance(begin, int):
                 begin = pl.multiple_of(begin, plan.tile)
             where = (number, slice(None), pl.ds(begin, plan.tile))
-            if fresh:
+            if add:
+                sum_ref[where] += product
+            else:
                 sum_ref[where] = product
-            else:
-                sum_ref[where] += product
 
     def both(pair):
         step = pair * 2
@@ -177,7 +174,7 @@
 
 
 def project(parts, rows, query_grads, plan, later, slot, running, others=(), laid=None):
-    width = query_grads.shape[2]
+    queries, _, width = query_grads.shape
     fresh = running is None
     any_spec = pl.BlockSpec(memory_space=pl.ANY)
     vmem_spec = pl.BlockSpec(memory_space=pltpu.VMEM)
@@ -189,7 +186,7 @@
         operands.append(running)
         in_specs.append(vmem_spec)
     out_shape = [
-        jax.ShapeDtypeStruct((plan.queries, rows, width), jnp.float32),
+        jax.ShapeDtypeStruct((queries, rows, width), jnp.float32),
         jax.ShapeDtypeStruct((8, 128), jnp.float32),
         jax.ShapeDtypeStruct(slot.shape, slot.dtype),
     ]
@@ -209,7 +206,9 @@
     ]
     limit = 2 * slot.size + (2 * rows * plan.depth if laid is None else 0) + 4 * 1024 * 1024
     return pl.pallas_call(
-        functools.partial(project_kernel, len(parts), plan, later, fresh, laid is not None),
+        functools.partial(
+            project_kernel, len(parts), plan, later, not fresh and laid is None, laid is not None
+        ),
         in_specs=in_specs + [any_spec] * len(others),
         out_specs=[vmem_spec] * len(out_shape),
         out_shape=out_shape,
@@ -222,7 +221,7 @@
 
 
 def score_kernel(inp_size, pair, queries, ring, *refs):
-    near_refs, refs = refs[:queries], refs[queries:]
+    near_ref, refs = refs[0], refs[1:]
     if inp_size > pair:
         far_ref, refs = refs[0], refs[1:]
     *a_refs, out_ref, held, sems = refs
@@ -261,7 +260,7 @@
             block = held[number, :, :, at:at + lanes].reshape(blocks * shard, lanes).astype(jnp.float32)
             for query in range(queries):
                 where = (slice(begin, begin + blocks * shard), slice(at, at + lanes))
-                rows = near_refs[query][(0, *where)] if number < pair else far_ref[(query, *where)]
+                rows = (near_ref if number < pair else far_ref)[(query, *where)]
                 term = rows * block
                 totals[query] = term if totals[query] is None else totals[query] + term
         for query in range(queries):
@@ -341,25 +340,27 @@
     return pltpu.with_memory_space_constraint(value, pltpu.HBM)
 
 
-def cut_kernel(spans, source_ref, *refs):
-    outs, sems = refs[:-1], refs[-1]
+def cut_kernel(spans, total, source_ref, a_ref, *refs):
+    outs, sems = refs[-1 - total:-1], refs[-1]
     copies = []
-    for at, (span, out_ref) in enumerate(zip(spans, outs)):
-        copies.append(pltpu.make_async_copy(source_ref.at[:, pl.ds(*span)], out_ref, sems.at[at]))
+    for at, out_ref in enumerate(outs):
+        piece = source_ref.at[:, pl.ds(*spans[at])] if at < len(spans) else a_ref
+        copies.append(pltpu.make_async_copy(piece, out_ref, sems.at[at]))
     run(copies, True)
     run(copies, False)
 
 
-def cut(source, spans):
-    return pl.pallas_call(
-        functools.partial(cut_kernel, spans),
-        in_specs=[pl.BlockSpec(memory_space=pl.ANY)],
-        out_specs=[pl.BlockSpec(memory_space=pltpu.VMEM)] * len(spans),
-        out_shape=[jax.ShapeDtypeStruct((source.shape[0], length), source.dtype) for _, length in spans],
-        scratch_shapes=[pltpu.SemaphoreType.DMA((len(spans),))],
+def cut(source, spans, activations, copied, *others):
+    shapes = [(source.shape[0], length) for _, length in spans] + [activations.shape] * copied
+    return pl.pallas_call(
+        functools.partial(cut_kernel, spans, len(shapes)),
+        in_specs=[pl.BlockSpec(memory_space=pl.ANY)] * (2 + len(others)),
+        out_specs=[pl.BlockSpec(memory_space=pltpu.VMEM)] * len(shapes),
+        out_shape=[jax.ShapeDtypeStruct(shape, source.dtype) for shape in shapes],
+        scratch_shapes=[pltpu.SemaphoreType.DMA((len(shapes),))],
         compiler_params=pltpu.CompilerParams(vmem_limit_bytes=HELPER_VMEM),
         name="cut",
-    )(source)
+    )(source, activations, *others)
 
 
 def shards(inp_size, out_size, activations, out_grads, query_grads, token_ids, loss_mask):
@@ -391,13 +392,13 @@
     line = inp_size == out_size and activations.shape[1] == shard and out_size > 1
     ring = list(range(0, out_size, 2)) + list(range(1, out_size, 2))[::-1]
     turn = [(ring[at - 1], ring[at]) for at in range(out_size)]
-    pieces_out = []
-    if chips > 1:
-        pieces_out = cut(own, spans[:1]) + (cut(own, spans[1:]) if chunks > 1 else [])
-
-    slots = [activations]
+    pieces_out = list(cut(own, spans[:1], activations, False)) if chips > 1 else []
+    *rest, moving = cut(own, spans[1:] if chips > 1 else [], activations, True, *pieces_out)
+    pieces_out += rest
+
+    slots = [moving]
     if line:
-        slots.append(lax.ppermute(activations, "out", turn))
+        slots.append(lax.ppermute(moving, "out", turn))
     else:
         slots = [lax.all_gather(activations, "out", axis=1, tiled=True)]
 
@@ -424,33 +425,38 @@
         return ended
 
     room = max(depth, STRIP_ROWS if depth >= STRIP_ROWS // 2 else 0)
-    plans = [plan_of(query, 1, 0, depth, width, depth) for query in range(queries)]
+    near_plan = plan_of(queries, 0, depth, width, depth)
+    early = near_plan.steps * 3 // 8 * 2 or near_plan.steps
+    plans = [near_plan._replace(steps=early)]
+    if early < near_plan.steps:
+        plans.append(near_plan._replace(first=early, steps=near_plan.steps - early))
+    near_calls = len(plans)
     chosen = []
     for count in GROUPS + (1,) * chunks:
         group, spans = (spans[:count], spans[count:]) if chips > 1 else ([], [])
         if group:
             chosen.append(count)
             length = sum(length for _, length in group)
-            plans.append(plan_of(0, queries, group[0][0], length, width, room))
+            plans.append(plan_of(queries, group[0][0], length, width, room))
     plans.append(None)
 
     slot, laid = load(pieces_out or [own], pair * rows, query_grads, plans[0], room)
-    sums = []
-    mark = None
-    for query in range(queries):
+    near_sum = None
+    got = 0
+    for at in range(near_calls):
         others = []
-        if query > 0:
+        if at > 0:
+            got = min(1, len(coming))
             others = receive(mark) + step_along(mark)
         near_sum, mark, slot, laid = project(
-            near if query == 0 else [], pair * rows, query_grads, plans[query], plans[query + 1], slot, None, others, laid
+            [] if at else near, pair * rows, query_grads, plans[at], plans[at + 1], slot, near_sum, others, laid
         )
-        sums.append(near_sum)
+    sums = [near_sum]
     running = None
-    got = min(queries - 1, len(coming))
     for at, count in enumerate(chosen):
         others = receive(mark, count - (got if at == 0 else 0)) + (step_along(mark) if at > 0 else [])
         running, mark, slot = project(
-            waiting, (inp_size - pair) * rows, query_grads, plans[queries + at], plans[queries + at + 1], slot, running, others
+            waiting, (inp_size - pair) * rows, query_grads, plans[near_calls + at], plans[near_calls + at + 1], slot, running, others
         )
         waiting.clear()
     if running is not None:

time: 114 us -> 112 us (0.982)
  Pallas kernels: 75.1 us -> 78.4 us
  waiting for transfers between devices: 15.8 us -> 13.3 us
  starting transfers between devices: 21.3 us -> 19.3 us
    ppermute x4, waiting for transfers between devices: 4.83 us -> 0.27 us  [shift(): lax.ppermute(value, 'inp', [(at, (at + pair * by) % inp_size) for at in r...]
    ppermute x2, waiting for transfers between devices: 0.01 us -> 4.17 us  [step_along(): slots.append(lax.ppermute(ended, 'out', turn))]
    pallas_call x5, Pallas kernels: 64.9 us -> 68.7 us  [project(): pl.pallas_call(functools.partial(project_kernel, len(parts), plan, later,...]
    ppermute x2, starting transfers between devices: 4.06 us -> 2.41 us  [step_along(): slots.append(lax.ppermute(ended, 'out', turn))]
    ppermute x6, waiting for transfers between devices: 5.28 us -> 3.8 us  [xor_sum(): lax.ppermute(value, axis, [(at, at ^ other) for at in range(size)])]
  transfers between devices with their start and end apart: 22 -> 22, of which waited for: 13 -> 11; matrix products, arithmetic and copies ran while one was open for 0% -> 0% of each run, Pallas kernels for 63% -> 67%
where the time goes in v6:
time: 112 us
  Pallas kernels  78.4 us (70%)
  starting transfers between devices  19.3 us (17%)
  waiting for transfers between devices  13.3 us (12%)
    pallas_call x5, Pallas kernels, project(): pl.pallas_call(functools.partial(project_kernel, len(parts), plan, later,...  68.7 us
    ppermute x6, starting transfers between devices, xor_sum(): lax.ppermute(value, axis, [(at, at ^ other) for at in range(size)])  6.38 us
    ppermute x4, starting transfers between devices, shift(): lax.ppermute(value, 'inp', [(at, (at + pair * by) % inp_size) for at in r...  5.11 us
    ppermute x9, waiting for transfers between devices, flip(): return lax.ppermute(value, 'inp', [(at, at ^ 1) for at in range(inp_size)])  5.02 us
    ppermute x2, waiting for transfers between devices, step_along(): slots.append(lax.ppermute(ended, 'out', turn))  4.17 us
    ppermute x6, waiting for transfers between devices, xor_sum(): lax.ppermute(value, axis, [(at, at ^ other) for at in range(size)])  3.8 us
    pallas_call x2, Pallas kernels, cut(): pl.pallas_call(functools.partial(cut_kernel, spans, len(shapes)), in_spec...  3.29 us
    pallas_call x1, Pallas kernels, load(): pl.pallas_call(functools.partial(load_kernel, plan, len(own)), in_specs=[...  3.13 us
  transfers between devices with their start and end apart: 22, of which 11 were waited for; matrix products, arithmetic and copies ran while one was open for 0% of the time, Pallas kernels for 67%

profile of v6, /device:TPU:0, one launch (start us, length us, event | category | flops | bytes accessed | tf_op | source)
XLA Modules:
  0.0 112.3 jit_solution(6468009045550052785)
XLA Ops:
  0.0 0.5 collective-permute-start
  0.5 1.3 %cut.2.refs_0_ = bf16[256,2304]{1,0:T(8,128)(2,1)S(1)} custom-call(bf16[256,7168]{1,0:T(8,128)(2,1)} %bitcast.12, bf16[2,128,2048]{2,1,0:T(8,128)(2,1)} %a_ref.3), custom_call_target="tpu_custom_call" | custom-call | tf_op jit(solution)/shard_map/cut/pallas_call | solution.py:355
  1.7 2.6 %collective-permute-start.1 = (bf16[256,2304]{1,0:T(8,128)(2,1)S(1)}, bf16[256,2304]{1,0:T(8,128)(2,1)S(1)}, u32[]{:S(2)}, u32[]{:S(2)}) collective-permute-start(bf16[256,2304]{1,0:T(8,128)(2,1)S(1)} %cut.2.refs_0_), channel_id=1, source_target_pairs={{0,8},{4,12},{8,0},{12,4},{1,9},{5,13},{9,1},{13,5},{2,10},{6,14},... | collective-permute-start | bytes 3538952 | tf_op jit(solution)/shard_map/ppermute | solution.py:386
  4.3 2.0 %cut.3 = (bf16[256,1536]{1,0:T(8,128)(2,1)S(1)}, bf16[256,1792]{1,0:T(8,128)(2,1)S(1)}, bf16[256,1536]{1,0:T(8,128)(2,1)S(1)}, bf16[2,128,2048]{2,1,0:T(8,128)(2,1)S(1)}) custom-call(bf16[256,7168]{1,0:T(8,128)(2,1)} %bitcast.13, bf16[2,128,2048]{2,1,0:T(8,128)(2,1)} %a_ref.3, bf16[256,2304]{1,0:T(8,128)(2,1)S(1)} %cut.2.refs_0_), custom_call_target="tpu_custom_call" | custom-call | tf_op jit(solution)/shard_map/cut/pallas_call | solution.py:355
  6.3 2.6 %collective-permute-start.2 = (bf16[2,128,2048]{2,1,0:T(8,128)(2,1)S(1)}, bf16[2,128,2048]{2,1,0:T(8,128)(2,1)S(1)}, u32[]{:S(2)}, u32[]{:S(2)}) collective-permute-start(bf16[2,128,2048]{2,1,0:T(8,128)(2,1)S(1)} %get-tuple-element.43.refs_2_), channel_id=1, source_target_pairs={{1,0},{0,2},{2,3},{3,1},{5,4},{4,6},{6,7},{7,5},{9,8},{8,10},{10,1... | collective-permute-start | bytes 3145736 | tf_op jit(solution)/shard_map/ppermute | solution.py:401
  9.0 0.5 collective-permute-start.7
  9.5 3.1 %load.1 = (bf16[8192,512]{1,0:T(8,128)(2,1)S(1)}, bf16[512,7168]{1,0:T(8,128)(2,1)S(1)}) custom-call(bf16[256,2304]{1,0:T(8,128)(2,1)S(1)} %cut.2.refs_0_, bf16[256,1536]{1,0:T(8,128)(2,1)S(1)} %get-tuple-element.33.refs_1_, bf16[256,1792]{1,0:T(8,128)(2,1)S(1)} %get-tuple-element.34.refs_2_, bf16[256,1536]{1,0:T(8,128)(2,1)S(1)} %get-tuple-element.35.refs_3_, ...), custom_call_target="tpu_custom_call" | custom-call | flops 1024 | bytes 1024 | tf_op jit(solution)/shard_map/load/pallas_call | solution.py:81
  12.6 24.1 %project.5 = (f32[2,512,2048]{2,1,0:T(8,128)S(1)}, f32[8,128]{1,0:T(8,128)S(1)}, bf16[8192,512]{1,0:T(8,128)(2,1)S(1)}, bf16[512,7168]{1,0:T(8,128)(2,1)S(1)}) custom-call(bf16[256,7168]{1,0:T(8,128)(2,1)S(1)} %collective-permute-done.refs_0_, bf16[2,7168,2048]{2,1,0:T(8,128)(2,1)} %refs_4_.5, ...), custom_call_target="tpu_custom_call", output_to_operand_aliasing={{2}: (2, {}), {3}: (3, {})} | custom-call | flops 1024 | bytes 1024 | tf_op jit(solution)/shard_map/project/pallas_call | solution.py:208
  36.8 1.8 %collective-permute-start.12 = (bf16[2,128,2048]{2,1,0:T(8,128)(2,1)S(1)}, bf16[2,128,2048]{2,1,0:T(8,128)(2,1)S(1)}, u32[]{:S(2)}, u32[]{:S(2)}) collective-permute-start(bf16[2,128,2048]{2,1,0:T(8,128)(2,1)S(1)} %after.2.refs_5_.refs_3_), channel_id=1, source_target_pairs={{1,0},{0,2},{2,3},{3,1},{5,4},{4,6},{6,7},{7,5},{9,8},{8,10},{10,1... | collective-permute-start | bytes 3145736 | tf_op jit(solution)/shard_map/ppermute | solution.py:409
  38.6 0.1 halve.4
  38.7 0.1 collective-permute-start.5
  38.8 0.5 collective-permute-start.6
  39.3 1.5 %collective-permute-start.4 = (bf16[256,1792]{1,0:T(8,128)(2,1)S(1)}, bf16[256,1792]{1,0:T(8,128)(2,1)S(1)}, u32[]{:S(2)}, u32[]{:S(2)}) collective-permute-start(bf16[256,1792]{1,0:T(8,128)(2,1)S(1)} %get-tuple-element.34.refs_2_), channel_id=1, source_target_pairs={{0,8},{4,12},{8,0},{12,4},{1,9},{5,13},{9,1},{13,5},{2,10},{6,14},... | collective-permute-start | bytes 2752520 | tf_op jit(solution)/shard_map/ppermute | solution.py:386
  40.8 11.9 %project.6 = (f32[2,512,2048]{2,1,0:T(8,128)S(1)}, f32[8,128]{1,0:T(8,128)S(1)}, bf16[8192,512]{1,0:T(8,128)(2,1)S(1)}, bf16[512,7168]{1,0:T(8,128)(2,1)S(1)}) custom-call(bf16[2,7168,2048]{2,1,0:T(8,128)(2,1)} %refs_4_.5, bf16[8192,512]{1,0:T(8,128)(2,1)S(1)} %get-tuple-element.38.refs_1_, ...), custom_call_target="tpu_custom_call", output_to_operand_aliasing={{2}: (1, {}), {0}: (2, {}), {3}: (3, {})} | custom-call | flops 1024 | bytes 1024 | tf_op jit(solution)/shard_map/project/pallas_call | solution.py:208
  52.8 0.1 halve.5
  52.9 0.1 collective-permute-start.8
  53.0 0.5 collective-permute-start.9
  53.5 0.5 collective-permute-start.3
  54.0 0.7 collective-permute-done.8.refs_5_
  54.7 0.6 collective-permute-done.9.refs_7_
  55.2 17.3 %project.7 = (f32[2,512,2048]{2,1,0:T(8,128)S(1)}, f32[8,128]{1,0:T(8,128)S(1)}, bf16[8192,512]{1,0:T(8,128)(2,1)S(1)}) custom-call(bf16[256,1152]{1,0:T(8,128)(2,1)S(1)} %get-tuple-element.42.refs_4_.refs_1_.refs_0_, bf16[256,1152]{1,0:T(8,128)(2,1)S(1)} %collective-permute-done.5.refs_2_.refs_1_, ...), custom_call_target="tpu_custom_call", output_to_operand_aliasing={{2}: (9, {})} | custom-call | flops 1024 | bytes 1024 | tf_op jit(solution)/shard_map/project/pallas_call | solution.py:208
  72.6 0.6 collective-permute-start.15
  73.2 0.1 halve.6
  73.3 0.1 collective-permute-start.10
  73.4 0.5 collective-permute-start.11
  73.9 1.3 %collective-permute-done.10.refs_1_ = bf16[256,896]{1,0:T(8,128)(2,1)S(1)} collective-permute-done((bf16[256,896]{1,0:T(8,128)(2,1)S(1)}, bf16[256,896]{1,0:T(8,128)(2,1)S(1)}, u32[]{:S(2)}, u32[]{:S(2)}) %collective-permute-start.10) | collective-permute-done | bytes 458784 | tf_op jit(solution)/shard_map/ppermute | solution.py:383
  75.2 0.7 collective-permute-done.11.refs_3_
  75.8 8.2 %project.8 = (f32[2,512,2048]{2,1,0:T(8,128)S(1)}, f32[8,128]{1,0:T(8,128)S(1)}, bf16[8192,512]{1,0:T(8,128)(2,1)S(1)}) custom-call(bf16[256,896]{1,0:T(8,128)(2,1)S(1)} %get-tuple-element.51.refs_0_.refs_7_, bf16[256,896]{1,0:T(8,128)(2,1)S(1)} %collective-permute-done.10.refs_1_, ...), custom_call_target="tpu_custom_call", output_to_operand_aliasing={{2}: (5, {}), {0}: (6, {})} | custom-call | flops 1024 | bytes 1024 | tf_op jit(solution)/shard_map/project/pallas_call | solution.py:208
  84.1 0.3 collective-permute-done.3.source_ref
  84.3 0.1 halve.7
  84.4 0.1 collective-permute-start.13
  84.5 0.5 collective-permute-start.14
  85.0 1.2 %collective-permute-done.13.refs_1_ = bf16[256,768]{1,0:T(8,128)(2,1)S(1)} collective-permute-done((bf16[256,768]{1,0:T(8,128)(2,1)S(1)}, bf16[256,768]{1,0:T(8,128)(2,1)S(1)}, u32[]{:S(2)}, u32[]{:S(2)}) %collective-permute-start.13) | collective-permute-done | bytes 393248 | tf_op jit(solution)/shard_map/ppermute | solution.py:383
  86.2 0.6 collective-permute-done.14.refs_3_
  86.8 7.1 %project.9 = (f32[2,512,2048]{2,1,0:T(8,128)S(1)}, f32[8,128]{1,0:T(8,128)}, bf16[8192,512]{1,0:T(8,128)(2,1)S(1)}) custom-call(bf16[256,768]{1,0:T(8,128)(2,1)S(1)} %get-tuple-element.56.refs_0_.refs_7_, bf16[256,768]{1,0:T(8,128)(2,1)S(1)} %collective-permute-done.13.refs_1_, ...), custom_call_target="tpu_custom_call", output_to_operand_aliasing={{2}: (5, {}), {0}: (6, {})} | custom-call | flops 1024 | bytes 1024 | tf_op jit(solution)/shard_map/project/pallas_call | solution.py:208
  93.9 4.2 %collective-permute-done.15.refs_5_ = bf16[2,128,2048]{2,1,0:T(8,128)(2,1)S(1)} collective-permute-done((bf16[2,128,2048]{2,1,0:T(8,128)(2,1)S(1)}, bf16[2,128,2048]{2,1,0:T(8,128)(2,1)S(1)}, u32[]{:S(2)}, u32[]{:S(2)}) %collective-permute-start.15) | collective-permute-done | bytes 1048608 | tf_op jit(solution)/shard_map/ppermute | solution.py:409
  98.1 2.9 %score.1 = f32[4,2,256]{2,1,0:T(2,128)S(1)} custom-call(f32[2,512,2048]{2,1,0:T(8,128)S(1)} %get-tuple-element.44.refs_0_, f32[2,512,2048]{2,1,0:T(8,128)S(1)} %get-tuple-element.60.refs_1_, bf16[2,128,2048]{2,1,0:T(8,128)(2,1)S(1)} %get-tuple-element.43.refs_2_, bf16[2,128,2048]{2,1,0:T(8,128)(2,1)S(1)} %after.2.refs_5_.refs_3_, ...), custom_call_target="tpu_custom_call" | custom-call | tf_op jit(solution)/shard_map/score/pallas_call | solution.py:272
  101.0 0.1 collective-permute-start.16
  101.1 0.5 collective-permute-start.17
  101.6 1.4 %collective-permute-start.18 = (f32[2,2,512]{2,1,0:T(2,128)S(1)}, f32[2,2,512]{2,1,0:T(2,128)S(1)}, u32[]{:S(2)}, u32[]{:S(2)}) collective-permute-start(f32[2,2,512]{2,1,0:T(2,128)S(1)} %copy_bitcast_fusion), channel_id=1, source_target_pairs={{0,12},{4,8},{8,4},{12,0},{1,13},{5,9},{9,5},{13,1},{2,14},{6,10},... | collective-permute-start | bytes 24584 | tf_op jit(solution)/shard_map/ppermute | solution.py:292
  103.0 0.4 convert_reduce_fusion
  103.4 1.4 %collective-permute-done.17 = f32[2,2,512]{2,1,0:T(2,128)S(1)} collective-permute-done((f32[2,2,512]{2,1,0:T(2,128)S(1)}, f32[2,2,512]{2,1,0:T(2,128)S(1)}, u32[]{:S(2)}, u32[]{:S(2)}) %collective-permute-start.17) | collective-permute-done | bytes 8224 | tf_op jit(solution)/shard_map/ppermute | solution.py:292
  104.8 1.4 %collective-permute-start.19 = (f32[2,2,512]{2,1,0:T(2,128)S(1)}, f32[2,2,512]{2,1,0:T(2,128)S(1)}, u32[]{:S(2)}, u32[]{:S(2)}) collective-permute-start(f32[2,2,512]{2,1,0:T(2,128)S(1)} %add_add_fusion), channel_id=1, source_target_pairs={{0,1},{1,0},{2,3},{3,2},{4,5},{5,4},{6,7},{7,6},{8,9},{9,8},{10,11... | collective-permute-start | bytes 24584 | tf_op jit(solution)/shard_map/ppermute | solution.py:292
  106.2 0.0 collective-permute-start.20
  106.2 3.1 %collective-permute-start.21 = (f32[2,2,512]{2,1,0:T(2,128)S(1)}, f32[2,2,512]{2,1,0:T(2,128)S(1)}, u32[]{:S(2)}, u32[]{:S(2)}) collective-permute-start(f32[2,2,512]{2,1,0:T(2,128)S(1)} %add_add_fusion), channel_id=1, source_target_pairs={{0,3},{1,2},{2,1},{3,0},{4,7},{5,6},{6,5},{7,4},{8,11},{9,10},{10,... | collective-permute-start | bytes 24584 | tf_op jit(solution)/shard_map/ppermute | solution.py:292
  109.3 1.4 %collective-permute-done.20 = f32[2,2,512]{2,1,0:T(2,128)S(1)} collective-permute-done((f32[2,2,512]{2,1,0:T(2,128)S(1)}, f32[2,2,512]{2,1,0:T(2,128)S(1)}, u32[]{:S(2)}, u32[]{:S(2)}) %collective-permute-start.20) | collective-permute-done | bytes 8224 | tf_op jit(solution)/shard_map/ppermute | solution.py:292
  110.8 0.9 collective-permute-done.21
  111.7 0.6 add_multiply_fusion
  (21 shorter events, 0.1 us)
Async XLA Ops:
  0.0 12.6 %collective-permute-start = (bf16[256,7168]{1,0:T(8,128)(2,1)}, bf16[256,7168]{1,0:T(8,128)(2,1)S(1)}, u32[]{:S(2)}, u32[]{:S(2)}) collective-permute-start(bf16[256,7168]{1,0:T(8,128)(2,1)} %bitcast.11), channel_id=1, source_target_pairs={{0,4},{4,0},{8,12},{12,8},{1,5},{5,1},{9,13},{13,9},{2,6},{6,2},{1... | collective-permute-start | bytes 11010056 | tf_op jit(solution)/shard_map/ppermute | solution.py:383
  1.7 36.9 %collective-permute-start.1 = (bf16[256,2304]{1,0:T(8,128)(2,1)S(1)}, bf16[256,2304]{1,0:T(8,128)(2,1)S(1)}, u32[]{:S(2)}, u32[]{:S(2)}) collective-permute-start(bf16[256,2304]{1,0:T(8,128)(2,1)S(1)} %cut.2.refs_0_), channel_id=1, source_target_pairs={{0,8},{4,12},{8,0},{12,4},{1,9},{5,13},{9,1},{13,5},{2,10},{6,14},... | collective-permute-start | bytes 3538952 | tf_op jit(solution)/shard_map/ppermute | solution.py:386
  6.3 30.4 %collective-permute-start.2 = (bf16[2,128,2048]{2,1,0:T(8,128)(2,1)S(1)}, bf16[2,128,2048]{2,1,0:T(8,128)(2,1)S(1)}, u32[]{:S(2)}, u32[]{:S(2)}) collective-permute-start(bf16[2,128,2048]{2,1,0:T(8,128)(2,1)S(1)} %get-tuple-element.43.refs_2_), channel_id=1, source_target_pairs={{1,0},{0,2},{2,3},{3,1},{5,4},{4,6},{6,7},{7,5},{9,8},{8,10},{10,1... | collective-permute-start | bytes 3145736 | tf_op jit(solution)/shard_map/ppermute | solution.py:401
  9.0 43.8 %collective-permute-start.7 = (bf16[256,1536]{1,0:T(8,128)(2,1)S(1)}, bf16[256,1536]{1,0:T(8,128)(2,1)S(1)}, u32[]{:S(2)}, u32[]{:S(2)}) collective-permute-start(bf16[256,1536]{1,0:T(8,128)(2,1)S(1)} %get-tuple-element.33.refs_1_), channel_id=1, source_target_pairs={{0,8},{4,12},{8,0},{12,4},{1,9},{5,13},{9,1},{13,5},{2,10},{6,14},... | collective-permute-start | bytes 2359304 | tf_op jit(solution)/shard_map/ppermute | solution.py:386
  36.8 35.8 %collective-permute-start.12 = (bf16[2,128,2048]{2,1,0:T(8,128)(2,1)S(1)}, bf16[2,128,2048]{2,1,0:T(8,128)(2,1)S(1)}, u32[]{:S(2)}, u32[]{:S(2)}) collective-permute-start(bf16[2,128,2048]{2,1,0:T(8,128)(2,1)S(1)} %after.2.refs_5_.refs_3_), channel_id=1, source_target_pairs={{1,0},{0,2},{2,3},{3,1},{5,4},{4,6},{6,7},{7,5},{9,8},{8,10},{10,1... | collective-permute-start | bytes 3145736 | tf_op jit(solution)/shard_map/ppermute | solution.py:409
  38.7 14.0 %collective-permute-start.5 = (bf16[256,1152]{1,0:T(8,128)(2,1)S(1)}, bf16[256,1152]{1,0:T(8,128)(2,1)S(1)}, u32[]{:S(2)}, u32[]{:S(2)}) collective-permute-start(bf16[256,1152]{1,0:T(8,128)(2,1)S(1)} %get-tuple-element.42.refs_4_.refs_1_.refs_0_), channel_id=1, source_target_pairs={{0,4},{4,0},{8,12},{12,8},{1,5},{5,1},{9,13},{13,9},{2,6},{6,2},{1... | collective-permute-start | bytes 1769480 | tf_op jit(solution)/shard_map/ppermute | solution.py:383
  38.8 14.0 %collective-permute-start.6 = (bf16[256,1152]{1,0:T(8,128)(2,1)S(1)}, bf16[256,1152]{1,0:T(8,128)(2,1)S(1)}, u32[]{:S(2)}, u32[]{:S(2)}) collective-permute-start(bf16[256,1152]{1,0:T(8,128)(2,1)S(1)} %get-tuple-element.45.refs_3_.refs_2_), channel_id=1, source_target_pairs={{0,4},{4,0},{8,12},{12,8},{1,5},{5,1},{9,13},{13,9},{2,6},{6,2},{1... | collective-permute-start | bytes 1769480 | tf_op jit(solution)/shard_map/ppermute | solution.py:383
  39.3 33.9 %collective-permute-start.4 = (bf16[256,1792]{1,0:T(8,128)(2,1)S(1)}, bf16[256,1792]{1,0:T(8,128)(2,1)S(1)}, u32[]{:S(2)}, u32[]{:S(2)}) collective-permute-start(bf16[256,1792]{1,0:T(8,128)(2,1)S(1)} %get-tuple-element.34.refs_2_), channel_id=1, source_target_pairs={{0,8},{4,12},{8,0},{12,4},{1,9},{5,13},{9,1},{13,5},{2,10},{6,14},... | collective-permute-start | bytes 2752520 | tf_op jit(solution)/shard_map/ppermute | solution.py:386
  52.9 1.8 %collective-permute-start.8 = (bf16[256,768]{1,0:T(8,128)(2,1)S(1)}, bf16[256,768]{1,0:T(8,128)(2,1)S(1)}, u32[]{:S(2)}, u32[]{:S(2)}) collective-permute-start(bf16[256,768]{1,0:T(8,128)(2,1)S(1)} %get-tuple-element.47.refs_4_.refs_10_), channel_id=1, source_target_pairs={{0,4},{4,0},{8,12},{12,8},{1,5},{5,1},{9,13},{13,9},{2,6},{6,2},{1... | collective-permute-start | bytes 1179656 | tf_op jit(solution)/shard_map/ppermute | solution.py:383
  53.0 2.3 %collective-permute-start.9 = (bf16[256,768]{1,0:T(8,128)(2,1)S(1)}, bf16[256,768]{1,0:T(8,128)(2,1)S(1)}, u32[]{:S(2)}, u32[]{:S(2)}) collective-permute-start(bf16[256,768]{1,0:T(8,128)(2,1)S(1)} %get-tuple-element.48.refs_6_), channel_id=1, source_target_pairs={{0,4},{4,0},{8,12},{12,8},{1,5},{5,1},{9,13},{13,9},{2,6},{6,2},{1... | collective-permute-start | bytes 1179656 | tf_op jit(solution)/shard_map/ppermute | solution.py:383
  53.5 30.9 %collective-permute-start.3 = (bf16[256,1536]{1,0:T(8,128)(2,1)S(1)}, bf16[256,1536]{1,0:T(8,128)(2,1)S(1)}, u32[]{:S(2)}, u32[]{:S(2)}) collective-permute-start(bf16[256,1536]{1,0:T(8,128)(2,1)S(1)} %get-tuple-element.35.refs_3_), channel_id=1, source_target_pairs={{0,8},{4,12},{8,0},{12,4},{1,9},{5,13},{9,1},{13,5},{2,10},{6,14},... | collective-permute-start | bytes 2359304 | tf_op jit(solution)/shard_map/ppermute | solution.py:386
  72.6 25.5 %collective-permute-start.15 = (bf16[2,128,2048]{2,1,0:T(8,128)(2,1)S(1)}, bf16[2,128,2048]{2,1,0:T(8,128)(2,1)S(1)}, u32[]{:S(2)}, u32[]{:S(2)}) collective-permute-start(bf16[2,128,2048]{2,1,0:T(8,128)(2,1)S(1)} %after.3.refs_8_.refs_4_), channel_id=1, source_target_pairs={{1,0},{0,2},{2,3},{3,1},{5,4},{4,6},{6,7},{7,5},{9,8},{8,10},{10,1... | collective-permute-start | bytes 3145736 | tf_op jit(solution)/shard_map/ppermute | solution.py:409
  73.3 1.9 %collective-permute-start.10 = (bf16[256,896]{1,0:T(8,128)(2,1)S(1)}, bf16[256,896]{1,0:T(8,128)(2,1)S(1)}, u32[]{:S(2)}, u32[]{:S(2)}) collective-permute-start(bf16[256,896]{1,0:T(8,128)(2,1)S(1)} %get-tuple-element.51.refs_0_.refs_7_), channel_id=1, source_target_pairs={{0,4},{4,0},{8,12},{12,8},{1,5},{5,1},{9,13},{13,9},{2,6},{6,2},{1... | collective-permute-start | bytes 1376264 | tf_op jit(solution)/shard_map/ppermute | solution.py:383
  73.4 2.5 %collective-permute-start.11 = (bf16[256,896]{1,0:T(8,128)(2,1)S(1)}, bf16[256,896]{1,0:T(8,128)(2,1)S(1)}, u32[]{:S(2)}, u32[]{:S(2)}) collective-permute-start(bf16[256,896]{1,0:T(8,128)(2,1)S(1)} %get-tuple-element.52.refs_2_), channel_id=1, source_target_pairs={{0,4},{4,0},{8,12},{12,8},{1,5},{5,1},{9,13},{13,9},{2,6},{6,2},{1... | collective-permute-start | bytes 1376264 | tf_op jit(solution)/shard_map/ppermute | solution.py:383
  84.4 1.8 %collective-permute-start.13 = (bf16[256,768]{1,0:T(8,128)(2,1)S(1)}, bf16[256,768]{1,0:T(8,128)(2,1)S(1)}, u32[]{:S(2)}, u32[]{:S(2)}) collective-permute-start(bf16[256,768]{1,0:T(8,128)(2,1)S(1)} %get-tuple-element.56.refs_0_.refs_7_), channel_id=1, source_target_pairs={{0,4},{4,0},{8,12},{12,8},{1,5},{5,1},{9,13},{13,9},{2,6},{6,2},{1... | collective-permute-start | bytes 1179656 | tf_op jit(solution)/shard_map/ppermute | solution.py:383
  84.5 2.3 %collective-permute-start.14 = (bf16[256,768]{1,0:T(8,128)(2,1)S(1)}, bf16[256,768]{1,0:T(8,128)(2,1)S(1)}, u32[]{:S(2)}, u32[]{:S(2)}) collective-permute-start(bf16[256,768]{1,0:T(8,128)(2,1)S(1)} %get-tuple-element.57.refs_2_), channel_id=1, source_target_pairs={{0,4},{4,0},{8,12},{12,8},{1,5},{5,1},{9,13},{13,9},{2,6},{6,2},{1... | collective-permute-start | bytes 1179656 | tf_op jit(solution)/shard_map/ppermute | solution.py:383
  98.1 4.9 %copy-start = (s32[2,512]{1,0:T(2,128)S(1)}, s32[2,512]{1,0:T(2,128)}, u32[]{:S(2)}) copy-start(s32[2,512]{1,0:T(2,128)} %param.8) | copy-start | bytes 12292
  98.1 11.2 %copy-start.1 = (s32[2,512]{1,0:T(2,128)S(1)}, s32[2,512]{1,0:T(2,128)}, u32[]{:S(2)}) copy-start(s32[2,512]{1,0:T(2,128)} %param.9) | copy-start | bytes 12292
  101.0 2.4 %collective-permute-start.16 = (f32[2,2,512]{2,1,0:T(2,128)S(1)}, f32[2,2,512]{2,1,0:T(2,128)S(1)}, u32[]{:S(2)}, u32[]{:S(2)}) collective-permute-start(f32[2,2,512]{2,1,0:T(2,128)S(1)} %copy_bitcast_fusion), channel_id=1, source_target_pairs={{0,4},{4,0},{8,12},{12,8},{1,5},{5,1},{9,13},{13,9},{2,6},{6,2},{1... | collective-permute-start | bytes 24584 | tf_op jit(solution)/shard_map/ppermute | solution.py:292
  101.1 3.7 %collective-permute-start.17 = (f32[2,2,512]{2,1,0:T(2,128)S(1)}, f32[2,2,512]{2,1,0:T(2,128)S(1)}, u32[]{:S(2)}, u32[]{:S(2)}) collective-permute-start(f32[2,2,512]{2,1,0:T(2,128)S(1)} %copy_bitcast_fusion), channel_id=1, source_target_pairs={{0,8},{4,12},{8,0},{12,4},{1,9},{5,13},{9,1},{13,5},{2,10},{6,14},... | collective-permute-start | bytes 24584 | tf_op jit(solution)/shard_map/ppermute | solution.py:292
  101.6 3.2 %collective-permute-start.18 = (f32[2,2,512]{2,1,0:T(2,128)S(1)}, f32[2,2,512]{2,1,0:T(2,128)S(1)}, u32[]{:S(2)}, u32[]{:S(2)}) collective-permute-start(f32[2,2,512]{2,1,0:T(2,128)S(1)} %copy_bitcast_fusion), channel_id=1, source_target_pairs={{0,12},{4,8},{8,4},{12,0},{1,13},{5,9},{9,5},{13,1},{2,14},{6,10},... | collective-permute-start | bytes 24584 | tf_op jit(solution)/shard_map/ppermute | solution.py:292
  104.8 4.5 %collective-permute-start.19 = (f32[2,2,512]{2,1,0:T(2,128)S(1)}, f32[2,2,512]{2,1,0:T(2,128)S(1)}, u32[]{:S(2)}, u32[]{:S(2)}) collective-permute-start(f32[2,2,512]{2,1,0:T(2,128)S(1)} %add_add_fusion), channel_id=1, source_target_pairs={{0,1},{1,0},{2,3},{3,2},{4,5},{5,4},{6,7},{7,6},{8,9},{9,8},{10,11... | collective-permute-start | bytes 24584 | tf_op jit(solution)/shard_map/ppermute | solution.py:292
  106.2 4.5 %collective-permute-start.20 = (f32[2,2,512]{2,1,0:T(2,128)S(1)}, f32[2,2,512]{2,1,0:T(2,128)S(1)}, u32[]{:S(2)}, u32[]{:S(2)}) collective-permute-start(f32[2,2,512]{2,1,0:T(2,128)S(1)} %add_add_fusion), channel_id=1, source_target_pairs={{0,2},{1,3},{2,0},{3,1},{4,6},{5,7},{6,4},{7,5},{8,10},{9,11},{10,... | collective-permute-start | bytes 24584 | tf_op jit(solution)/shard_map/ppermute | solution.py:292
  106.2 5.4 %collective-permute-start.21 = (f32[2,2,512]{2,1,0:T(2,128)S(1)}, f32[2,2,512]{2,1,0:T(2,128)S(1)}, u32[]{:S(2)}, u32[]{:S(2)}) collective-permute-start(f32[2,2,512]{2,1,0:T(2,128)S(1)} %add_add_fusion), channel_id=1, source_target_pairs={{0,3},{1,2},{2,1},{3,0},{4,7},{5,6},{6,5},{7,4},{8,11},{9,10},{10,... | collective-permute-start | bytes 24584 | tf_op jit(solution)/shard_map/ppermute | solution.py:292

commit v7 on v6

--- a/solution.py
+++ b/solution.py
@@ -9,10 +9,8 @@
 from jax.sharding import PartitionSpec as P
 
 WEIGHTS = (9, 6, 7, 6)
-GROUPS = (2, 1, 1)
 HELPER_VMEM = 1024 * 1024
 TILE = 512
-STRIP_ROWS = 8192
 
 
 def tile_of(length, most):
@@ -204,7 +202,7 @@
         pltpu.SemaphoreType.DMA((max(plan.strips, later.strips if later else 1),)),
         pltpu.SemaphoreType.DMA((plan.strips,)),
     ]
-    limit = 2 * slot.size + (2 * rows * plan.depth if laid is None else 0) + 4 * 1024 * 1024
+    limit = 2 * slot.size + (2 * rows * plan.depth if laid is None else 0) + 3 * 1024 * 1024
     return pl.pallas_call(
         functools.partial(
             project_kernel, len(parts), plan, later, not fresh and laid is None, laid is not None
@@ -417,50 +415,45 @@
     def receive(mark, count=1):
         ended = []
         for _ in range(min(count, len(coming))):
-            pieces = [halve(piece, mark, *waiting) for piece in coming.pop(0)]
+            pieces = [halve(piece, mark, *sum(waiting, [])) for piece in coming.pop(0)]
+            parts = []
             for halves in zip(*pieces):
                 for half in halves:
-                    waiting.extend([half, flip(half)] if pair == 2 else [half])
+                    parts += [half, flip(half)] if pair == 2 else [half]
+            waiting.append(parts)
             ended += [halves[0] for halves in pieces]
         return ended
 
-    room = max(depth, STRIP_ROWS if depth >= STRIP_ROWS // 2 else 0)
+    room = depth
     near_plan = plan_of(queries, 0, depth, width, depth)
     early = near_plan.steps * 3 // 8 * 2 or near_plan.steps
     plans = [near_plan._replace(steps=early)]
     if early < near_plan.steps:
         plans.append(near_plan._replace(first=early, steps=near_plan.steps - early))
-    near_calls = len(plans)
-    chosen = []
-    for count in GROUPS + (1,) * chunks:
-        group, spans = (spans[:count], spans[count:]) if chips > 1 else ([], [])
-        if group:
-            chosen.append(count)
-            length = sum(length for _, length in group)
-            plans.append(plan_of(queries, group[0][0], length, width, room))
-    plans.append(None)
+    far_plans = [plan_of(queries, begin, length, width, room) for begin, length in spans] if chips > 1 else []
+
+    calls = [("near", plans[0], 0), *[("far", plan, 1) for plan in far_plans[:1]]]
+    calls += [("near", plan, min(1, len(far_plans[1:]))) for plan in plans[1:]]
+    calls += [("far", plan, 0 if at == 0 and len(plans) > 1 else 1) for at, plan in enumerate(far_plans[1:])]
 
     slot, laid = load(pieces_out or [own], pair * rows, query_grads, plans[0], room)
-    near_sum = None
-    got = 0
-    for at in range(near_calls):
-        others = []
-        if at > 0:
-            got = min(1, len(coming))
-            others = receive(mark) + step_along(mark)
-        near_sum, mark, slot, laid = project(
-            [] if at else near, pair * rows, query_grads, plans[at], plans[at + 1], slot, near_sum, others, laid
-        )
-    sums = [near_sum]
-    running = None
-    for at, count in enumerate(chosen):
-        others = receive(mark, count - (got if at == 0 else 0)) + (step_along(mark) if at > 0 else [])
-        running, mark, slot = project(
-            waiting, (inp_size - pair) * rows, query_grads, plans[near_calls + at], plans[near_calls + at + 1], slot, running, others
-        )
-        waiting.clear()
-    if running is not None:
-        sums.append(running)
+    near_sum = far_sum = None
+    for at, (kind, plan, count) in enumerate(calls):
+        later = calls[at + 1][1] if at + 1 < len(calls) else None
+        others = receive(mark, count) if at > 0 else []
+        if kind == "far" and count:
+            others += step_along(mark)
+        if kind == "far" and any(later_kind == "near" for later_kind, _, _ in calls[at:]):
+            others.append(pltpu.with_memory_space_constraint(laid, pltpu.VMEM))
+        if kind == "near":
+            near_sum, mark, slot, laid = project(
+                near if at == 0 else [], pair * rows, query_grads, plan, later, slot, near_sum, others, laid
+            )
+        else:
+            far_sum, mark, slot = project(
+                waiting.pop(0), (inp_size - pair) * rows, query_grads, plan, later, slot, far_sum, others
+            )
+    sums = [near_sum] + ([] if far_sum is None else [far_sum])
     raw = score(sums, slots, ring, inp_size, pair, queries, blocks, shard)
     raw = raw.reshape(inp_size, queries, blocks, shard).transpose(1, 2, 0, 3).reshape(queries, blocks, tokens)
     raw = xor_sum(xor_sum(raw, "inp", inp_size), "out", out_size)

time: 112 us -> 114 us (1.018)
  Pallas kernels: 78.4 us -> 79.6 us
    pallas_call x5 -> x6, Pallas kernels: 68.7 us -> 70.1 us  [project(): pl.pallas_call(functools.partial(project_kernel, len(parts), plan, later,...]
  transfers between devices with their start and end apart: 22 -> 22, of which waited for: 11 -> 9; matrix products, arithmetic and copies ran while one was open for 0% -> 0% of each run, Pallas kernels for 67% -> 68%
where the time goes in v7:
time: 114 us
  Pallas kernels  79.6 us (70%)
  starting transfers between devices  20.3 us (18%)
  waiting for transfers between devices  12.5 us (11%)
    pallas_call x6, Pallas kernels, project(): pl.pallas_call(functools.partial(project_kernel, len(parts), plan, later,...  70.1 us
    ppermute x6, starting transfers between devices, xor_sum(): lax.ppermute(value, axis, [(at, at ^ other) for at in range(size)])  6.38 us
    ppermute x4, starting transfers between devices, shift(): lax.ppermute(value, 'inp', [(at, (at + pair * by) % inp_size) for at in r...  6.13 us
    ppermute x9, waiting for transfers between devices, flip(): return lax.ppermute(value, 'inp', [(at, at ^ 1) for at in range(inp_size)])  4.56 us
    ppermute x2, waiting for transfers between devices, step_along(): slots.append(lax.ppermute(ended, 'out', turn))  4.13 us
    ppermute x6, waiting for transfers between devices, xor_sum(): lax.ppermute(value, axis, [(at, at ^ other) for at in range(size)])  3.81 us
    pallas_call x2, Pallas kernels, cut(): pl.pallas_call(functools.partial(cut_kernel, spans, len(shapes)), in_spec...  3.29 us
    pallas_call x1, Pallas kernels, load(): pl.pallas_call(functools.partial(load_kernel, plan, len(own)), in_specs=[...  3.13 us
  transfers between devices with their start and end apart: 22, of which 9 were waited for; matrix products, arithmetic and copies ran while one was open for 0% of the time, Pallas kernels for 68%

profile of v7, /device:TPU:0, one launch (start us, length us, event | category | flops | bytes accessed | tf_op | source)
XLA Modules:
  0.0 113.8 jit_solution(11440890659214209627)
XLA Ops:
  0.0 0.5 collective-permute-start.1
  0.5 1.3 %cut.2.refs_0_ = bf16[256,2304]{1,0:T(8,128)(2,1)S(1)} custom-call(bf16[256,7168]{1,0:T(8,128)(2,1)} %bitcast.12, bf16[2,128,2048]{2,1,0:T(8,128)(2,1)} %a_ref.3), custom_call_target="tpu_custom_call" | custom-call | tf_op jit(solution)/shard_map/cut/pallas_call | solution.py:353
  1.7 2.6 %collective-permute-start = (bf16[256,2304]{1,0:T(8,128)(2,1)S(1)}, bf16[256,2304]{1,0:T(8,128)(2,1)S(1)}, u32[]{:S(2)}, u32[]{:S(2)}) collective-permute-start(bf16[256,2304]{1,0:T(8,128)(2,1)S(1)} %cut.2.refs_0_), channel_id=1, source_target_pairs={{0,8},{4,12},{8,0},{12,4},{1,9},{5,13},{9,1},{13,5},{2,10},{6,14},... | collective-permute-start | bytes 3538952 | tf_op jit(solution)/shard_map/ppermute | solution.py:384
  4.3 2.0 %cut.3 = (bf16[256,1536]{1,0:T(8,128)(2,1)S(1)}, bf16[256,1792]{1,0:T(8,128)(2,1)S(1)}, bf16[256,1536]{1,0:T(8,128)(2,1)S(1)}, bf16[2,128,2048]{2,1,0:T(8,128)(2,1)S(1)}) custom-call(bf16[256,7168]{1,0:T(8,128)(2,1)} %bitcast.13, bf16[2,128,2048]{2,1,0:T(8,128)(2,1)} %a_ref.3, bf16[256,2304]{1,0:T(8,128)(2,1)S(1)} %cut.2.refs_0_), custom_call_target="tpu_custom_call" | custom-call | tf_op jit(solution)/shard_map/cut/pallas_call | solution.py:353
  6.3 2.6 %collective-permute-start.4 = (bf16[2,128,2048]{2,1,0:T(8,128)(2,1)S(1)}, bf16[2,128,2048]{2,1,0:T(8,128)(2,1)S(1)}, u32[]{:S(2)}, u32[]{:S(2)}) collective-permute-start(bf16[2,128,2048]{2,1,0:T(8,128)(2,1)S(1)} %get-tuple-element.44.refs_2_), channel_id=1, source_target_pairs={{1,0},{0,2},{2,3},{3,1},{5,4},{4,6},{6,7},{7,5},{9,8},{8,10},{10,1... | collective-permute-start | bytes 3145736 | tf_op jit(solution)/shard_map/ppermute | solution.py:399
  9.0 0.5 collective-permute-start.5
  9.5 3.1 %load.1 = (bf16[7168,512]{1,0:T(8,128)(2,1)S(1)}, bf16[512,7168]{1,0:T(8,128)(2,1)S(1)}) custom-call(bf16[256,2304]{1,0:T(8,128)(2,1)S(1)} %cut.2.refs_0_, bf16[256,1536]{1,0:T(8,128)(2,1)S(1)} %get-tuple-element.35.refs_1_, bf16[256,1792]{1,0:T(8,128)(2,1)S(1)} %get-tuple-element.36.refs_2_, bf16[256,1536]{1,0:T(8,128)(2,1)S(1)} %get-tuple-element.37.refs_3_, ...), custom_call_target="tpu_custom_call" | custom-call | flops 1024 | bytes 1024 | tf_op jit(solution)/shard_map/load/pallas_call | solution.py:79
  12.6 24.1 %project.6 = (f32[2,512,2048]{2,1,0:T(8,128)S(1)}, f32[8,128]{1,0:T(8,128)S(1)}, bf16[7168,512]{1,0:T(8,128)(2,1)S(1)}, bf16[512,7168]{1,0:T(8,128)(2,1)S(1)}) custom-call(bf16[256,7168]{1,0:T(8,128)(2,1)S(1)} %collective-permute-done.1.refs_0_, bf16[2,7168,2048]{2,1,0:T(8,128)(2,1)} %refs_4_.9, ...), custom_call_target="tpu_custom_call", output_to_operand_aliasing={{2}: (2, {}), {3}: (3, {})} | custom-call | flops 1024 | bytes 1024 | tf_op jit(solution)/shard_map/project/pallas_call | solution.py:206
  36.7 1.8 %collective-permute-start.12 = (bf16[2,128,2048]{2,1,0:T(8,128)(2,1)S(1)}, bf16[2,128,2048]{2,1,0:T(8,128)(2,1)S(1)}, u32[]{:S(2)}, u32[]{:S(2)}) collective-permute-start(bf16[2,128,2048]{2,1,0:T(8,128)(2,1)S(1)} %after.2.refs_7_.refs_3_), channel_id=1, source_target_pairs={{1,0},{0,2},{2,3},{3,1},{5,4},{4,6},{6,7},{7,5},{9,8},{8,10},{10,1... | collective-permute-start | bytes 3145736 | tf_op jit(solution)/shard_map/ppermute | solution.py:407
  38.5 0.0 collective-permute-done.source_ref
  38.6 0.1 halve.4
  38.7 0.1 collective-permute-start.2
  38.8 0.5 collective-permute-start.3
  39.3 1.5 %collective-permute-start.7 = (bf16[256,1792]{1,0:T(8,128)(2,1)S(1)}, bf16[256,1792]{1,0:T(8,128)(2,1)S(1)}, u32[]{:S(2)}, u32[]{:S(2)}) collective-permute-start(bf16[256,1792]{1,0:T(8,128)(2,1)S(1)} %get-tuple-element.36.refs_2_), channel_id=1, source_target_pairs={{0,8},{4,12},{8,0},{12,4},{1,9},{5,13},{9,1},{13,5},{2,10},{6,14},... | collective-permute-start | bytes 2752520 | tf_op jit(solution)/shard_map/ppermute | solution.py:384
  40.8 0.8 collective-permute-done.3.refs_3_
  41.6 10.8 %project.7 = (f32[2,512,2048]{2,1,0:T(8,128)S(1)}, f32[8,128]{1,0:T(8,128)S(1)}, bf16[7168,512]{1,0:T(8,128)(2,1)S(1)}) custom-call(bf16[256,1152]{1,0:T(8,128)(2,1)S(1)} %get-tuple-element.41.refs_0_.refs_6_, bf16[256,1152]{1,0:T(8,128)(2,1)S(1)} %collective-permute-done.2.refs_1_, ...), custom_call_target="tpu_custom_call", output_to_operand_aliasing={{2}: (5, {})} | custom-call | flops 1024 | bytes 1024 | tf_op jit(solution)/shard_map/project/pallas_call | solution.py:206
  52.4 0.1 halve.5
  52.5 0.2 collective-permute-start.8
  52.7 0.4 collective-permute-start.9
  53.1 1.5 %collective-permute-start.6 = (bf16[256,1536]{1,0:T(8,128)(2,1)S(1)}, bf16[256,1536]{1,0:T(8,128)(2,1)S(1)}, u32[]{:S(2)}, u32[]{:S(2)}) collective-permute-start(bf16[256,1536]{1,0:T(8,128)(2,1)S(1)} %get-tuple-element.37.refs_3_), channel_id=1, source_target_pairs={{0,8},{4,12},{8,0},{12,4},{1,9},{5,13},{9,1},{13,5},{2,10},{6,14},... | collective-permute-start | bytes 2359304 | tf_op jit(solution)/shard_map/ppermute | solution.py:384
  54.6 12.8 %project.8 = (f32[2,512,2048]{2,1,0:T(8,128)S(1)}, f32[8,128]{1,0:T(8,128)}, bf16[7168,512]{1,0:T(8,128)(2,1)S(1)}, bf16[512,7168]{1,0:T(8,128)(2,1)S(1)}) custom-call(bf16[2,7168,2048]{2,1,0:T(8,128)(2,1)} %refs_4_.9, bf16[7168,512]{1,0:T(8,128)(2,1)S(1)} %get-tuple-element.46.refs_1_, ...), custom_call_target="tpu_custom_call", output_to_operand_aliasing={{2}: (1, {}), {0}: (2, {}), {3}: (3, {})} | custom-call | flops 1024 | bytes 1024 | tf_op jit(solution)/shard_map/project/pallas_call | solution.py:206
  67.4 7.1 %project.9 = (f32[2,512,2048]{2,1,0:T(8,128)S(1)}, f32[8,128]{1,0:T(8,128)S(1)}, bf16[7168,512]{1,0:T(8,128)(2,1)S(1)}) custom-call(bf16[256,768]{1,0:T(8,128)(2,1)S(1)} %get-tuple-element.49.refs_4_.refs_0_, bf16[256,768]{1,0:T(8,128)(2,1)S(1)} %collective-permute-done.8.refs_1_, ...), custom_call_target="tpu_custom_call", output_to_operand_aliasing={{2}: (5, {}), {0}: (6, {})} | custom-call | flops 1024 | bytes 1024 | tf_op jit(solution)/shard_map/project/pallas_call | solution.py:206
  74.6 0.6 collective-permute-start.15
  75.2 0.1 halve.6
  75.3 0.1 collective-permute-start.10
  75.4 0.5 collective-permute-start.11
  75.9 1.3 %collective-permute-done.10.refs_1_ = bf16[256,896]{1,0:T(8,128)(2,1)S(1)} collective-permute-done((bf16[256,896]{1,0:T(8,128)(2,1)S(1)}, bf16[256,896]{1,0:T(8,128)(2,1)S(1)}, u32[]{:S(2)}, u32[]{:S(2)}) %collective-permute-start.10) | collective-permute-done | bytes 458784 | tf_op jit(solution)/shard_map/ppermute | solution.py:381
  77.2 0.7 collective-permute-done.11.refs_3_
  77.8 8.2 %project.10 = (f32[2,512,2048]{2,1,0:T(8,128)S(1)}, f32[8,128]{1,0:T(8,128)S(1)}, bf16[7168,512]{1,0:T(8,128)(2,1)S(1)}) custom-call(bf16[256,896]{1,0:T(8,128)(2,1)S(1)} %get-tuple-element.55.refs_0_.refs_7_, bf16[256,896]{1,0:T(8,128)(2,1)S(1)} %collective-permute-done.10.refs_1_, ...), custom_call_target="tpu_custom_call", output_to_operand_aliasing={{2}: (5, {}), {0}: (6, {})} | custom-call | flops 1024 | bytes 1024 | tf_op jit(solution)/shard_map/project/pallas_call | solution.py:206
  86.1 0.1 halve.7
  86.2 0.2 collective-permute-start.13
  86.4 0.4 collective-permute-start.14
  86.7 1.2 %collective-permute-done.13.refs_1_ = bf16[256,768]{1,0:T(8,128)(2,1)S(1)} collective-permute-done((bf16[256,768]{1,0:T(8,128)(2,1)S(1)}, bf16[256,768]{1,0:T(8,128)(2,1)S(1)}, u32[]{:S(2)}, u32[]{:S(2)}) %collective-permute-start.13) | collective-permute-done | bytes 393248 | tf_op jit(solution)/shard_map/ppermute | solution.py:381
  87.9 0.6 collective-permute-done.14.refs_3_
  88.5 7.1 %project.11 = (f32[2,512,2048]{2,1,0:T(8,128)S(1)}, f32[8,128]{1,0:T(8,128)}, bf16[7168,512]{1,0:T(8,128)(2,1)S(1)}) custom-call(bf16[256,768]{1,0:T(8,128)(2,1)S(1)} %get-tuple-element.60.refs_0_.refs_7_, bf16[256,768]{1,0:T(8,128)(2,1)S(1)} %collective-permute-done.13.refs_1_, ...), custom_call_target="tpu_custom_call", output_to_operand_aliasing={{2}: (5, {}), {0}: (6, {})} | custom-call | flops 1024 | bytes 1024 | tf_op jit(solution)/shard_map/project/pallas_call | solution.py:206
  95.6 4.1 %collective-permute-done.15.refs_5_ = bf16[2,128,2048]{2,1,0:T(8,128)(2,1)S(1)} collective-permute-done((bf16[2,128,2048]{2,1,0:T(8,128)(2,1)S(1)}, bf16[2,128,2048]{2,1,0:T(8,128)(2,1)S(1)}, u32[]{:S(2)}, u32[]{:S(2)}) %collective-permute-start.15) | collective-permute-done | bytes 1048608 | tf_op jit(solution)/shard_map/ppermute | solution.py:407
  99.8 2.7 %score.1 = f32[4,2,256]{2,1,0:T(2,128)S(1)} custom-call(f32[2,512,2048]{2,1,0:T(8,128)S(1)} %get-tuple-element.50.refs_0_, f32[2,512,2048]{2,1,0:T(8,128)S(1)} %get-tuple-element.64.refs_1_, bf16[2,128,2048]{2,1,0:T(8,128)(2,1)S(1)} %get-tuple-element.44.refs_2_, bf16[2,128,2048]{2,1,0:T(8,128)(2,1)S(1)} %after.2.refs_7_.refs_3_, ...), custom_call_target="tpu_custom_call" | custom-call | tf_op jit(solution)/shard_map/score/pallas_call | solution.py:270
  102.5 0.1 collective-permute-start.16
  102.6 0.5 collective-permute-start.17
  103.1 1.3 %collective-permute-start.18 = (f32[2,2,512]{2,1,0:T(2,128)S(1)}, f32[2,2,512]{2,1,0:T(2,128)S(1)}, u32[]{:S(2)}, u32[]{:S(2)}) collective-permute-start(f32[2,2,512]{2,1,0:T(2,128)S(1)} %copy_bitcast_fusion), channel_id=1, source_target_pairs={{0,12},{4,8},{8,4},{12,0},{1,13},{5,9},{9,5},{13,1},{2,14},{6,10},... | collective-permute-start | bytes 24584 | tf_op jit(solution)/shard_map/ppermute | solution.py:290
  104.4 0.4 convert_reduce_fusion
  104.8 1.4 %collective-permute-done.17 = f32[2,2,512]{2,1,0:T(2,128)S(1)} collective-permute-done((f32[2,2,512]{2,1,0:T(2,128)S(1)}, f32[2,2,512]{2,1,0:T(2,128)S(1)}, u32[]{:S(2)}, u32[]{:S(2)}) %collective-permute-start.17) | collective-permute-done | bytes 8224 | tf_op jit(solution)/shard_map/ppermute | solution.py:290
  106.3 1.4 %collective-permute-start.19 = (f32[2,2,512]{2,1,0:T(2,128)S(1)}, f32[2,2,512]{2,1,0:T(2,128)S(1)}, u32[]{:S(2)}, u32[]{:S(2)}) collective-permute-start(f32[2,2,512]{2,1,0:T(2,128)S(1)} %add_add_fusion), channel_id=1, source_target_pairs={{0,1},{1,0},{2,3},{3,2},{4,5},{5,4},{6,7},{7,6},{8,9},{9,8},{10,11... | collective-permute-start | bytes 24584 | tf_op jit(solution)/shard_map/ppermute | solution.py:290
  107.7 0.0 collective-permute-start.20
  107.7 3.1 %collective-permute-start.21 = (f32[2,2,512]{2,1,0:T(2,128)S(1)}, f32[2,2,512]{2,1,0:T(2,128)S(1)}, u32[]{:S(2)}, u32[]{:S(2)}) collective-permute-start(f32[2,2,512]{2,1,0:T(2,128)S(1)} %add_add_fusion), channel_id=1, source_target_pairs={{0,3},{1,2},{2,1},{3,0},{4,7},{5,6},{6,5},{7,4},{8,11},{9,10},{10,... | collective-permute-start | bytes 24584 | tf_op jit(solution)/shard_map/ppermute | solution.py:290
  110.8 1.5 %collective-permute-done.20 = f32[2,2,512]{2,1,0:T(2,128)S(1)} collective-permute-done((f32[2,2,512]{2,1,0:T(2,128)S(1)}, f32[2,2,512]{2,1,0:T(2,128)S(1)}, u32[]{:S(2)}, u32[]{:S(2)}) %collective-permute-start.20) | collective-permute-done | bytes 8224 | tf_op jit(solution)/shard_map/ppermute | solution.py:290
  112.2 0.9 collective-permute-done.21
  113.1 0.6 add_multiply_fusion
  (22 shorter events, 0.1 us)
Async XLA Ops:
  0.0 12.6 %collective-permute-start.1 = (bf16[256,7168]{1,0:T(8,128)(2,1)}, bf16[256,7168]{1,0:T(8,128)(2,1)S(1)}, u32[]{:S(2)}, u32[]{:S(2)}) collective-permute-start(bf16[256,7168]{1,0:T(8,128)(2,1)} %bitcast.11), channel_id=1, source_target_pairs={{0,4},{4,0},{8,12},{12,8},{1,5},{5,1},{9,13},{13,9},{2,6},{6,2},{1... | collective-permute-start | bytes 11010056 | tf_op jit(solution)/shard_map/ppermute | solution.py:381
  1.7 36.8 %collective-permute-start = (bf16[256,2304]{1,0:T(8,128)(2,1)S(1)}, bf16[256,2304]{1,0:T(8,128)(2,1)S(1)}, u32[]{:S(2)}, u32[]{:S(2)}) collective-permute-start(bf16[256,2304]{1,0:T(8,128)(2,1)S(1)} %cut.2.refs_0_), channel_id=1, source_target_pairs={{0,8},{4,12},{8,0},{12,4},{1,9},{5,13},{9,1},{13,5},{2,10},{6,14},... | collective-permute-start | bytes 3538952 | tf_op jit(solution)/shard_map/ppermute | solution.py:384
  6.3 30.4 %collective-permute-start.4 = (bf16[2,128,2048]{2,1,0:T(8,128)(2,1)S(1)}, bf16[2,128,2048]{2,1,0:T(8,128)(2,1)S(1)}, u32[]{:S(2)}, u32[]{:S(2)}) collective-permute-start(bf16[2,128,2048]{2,1,0:T(8,128)(2,1)S(1)} %get-tuple-element.44.refs_2_), channel_id=1, source_target_pairs={{1,0},{0,2},{2,3},{3,1},{5,4},{4,6},{6,7},{7,5},{9,8},{8,10},{10,1... | collective-permute-start | bytes 3145736 | tf_op jit(solution)/shard_map/ppermute | solution.py:399
  9.0 43.4 %collective-permute-start.5 = (bf16[256,1536]{1,0:T(8,128)(2,1)S(1)}, bf16[256,1536]{1,0:T(8,128)(2,1)S(1)}, u32[]{:S(2)}, u32[]{:S(2)}) collective-permute-start(bf16[256,1536]{1,0:T(8,128)(2,1)S(1)} %get-tuple-element.35.refs_1_), channel_id=1, source_target_pairs={{0,8},{4,12},{8,0},{12,4},{1,9},{5,13},{9,1},{13,5},{2,10},{6,14},... | collective-permute-start | bytes 2359304 | tf_op jit(solution)/shard_map/ppermute | solution.py:384
  36.7 37.8 %collective-permute-start.12 = (bf16[2,128,2048]{2,1,0:T(8,128)(2,1)S(1)}, bf16[2,128,2048]{2,1,0:T(8,128)(2,1)S(1)}, u32[]{:S(2)}, u32[]{:S(2)}) collective-permute-start(bf16[2,128,2048]{2,1,0:T(8,128)(2,1)S(1)} %after.2.refs_7_.refs_3_), channel_id=1, source_target_pairs={{1,0},{0,2},{2,3},{3,1},{5,4},{4,6},{6,7},{7,5},{9,8},{8,10},{10,1... | collective-permute-start | bytes 3145736 | tf_op jit(solution)/shard_map/ppermute | solution.py:407
  38.7 2.1 %collective-permute-start.2 = (bf16[256,1152]{1,0:T(8,128)(2,1)S(1)}, bf16[256,1152]{1,0:T(8,128)(2,1)S(1)}, u32[]{:S(2)}, u32[]{:S(2)}) collective-permute-start(bf16[256,1152]{1,0:T(8,128)(2,1)S(1)} %get-tuple-element.41.refs_0_.refs_6_), channel_id=1, source_target_pairs={{0,4},{4,0},{8,12},{12,8},{1,5},{5,1},{9,13},{13,9},{2,6},{6,2},{1... | collective-permute-start | bytes 1769480 | tf_op jit(solution)/shard_map/ppermute | solution.py:381
  38.8 2.8 %collective-permute-start.3 = (bf16[256,1152]{1,0:T(8,128)(2,1)S(1)}, bf16[256,1152]{1,0:T(8,128)(2,1)S(1)}, u32[]{:S(2)}, u32[]{:S(2)}) collective-permute-start(bf16[256,1152]{1,0:T(8,128)(2,1)S(1)} %get-tuple-element.42.refs_2_), channel_id=1, source_target_pairs={{0,4},{4,0},{8,12},{12,8},{1,5},{5,1},{9,13},{13,9},{2,6},{6,2},{1... | collective-permute-start | bytes 1769480 | tf_op jit(solution)/shard_map/ppermute | solution.py:381
  39.3 35.9 %collective-permute-start.7 = (bf16[256,1792]{1,0:T(8,128)(2,1)S(1)}, bf16[256,1792]{1,0:T(8,128)(2,1)S(1)}, u32[]{:S(2)}, u32[]{:S(2)}) collective-permute-start(bf16[256,1792]{1,0:T(8,128)(2,1)S(1)} %get-tuple-element.36.refs_2_), channel_id=1, source_target_pairs={{0,8},{4,12},{8,0},{12,4},{1,9},{5,13},{9,1},{13,5},{2,10},{6,14},... | collective-permute-start | bytes 2752520 | tf_op jit(solution)/shard_map/ppermute | solution.py:384
  52.5 14.9 %collective-permute-start.8 = (bf16[256,768]{1,0:T(8,128)(2,1)S(1)}, bf16[256,768]{1,0:T(8,128)(2,1)S(1)}, u32[]{:S(2)}, u32[]{:S(2)}) collective-permute-start(bf16[256,768]{1,0:T(8,128)(2,1)S(1)} %get-tuple-element.49.refs_4_.refs_0_), channel_id=1, source_target_pairs={{0,4},{4,0},{8,12},{12,8},{1,5},{5,1},{9,13},{13,9},{2,6},{6,2},{1... | collective-permute-start | bytes 1179656 | tf_op jit(solution)/shard_map/ppermute | solution.py:381
  52.7 14.7 %collective-permute-start.9 = (bf16[256,768]{1,0:T(8,128)(2,1)S(1)}, bf16[256,768]{1,0:T(8,128)(2,1)S(1)}, u32[]{:S(2)}, u32[]{:S(2)}) collective-permute-start(bf16[256,768]{1,0:T(8,128)(2,1)S(1)} %get-tuple-element.51.refs_2_), channel_id=1, source_target_pairs={{0,4},{4,0},{8,12},{12,8},{1,5},{5,1},{9,13},{13,9},{2,6},{6,2},{1... | collective-permute-start | bytes 1179656 | tf_op jit(solution)/shard_map/ppermute | solution.py:381
  53.1 33.0 %collective-permute-start.6 = (bf16[256,1536]{1,0:T(8,128)(2,1)S(1)}, bf16[256,1536]{1,0:T(8,128)(2,1)S(1)}, u32[]{:S(2)}, u32[]{:S(2)}) collective-permute-start(bf16[256,1536]{1,0:T(8,128)(2,1)S(1)} %get-tuple-element.37.refs_3_), channel_id=1, source_target_pairs={{0,8},{4,12},{8,0},{12,4},{1,9},{5,13},{9,1},{13,5},{2,10},{6,14},... | collective-permute-start | bytes 2359304 | tf_op jit(solution)/shard_map/ppermute | solution.py:384
  74.6 25.2 %collective-permute-start.15 = (bf16[2,128,2048]{2,1,0:T(8,128)(2,1)S(1)}, bf16[2,128,2048]{2,1,0:T(8,128)(2,1)S(1)}, u32[]{:S(2)}, u32[]{:S(2)}) collective-permute-start(bf16[2,128,2048]{2,1,0:T(8,128)(2,1)S(1)} %after.3.refs_8_.refs_4_), channel_id=1, source_target_pairs={{1,0},{0,2},{2,3},{3,1},{5,4},{4,6},{6,7},{7,5},{9,8},{8,10},{10,1... | collective-permute-start | bytes 3145736 | tf_op jit(solution)/shard_map/ppermute | solution.py:407
  75.3 1.9 %collective-permute-start.10 = (bf16[256,896]{1,0:T(8,128)(2,1)S(1)}, bf16[256,896]{1,0:T(8,128)(2,1)S(1)}, u32[]{:S(2)}, u32[]{:S(2)}) collective-permute-start(bf16[256,896]{1,0:T(8,128)(2,1)S(1)} %get-tuple-element.55.refs_0_.refs_7_), channel_id=1, source_target_pairs={{0,4},{4,0},{8,12},{12,8},{1,5},{5,1},{9,13},{13,9},{2,6},{6,2},{1... | collective-permute-start | bytes 1376264 | tf_op jit(solution)/shard_map/ppermute | solution.py:381
  75.4 2.5 %collective-permute-start.11 = (bf16[256,896]{1,0:T(8,128)(2,1)S(1)}, bf16[256,896]{1,0:T(8,128)(2,1)S(1)}, u32[]{:S(2)}, u32[]{:S(2)}) collective-permute-start(bf16[256,896]{1,0:T(8,128)(2,1)S(1)} %get-tuple-element.56.refs_2_), channel_id=1, source_target_pairs={{0,4},{4,0},{8,12},{12,8},{1,5},{5,1},{9,13},{13,9},{2,6},{6,2},{1... | collective-permute-start | bytes 1376264 | tf_op jit(solution)/shard_map/ppermute | solution.py:381
  86.2 1.8 %collective-permute-start.13 = (bf16[256,768]{1,0:T(8,128)(2,1)S(1)}, bf16[256,768]{1,0:T(8,128)(2,1)S(1)}, u32[]{:S(2)}, u32[]{:S(2)}) collective-permute-start(bf16[256,768]{1,0:T(8,128)(2,1)S(1)} %get-tuple-element.60.refs_0_.refs_7_), channel_id=1, source_target_pairs={{0,4},{4,0},{8,12},{12,8},{1,5},{5,1},{9,13},{13,9},{2,6},{6,2},{1... | collective-permute-start | bytes 1179656 | tf_op jit(solution)/shard_map/ppermute | solution.py:381
  86.4 2.1 %collective-permute-start.14 = (bf16[256,768]{1,0:T(8,128)(2,1)S(1)}, bf16[256,768]{1,0:T(8,128)(2,1)S(1)}, u32[]{:S(2)}, u32[]{:S(2)}) collective-permute-start(bf16[256,768]{1,0:T(8,128)(2,1)S(1)} %get-tuple-element.61.refs_2_), channel_id=1, source_target_pairs={{0,4},{4,0},{8,12},{12,8},{1,5},{5,1},{9,13},{13,9},{2,6},{6,2},{1... | collective-permute-start | bytes 1179656 | tf_op jit(solution)/shard_map/ppermute | solution.py:381
  99.8 4.7 %copy-start = (s32[2,512]{1,0:T(2,128)S(1)}, s32[2,512]{1,0:T(2,128)}, u32[]{:S(2)}) copy-start(s32[2,512]{1,0:T(2,128)} %param.8) | copy-start | bytes 12292
  99.8 11.0 %copy-start.1 = (s32[2,512]{1,0:T(2,128)S(1)}, s32[2,512]{1,0:T(2,128)}, u32[]{:S(2)}) copy-start(s32[2,512]{1,0:T(2,128)} %param.9) | copy-start | bytes 12292
  102.5 2.4 %collective-permute-start.16 = (f32[2,2,512]{2,1,0:T(2,128)S(1)}, f32[2,2,512]{2,1,0:T(2,128)S(1)}, u32[]{:S(2)}, u32[]{:S(2)}) collective-permute-start(f32[2,2,512]{2,1,0:T(2,128)S(1)} %copy_bitcast_fusion), channel_id=1, source_target_pairs={{0,4},{4,0},{8,12},{12,8},{1,5},{5,1},{9,13},{13,9},{2,6},{6,2},{1... | collective-permute-start | bytes 24584 | tf_op jit(solution)/shard_map/ppermute | solution.py:290
  102.6 3.7 %collective-permute-start.17 = (f32[2,2,512]{2,1,0:T(2,128)S(1)}, f32[2,2,512]{2,1,0:T(2,128)S(1)}, u32[]{:S(2)}, u32[]{:S(2)}) collective-permute-start(f32[2,2,512]{2,1,0:T(2,128)S(1)} %copy_bitcast_fusion), channel_id=1, source_target_pairs={{0,8},{4,12},{8,0},{12,4},{1,9},{5,13},{9,1},{13,5},{2,10},{6,14},... | collective-permute-start | bytes 24584 | tf_op jit(solution)/shard_map/ppermute | solution.py:290
  103.1 3.2 %collective-permute-start.18 = (f32[2,2,512]{2,1,0:T(2,128)S(1)}, f32[2,2,512]{2,1,0:T(2,128)S(1)}, u32[]{:S(2)}, u32[]{:S(2)}) collective-permute-start(f32[2,2,512]{2,1,0:T(2,128)S(1)} %copy_bitcast_fusion), channel_id=1, source_target_pairs={{0,12},{4,8},{8,4},{12,0},{1,13},{5,9},{9,5},{13,1},{2,14},{6,10},... | collective-permute-start | bytes 24584 | tf_op jit(solution)/shard_map/ppermute | solution.py:290
  106.3 4.5 %collective-permute-start.19 = (f32[2,2,512]{2,1,0:T(2,128)S(1)}, f32[2,2,512]{2,1,0:T(2,128)S(1)}, u32[]{:S(2)}, u32[]{:S(2)}) collective-permute-start(f32[2,2,512]{2,1,0:T(2,128)S(1)} %add_add_fusion), channel_id=1, source_target_pairs={{0,1},{1,0},{2,3},{3,2},{4,5},{5,4},{6,7},{7,6},{8,9},{9,8},{10,11... | collective-permute-start | bytes 24584 | tf_op jit(solution)/shard_map/ppermute | solution.py:290
  107.7 4.5 %collective-permute-start.20 = (f32[2,2,512]{2,1,0:T(2,128)S(1)}, f32[2,2,512]{2,1,0:T(2,128)S(1)}, u32[]{:S(2)}, u32[]{:S(2)}) collective-permute-start(f32[2,2,512]{2,1,0:T(2,128)S(1)} %add_add_fusion), channel_id=1, source_target_pairs={{0,2},{1,3},{2,0},{3,1},{4,6},{5,7},{6,4},{7,5},{8,10},{9,11},{10,... | collective-permute-start | bytes 24584 | tf_op jit(solution)/shard_map/ppermute | solution.py:290
  107.7 5.4 %collective-permute-start.21 = (f32[2,2,512]{2,1,0:T(2,128)S(1)}, f32[2,2,512]{2,1,0:T(2,128)S(1)}, u32[]{:S(2)}, u32[]{:S(2)}) collective-permute-start(f32[2,2,512]{2,1,0:T(2,128)S(1)} %add_add_fusion), channel_id=1, source_target_pairs={{0,3},{1,2},{2,1},{3,0},{4,7},{5,6},{6,5},{7,4},{8,11},{9,10},{10,... | collective-permute-start | bytes 24584 | tf_op jit(solution)/shard_map/ppermute | solution.py:290

commit v8 on v7

--- a/solution.py
+++ b/solution.py
@@ -8,7 +8,7 @@
 from jax.experimental.pallas import tpu as pltpu
 from jax.sharding import PartitionSpec as P
 
-WEIGHTS = (9, 6, 7, 6)
+WEIGHTS = (10, 7, 5, 6)
 HELPER_VMEM = 1024 * 1024
 TILE = 512
 
@@ -441,7 +441,7 @@
     for at, (kind, plan, count) in enumerate(calls):
         later = calls[at + 1][1] if at + 1 < len(calls) else None
         others = receive(mark, count) if at > 0 else []
-        if kind == "far" and count:
+        if kind == "far":
             others += step_along(mark)
         if kind == "far" and any(later_kind == "near" for later_kind, _, _ in calls[at:]):
             others.append(pltpu.with_memory_space_constraint(laid, pltpu.VMEM))

time: 114 us -> 113 us (level)
  waiting for transfers between devices: 12.5 us -> 9.18 us
  starting transfers between devices: 20.3 us -> 22.7 us
    ppermute x2, waiting for transfers between devices: 4.13 us -> 0.01 us  [step_along(): slots.append(lax.ppermute(ended, 'out', turn))]
    ppermute x2, starting transfers between devices: 2.42 us -> 4.46 us  [step_along(): slots.append(lax.ppermute(ended, 'out', turn))]
  transfers between devices with their start and end apart: 22 -> 22, of which waited for: 9 -> 10; matrix products, arithmetic and copies ran while one was open for 0% -> 0% of each run, Pallas kernels for 68% -> 68%
where the time goes in v8:
time: 113 us
  Pallas kernels  79.3 us (70%)
  starting transfers between devices  22.7 us (20%)
  waiting for transfers between devices  9.18 us (8%)
    pallas_call x6, Pallas kernels, project(): pl.pallas_call(functools.partial(project_kernel, len(parts), plan, later,...  69.6 us
    ppermute x4, starting transfers between devices, shift(): lax.ppermute(value, 'inp', [(at, (at + pair * by) % inp_size) for at in r...  6.55 us
    ppermute x6, starting transfers between devices, xor_sum(): lax.ppermute(value, axis, [(at, at ^ other) for at in range(size)])  6.37 us
    ppermute x6, waiting for transfers between devices, xor_sum(): lax.ppermute(value, axis, [(at, at ^ other) for at in range(size)])  4.5 us
    ppermute x2, starting transfers between devices, step_along(): slots.append(lax.ppermute(ended, 'out', turn))  4.46 us
    ppermute x9, waiting for transfers between devices, flip(): return lax.ppermute(value, 'inp', [(at, at ^ 1) for at in range(inp_size)])  4.38 us
    pallas_call x2, Pallas kernels, cut(): pl.pallas_call(functools.partial(cut_kernel, spans, len(shapes)), in_spec...  3.3 us
    pallas_call x1, Pallas kernels, load(): pl.pallas_call(functools.partial(load_kernel, plan, len(own)), in_specs=[...  3.13 us
  transfers between devices with their start and end apart: 22, of which 10 were waited for; matrix products, arithmetic and copies ran while one was open for 0% of the time, Pallas kernels for 68%

profile of v8, /device:TPU:0, one launch (start us, length us, event | category | flops | bytes accessed | tf_op | source)
XLA Modules:
  0.0 112.6 jit_solution(12812534157713048035)
XLA Ops:
  0.0 0.5 collective-permute-start.1
  0.5 1.3 %cut.2.refs_0_ = bf16[256,2560]{1,0:T(8,128)(2,1)S(1)} custom-call(bf16[256,7168]{1,0:T(8,128)(2,1)} %bitcast.12, bf16[2,128,2048]{2,1,0:T(8,128)(2,1)} %a_ref.3), custom_call_target="tpu_custom_call" | custom-call | tf_op jit(solution)/shard_map/cut/pallas_call | solution.py:353
  1.8 2.6 %collective-permute-start = (bf16[256,2560]{1,0:T(8,128)(2,1)S(1)}, bf16[256,2560]{1,0:T(8,128)(2,1)S(1)}, u32[]{:S(2)}, u32[]{:S(2)}) collective-permute-start(bf16[256,2560]{1,0:T(8,128)(2,1)S(1)} %cut.2.refs_0_), channel_id=1, source_target_pairs={{0,8},{4,12},{8,0},{12,4},{1,9},{5,13},{9,1},{13,5},{2,10},{6,14},... | collective-permute-start | bytes 3932168 | tf_op jit(solution)/shard_map/ppermute | solution.py:384
  4.4 2.0 %cut.3 = (bf16[256,1792]{1,0:T(8,128)(2,1)S(1)}, bf16[256,1280]{1,0:T(8,128)(2,1)S(1)}, bf16[256,1536]{1,0:T(8,128)(2,1)S(1)}, bf16[2,128,2048]{2,1,0:T(8,128)(2,1)S(1)}) custom-call(bf16[256,7168]{1,0:T(8,128)(2,1)} %bitcast.13, bf16[2,128,2048]{2,1,0:T(8,128)(2,1)} %a_ref.3, bf16[256,2560]{1,0:T(8,128)(2,1)S(1)} %cut.2.refs_0_), custom_call_target="tpu_custom_call" | custom-call | tf_op jit(solution)/shard_map/cut/pallas_call | solution.py:353
  6.4 2.6 %collective-permute-start.4 = (bf16[2,128,2048]{2,1,0:T(8,128)(2,1)S(1)}, bf16[2,128,2048]{2,1,0:T(8,128)(2,1)S(1)}, u32[]{:S(2)}, u32[]{:S(2)}) collective-permute-start(bf16[2,128,2048]{2,1,0:T(8,128)(2,1)S(1)} %get-tuple-element.45.refs_2_), channel_id=1, source_target_pairs={{1,0},{0,2},{2,3},{3,1},{5,4},{4,6},{6,7},{7,5},{9,8},{8,10},{10,1... | collective-permute-start | bytes 3145736 | tf_op jit(solution)/shard_map/ppermute | solution.py:399
  9.0 0.5 collective-permute-start.5
  9.5 3.1 %load.1 = (bf16[7168,512]{1,0:T(8,128)(2,1)S(1)}, bf16[512,7168]{1,0:T(8,128)(2,1)S(1)}) custom-call(bf16[256,2560]{1,0:T(8,128)(2,1)S(1)} %cut.2.refs_0_, bf16[256,1792]{1,0:T(8,128)(2,1)S(1)} %get-tuple-element.36.refs_1_, bf16[256,1280]{1,0:T(8,128)(2,1)S(1)} %get-tuple-element.37.refs_2_, bf16[256,1536]{1,0:T(8,128)(2,1)S(1)} %get-tuple-element.38.refs_3_, ...), custom_call_target="tpu_custom_call" | custom-call | flops 1024 | bytes 1024 | tf_op jit(solution)/shard_map/load/pallas_call | solution.py:79
  12.7 24.1 %project.6 = (f32[2,512,2048]{2,1,0:T(8,128)S(1)}, f32[8,128]{1,0:T(8,128)S(1)}, bf16[7168,512]{1,0:T(8,128)(2,1)S(1)}, bf16[512,7168]{1,0:T(8,128)(2,1)S(1)}) custom-call(bf16[256,7168]{1,0:T(8,128)(2,1)S(1)} %collective-permute-done.1.refs_0_, bf16[2,7168,2048]{2,1,0:T(8,128)(2,1)} %refs_4_.9, ...), custom_call_target="tpu_custom_call", output_to_operand_aliasing={{2}: (2, {}), {3}: (3, {})} | custom-call | flops 1024 | bytes 1024 | tf_op jit(solution)/shard_map/project/pallas_call | solution.py:206
  36.7 1.6 %collective-permute-start.10 = (bf16[2,128,2048]{2,1,0:T(8,128)(2,1)S(1)}, bf16[2,128,2048]{2,1,0:T(8,128)(2,1)S(1)}, u32[]{:S(2)}, u32[]{:S(2)}) collective-permute-start(bf16[2,128,2048]{2,1,0:T(8,128)(2,1)S(1)} %after.2.refs_7_.refs_3_), channel_id=1, source_target_pairs={{1,0},{0,2},{2,3},{3,1},{5,4},{4,6},{6,7},{7,5},{9,8},{8,10},{10,1... | collective-permute-start | bytes 3145736 | tf_op jit(solution)/shard_map/ppermute | solution.py:407
  38.4 0.1 halve.4
  38.5 0.1 collective-permute-start.2
  38.6 0.5 collective-permute-start.3
  39.1 1.5 %collective-permute-start.7 = (bf16[256,1280]{1,0:T(8,128)(2,1)S(1)}, bf16[256,1280]{1,0:T(8,128)(2,1)S(1)}, u32[]{:S(2)}, u32[]{:S(2)}) collective-permute-start(bf16[256,1280]{1,0:T(8,128)(2,1)S(1)} %get-tuple-element.37.refs_2_), channel_id=1, source_target_pairs={{0,8},{4,12},{8,0},{12,4},{1,9},{5,13},{9,1},{13,5},{2,10},{6,14},... | collective-permute-start | bytes 1966088 | tf_op jit(solution)/shard_map/ppermute | solution.py:384
  40.6 0.1 collective-permute-done.2.refs_1_
  40.7 0.9 collective-permute-done.3.refs_3_
  41.6 11.8 %project.7 = (f32[2,512,2048]{2,1,0:T(8,128)S(1)}, f32[8,128]{1,0:T(8,128)S(1)}, bf16[7168,512]{1,0:T(8,128)(2,1)S(1)}) custom-call(bf16[256,1280]{1,0:T(8,128)(2,1)S(1)} %get-tuple-element.42.refs_0_.refs_6_, bf16[256,1280]{1,0:T(8,128)(2,1)S(1)} %collective-permute-done.2.refs_1_, ...), custom_call_target="tpu_custom_call", output_to_operand_aliasing={{2}: (5, {})} | custom-call | flops 1024 | bytes 1024 | tf_op jit(solution)/shard_map/project/pallas_call | solution.py:206
  53.4 0.3 collective-permute-done.5.source_ref
  53.7 0.1 halve.5
  53.8 0.1 collective-permute-start.8
  53.8 0.5 collective-permute-start.9
  54.3 1.9 %collective-permute-start.6 = (bf16[256,1536]{1,0:T(8,128)(2,1)S(1)}, bf16[256,1536]{1,0:T(8,128)(2,1)S(1)}, u32[]{:S(2)}, u32[]{:S(2)}) collective-permute-start(bf16[256,1536]{1,0:T(8,128)(2,1)S(1)} %get-tuple-element.38.refs_3_), channel_id=1, source_target_pairs={{0,8},{4,12},{8,0},{12,4},{1,9},{5,13},{9,1},{13,5},{2,10},{6,14},... | collective-permute-start | bytes 2359304 | tf_op jit(solution)/shard_map/ppermute | solution.py:384
  56.3 12.4 %project.8 = (f32[2,512,2048]{2,1,0:T(8,128)S(1)}, f32[8,128]{1,0:T(8,128)S(1)}, bf16[7168,512]{1,0:T(8,128)(2,1)S(1)}, bf16[512,7168]{1,0:T(8,128)(2,1)S(1)}) custom-call(bf16[2,7168,2048]{2,1,0:T(8,128)(2,1)} %refs_4_.9, bf16[7168,512]{1,0:T(8,128)(2,1)S(1)} %get-tuple-element.47.refs_1_, ...), custom_call_target="tpu_custom_call", output_to_operand_aliasing={{2}: (1, {}), {0}: (2, {}), {3}: (3, {})} | custom-call | flops 1024 | bytes 1024 | tf_op jit(solution)/shard_map/project/pallas_call | solution.py:206
  68.7 2.8 %collective-permute-start.15 = (bf16[2,128,2048]{2,1,0:T(8,128)(2,1)S(1)}, bf16[2,128,2048]{2,1,0:T(8,128)(2,1)S(1)}, u32[]{:S(2)}, u32[]{:S(2)}) collective-permute-start(bf16[2,128,2048]{2,1,0:T(8,128)(2,1)S(1)} %after.3.refs_7_.refs_4_), channel_id=1, source_target_pairs={{1,0},{0,2},{2,3},{3,1},{5,4},{4,6},{6,7},{7,5},{9,8},{8,10},{10,1... | collective-permute-start | bytes 3145736 | tf_op jit(solution)/shard_map/ppermute | solution.py:407
  71.5 8.2 %project.9 = (f32[2,512,2048]{2,1,0:T(8,128)S(1)}, f32[8,128]{1,0:T(8,128)S(1)}, bf16[7168,512]{1,0:T(8,128)(2,1)S(1)}) custom-call(bf16[256,896]{1,0:T(8,128)(2,1)S(1)} %get-tuple-element.50.refs_4_.refs_0_, bf16[256,896]{1,0:T(8,128)(2,1)S(1)} %collective-permute-done.8.refs_1_, ...), custom_call_target="tpu_custom_call", output_to_operand_aliasing={{2}: (5, {}), {0}: (6, {})} | custom-call | flops 1024 | bytes 1024 | tf_op jit(solution)/shard_map/project/pallas_call | solution.py:206
  79.8 0.1 halve.6
  79.9 0.1 collective-permute-start.11
  80.0 0.5 collective-permute-start.12
  80.5 1.1 collective-permute-done.11.refs_1_
  81.6 0.5 collective-permute-done.12.refs_3_
  82.0 6.0 %project.10 = (f32[2,512,2048]{2,1,0:T(8,128)S(1)}, f32[8,128]{1,0:T(8,128)S(1)}, bf16[7168,512]{1,0:T(8,128)(2,1)S(1)}) custom-call(bf16[256,640]{1,0:T(8,128)(2,1)S(1)} %get-tuple-element.57.refs_0_.refs_7_, bf16[256,640]{1,0:T(8,128)(2,1)S(1)} %collective-permute-done.11.refs_1_, ...), custom_call_target="tpu_custom_call", output_to_operand_aliasing={{2}: (5, {}), {0}: (6, {})} | custom-call | flops 1024 | bytes 1024 | tf_op jit(solution)/shard_map/project/pallas_call | solution.py:206
  88.1 0.1 halve.7
  88.2 0.2 collective-permute-start.13
  88.4 0.4 collective-permute-start.14
  88.8 1.2 %collective-permute-done.13.refs_1_ = bf16[256,768]{1,0:T(8,128)(2,1)S(1)} collective-permute-done((bf16[256,768]{1,0:T(8,128)(2,1)S(1)}, bf16[256,768]{1,0:T(8,128)(2,1)S(1)}, u32[]{:S(2)}, u32[]{:S(2)}) %collective-permute-start.13) | collective-permute-done | bytes 393248 | tf_op jit(solution)/shard_map/ppermute | solution.py:381
  90.0 0.6 collective-permute-done.14.refs_3_
  90.6 7.1 %project.11 = (f32[2,512,2048]{2,1,0:T(8,128)S(1)}, f32[8,128]{1,0:T(8,128)}, bf16[7168,512]{1,0:T(8,128)(2,1)S(1)}) custom-call(bf16[256,768]{1,0:T(8,128)(2,1)S(1)} %get-tuple-element.62.refs_0_.refs_7_, bf16[256,768]{1,0:T(8,128)(2,1)S(1)} %collective-permute-done.13.refs_1_, ...), custom_call_target="tpu_custom_call", output_to_operand_aliasing={{2}: (5, {}), {0}: (6, {})} | custom-call | flops 1024 | bytes 1024 | tf_op jit(solution)/shard_map/project/pallas_call | solution.py:206
  97.7 2.9 %score.1 = f32[4,2,256]{2,1,0:T(2,128)S(1)} custom-call(f32[2,512,2048]{2,1,0:T(8,128)S(1)} %get-tuple-element.51.refs_0_, f32[2,512,2048]{2,1,0:T(8,128)S(1)} %get-tuple-element.66.refs_1_, bf16[2,128,2048]{2,1,0:T(8,128)(2,1)S(1)} %get-tuple-element.45.refs_2_, bf16[2,128,2048]{2,1,0:T(8,128)(2,1)S(1)} %after.2.refs_7_.refs_3_, ...), custom_call_target="tpu_custom_call" | custom-call | tf_op jit(solution)/shard_map/score/pallas_call | solution.py:270
  100.7 0.2 collective-permute-start.16
  100.9 0.5 collective-permute-start.17
  101.4 1.2 %collective-permute-start.18 = (f32[2,2,512]{2,1,0:T(2,128)S(1)}, f32[2,2,512]{2,1,0:T(2,128)S(1)}, u32[]{:S(2)}, u32[]{:S(2)}) collective-permute-start(f32[2,2,512]{2,1,0:T(2,128)S(1)} %copy_bitcast_fusion), channel_id=1, source_target_pairs={{0,12},{4,8},{8,4},{12,0},{1,13},{5,9},{9,5},{13,1},{2,14},{6,10},... | collective-permute-start | bytes 24584 | tf_op jit(solution)/shard_map/ppermute | solution.py:290
  102.6 0.4 convert_reduce_fusion
  103.0 1.6 %collective-permute-done.17 = f32[2,2,512]{2,1,0:T(2,128)S(1)} collective-permute-done((f32[2,2,512]{2,1,0:T(2,128)S(1)}, f32[2,2,512]{2,1,0:T(2,128)S(1)}, u32[]{:S(2)}, u32[]{:S(2)}) %collective-permute-start.17) | collective-permute-done | bytes 8224 | tf_op jit(solution)/shard_map/ppermute | solution.py:290
  104.6 0.1 collective-permute-start.19
  104.7 1.9 %collective-permute-start.20 = (f32[2,2,512]{2,1,0:T(2,128)S(1)}, f32[2,2,512]{2,1,0:T(2,128)S(1)}, u32[]{:S(2)}, u32[]{:S(2)}) collective-permute-start(f32[2,2,512]{2,1,0:T(2,128)S(1)} %add_add_fusion), channel_id=1, source_target_pairs={{0,2},{1,3},{2,0},{3,1},{4,6},{5,7},{6,4},{7,5},{8,10},{9,11},{10,... | collective-permute-start | bytes 24584 | tf_op jit(solution)/shard_map/ppermute | solution.py:290
  106.6 2.5 %collective-permute-start.21 = (f32[2,2,512]{2,1,0:T(2,128)S(1)}, f32[2,2,512]{2,1,0:T(2,128)S(1)}, u32[]{:S(2)}, u32[]{:S(2)}) collective-permute-start(f32[2,2,512]{2,1,0:T(2,128)S(1)} %add_add_fusion), channel_id=1, source_target_pairs={{0,3},{1,2},{2,1},{3,0},{4,7},{5,6},{6,5},{7,4},{8,11},{9,10},{10,... | collective-permute-start | bytes 24584 | tf_op jit(solution)/shard_map/ppermute | solution.py:290
  109.1 0.2 collective-permute-done.20
  109.3 2.7 %collective-permute-done.21 = f32[2,2,512]{2,1,0:T(2,128)S(1)} collective-permute-done((f32[2,2,512]{2,1,0:T(2,128)S(1)}, f32[2,2,512]{2,1,0:T(2,128)S(1)}, u32[]{:S(2)}, u32[]{:S(2)}) %collective-permute-start.21) | collective-permute-done | bytes 8224 | tf_op jit(solution)/shard_map/ppermute | solution.py:290
  112.0 0.6 add_multiply_fusion
  (22 shorter events, 0.1 us)
Async XLA Ops:
  0.0 12.6 %collective-permute-start.1 = (bf16[256,7168]{1,0:T(8,128)(2,1)}, bf16[256,7168]{1,0:T(8,128)(2,1)S(1)}, u32[]{:S(2)}, u32[]{:S(2)}) collective-permute-start(bf16[256,7168]{1,0:T(8,128)(2,1)} %bitcast.11), channel_id=1, source_target_pairs={{0,4},{4,0},{8,12},{12,8},{1,5},{5,1},{9,13},{13,9},{2,6},{6,2},{1... | collective-permute-start | bytes 11010056 | tf_op jit(solution)/shard_map/ppermute | solution.py:381
  1.8 36.6 %collective-permute-start = (bf16[256,2560]{1,0:T(8,128)(2,1)S(1)}, bf16[256,2560]{1,0:T(8,128)(2,1)S(1)}, u32[]{:S(2)}, u32[]{:S(2)}) collective-permute-start(bf16[256,2560]{1,0:T(8,128)(2,1)S(1)} %cut.2.refs_0_), channel_id=1, source_target_pairs={{0,8},{4,12},{8,0},{12,4},{1,9},{5,13},{9,1},{13,5},{2,10},{6,14},... | collective-permute-start | bytes 3932168 | tf_op jit(solution)/shard_map/ppermute | solution.py:384
  6.4 30.4 %collective-permute-start.4 = (bf16[2,128,2048]{2,1,0:T(8,128)(2,1)S(1)}, bf16[2,128,2048]{2,1,0:T(8,128)(2,1)S(1)}, u32[]{:S(2)}, u32[]{:S(2)}) collective-permute-start(bf16[2,128,2048]{2,1,0:T(8,128)(2,1)S(1)} %get-tuple-element.45.refs_2_), channel_id=1, source_target_pairs={{1,0},{0,2},{2,3},{3,1},{5,4},{4,6},{6,7},{7,5},{9,8},{8,10},{10,1... | collective-permute-start | bytes 3145736 | tf_op jit(solution)/shard_map/ppermute | solution.py:399
  9.0 44.7 %collective-permute-start.5 = (bf16[256,1792]{1,0:T(8,128)(2,1)S(1)}, bf16[256,1792]{1,0:T(8,128)(2,1)S(1)}, u32[]{:S(2)}, u32[]{:S(2)}) collective-permute-start(bf16[256,1792]{1,0:T(8,128)(2,1)S(1)} %get-tuple-element.36.refs_1_), channel_id=1, source_target_pairs={{0,8},{4,12},{8,0},{12,4},{1,9},{5,13},{9,1},{13,5},{2,10},{6,14},... | collective-permute-start | bytes 2752520 | tf_op jit(solution)/shard_map/ppermute | solution.py:384
  36.7 32.0 %collective-permute-start.10 = (bf16[2,128,2048]{2,1,0:T(8,128)(2,1)S(1)}, bf16[2,128,2048]{2,1,0:T(8,128)(2,1)S(1)}, u32[]{:S(2)}, u32[]{:S(2)}) collective-permute-start(bf16[2,128,2048]{2,1,0:T(8,128)(2,1)S(1)} %after.2.refs_7_.refs_3_), channel_id=1, source_target_pairs={{1,0},{0,2},{2,3},{3,1},{5,4},{4,6},{6,7},{7,5},{9,8},{8,10},{10,1... | collective-permute-start | bytes 3145736 | tf_op jit(solution)/shard_map/ppermute | solution.py:407
  38.5 2.2 %collective-permute-start.2 = (bf16[256,1280]{1,0:T(8,128)(2,1)S(1)}, bf16[256,1280]{1,0:T(8,128)(2,1)S(1)}, u32[]{:S(2)}, u32[]{:S(2)}) collective-permute-start(bf16[256,1280]{1,0:T(8,128)(2,1)S(1)} %get-tuple-element.42.refs_0_.refs_6_), channel_id=1, source_target_pairs={{0,4},{4,0},{8,12},{12,8},{1,5},{5,1},{9,13},{13,9},{2,6},{6,2},{1... | collective-permute-start | bytes 1966088 | tf_op jit(solution)/shard_map/ppermute | solution.py:381
  38.6 3.0 %collective-permute-start.3 = (bf16[256,1280]{1,0:T(8,128)(2,1)S(1)}, bf16[256,1280]{1,0:T(8,128)(2,1)S(1)}, u32[]{:S(2)}, u32[]{:S(2)}) collective-permute-start(bf16[256,1280]{1,0:T(8,128)(2,1)S(1)} %get-tuple-element.43.refs_2_), channel_id=1, source_target_pairs={{0,4},{4,0},{8,12},{12,8},{1,5},{5,1},{9,13},{13,9},{2,6},{6,2},{1... | collective-permute-start | bytes 1966088 | tf_op jit(solution)/shard_map/ppermute | solution.py:381
  39.1 40.7 %collective-permute-start.7 = (bf16[256,1280]{1,0:T(8,128)(2,1)S(1)}, bf16[256,1280]{1,0:T(8,128)(2,1)S(1)}, u32[]{:S(2)}, u32[]{:S(2)}) collective-permute-start(bf16[256,1280]{1,0:T(8,128)(2,1)S(1)} %get-tuple-element.37.refs_2_), channel_id=1, source_target_pairs={{0,8},{4,12},{8,0},{12,4},{1,9},{5,13},{9,1},{13,5},{2,10},{6,14},... | collective-permute-start | bytes 1966088 | tf_op jit(solution)/shard_map/ppermute | solution.py:384
  53.8 17.8 %collective-permute-start.8 = (bf16[256,896]{1,0:T(8,128)(2,1)S(1)}, bf16[256,896]{1,0:T(8,128)(2,1)S(1)}, u32[]{:S(2)}, u32[]{:S(2)}) collective-permute-start(bf16[256,896]{1,0:T(8,128)(2,1)S(1)} %get-tuple-element.50.refs_4_.refs_0_), channel_id=1, source_target_pairs={{0,4},{4,0},{8,12},{12,8},{1,5},{5,1},{9,13},{13,9},{2,6},{6,2},{1... | collective-permute-start | bytes 1376264 | tf_op jit(solution)/shard_map/ppermute | solution.py:381
  53.8 17.7 %collective-permute-start.9 = (bf16[256,896]{1,0:T(8,128)(2,1)S(1)}, bf16[256,896]{1,0:T(8,128)(2,1)S(1)}, u32[]{:S(2)}, u32[]{:S(2)}) collective-permute-start(bf16[256,896]{1,0:T(8,128)(2,1)S(1)} %get-tuple-element.52.refs_2_), channel_id=1, source_target_pairs={{0,4},{4,0},{8,12},{12,8},{1,5},{5,1},{9,13},{13,9},{2,6},{6,2},{1... | collective-permute-start | bytes 1376264 | tf_op jit(solution)/shard_map/ppermute | solution.py:381
  54.3 33.8 %collective-permute-start.6 = (bf16[256,1536]{1,0:T(8,128)(2,1)S(1)}, bf16[256,1536]{1,0:T(8,128)(2,1)S(1)}, u32[]{:S(2)}, u32[]{:S(2)}) collective-permute-start(bf16[256,1536]{1,0:T(8,128)(2,1)S(1)} %get-tuple-element.38.refs_3_), channel_id=1, source_target_pairs={{0,8},{4,12},{8,0},{12,4},{1,9},{5,13},{9,1},{13,5},{2,10},{6,14},... | collective-permute-start | bytes 2359304 | tf_op jit(solution)/shard_map/ppermute | solution.py:384
  68.7 29.0 %collective-permute-start.15 = (bf16[2,128,2048]{2,1,0:T(8,128)(2,1)S(1)}, bf16[2,128,2048]{2,1,0:T(8,128)(2,1)S(1)}, u32[]{:S(2)}, u32[]{:S(2)}) collective-permute-start(bf16[2,128,2048]{2,1,0:T(8,128)(2,1)S(1)} %after.3.refs_7_.refs_4_), channel_id=1, source_target_pairs={{1,0},{0,2},{2,3},{3,1},{5,4},{4,6},{6,7},{7,5},{9,8},{8,10},{10,1... | collective-permute-start | bytes 3145736 | tf_op jit(solution)/shard_map/ppermute | solution.py:407
  79.9 1.7 %collective-permute-start.11 = (bf16[256,640]{1,0:T(8,128)(2,1)S(1)}, bf16[256,640]{1,0:T(8,128)(2,1)S(1)}, u32[]{:S(2)}, u32[]{:S(2)}) collective-permute-start(bf16[256,640]{1,0:T(8,128)(2,1)S(1)} %get-tuple-element.57.refs_0_.refs_7_), channel_id=1, source_target_pairs={{0,4},{4,0},{8,12},{12,8},{1,5},{5,1},{9,13},{13,9},{2,6},{6,2},{1... | collective-permute-start | bytes 983048 | tf_op jit(solution)/shard_map/ppermute | solution.py:381
  80.0 2.1 %collective-permute-start.12 = (bf16[256,640]{1,0:T(8,128)(2,1)S(1)}, bf16[256,640]{1,0:T(8,128)(2,1)S(1)}, u32[]{:S(2)}, u32[]{:S(2)}) collective-permute-start(bf16[256,640]{1,0:T(8,128)(2,1)S(1)} %get-tuple-element.58.refs_2_), channel_id=1, source_target_pairs={{0,4},{4,0},{8,12},{12,8},{1,5},{5,1},{9,13},{13,9},{2,6},{6,2},{1... | collective-permute-start | bytes 983048 | tf_op jit(solution)/shard_map/ppermute | solution.py:381
  88.2 1.8 %collective-permute-start.13 = (bf16[256,768]{1,0:T(8,128)(2,1)S(1)}, bf16[256,768]{1,0:T(8,128)(2,1)S(1)}, u32[]{:S(2)}, u32[]{:S(2)}) collective-permute-start(bf16[256,768]{1,0:T(8,128)(2,1)S(1)} %get-tuple-element.62.refs_0_.refs_7_), channel_id=1, source_target_pairs={{0,4},{4,0},{8,12},{12,8},{1,5},{5,1},{9,13},{13,9},{2,6},{6,2},{1... | collective-permute-start | bytes 1179656 | tf_op jit(solution)/shard_map/ppermute | solution.py:381
  88.4 2.1 %collective-permute-start.14 = (bf16[256,768]{1,0:T(8,128)(2,1)S(1)}, bf16[256,768]{1,0:T(8,128)(2,1)S(1)}, u32[]{:S(2)}, u32[]{:S(2)}) collective-permute-start(bf16[256,768]{1,0:T(8,128)(2,1)S(1)} %get-tuple-element.63.refs_2_), channel_id=1, source_target_pairs={{0,4},{4,0},{8,12},{12,8},{1,5},{5,1},{9,13},{13,9},{2,6},{6,2},{1... | collective-permute-start | bytes 1179656 | tf_op jit(solution)/shard_map/ppermute | solution.py:381
  97.7 4.9 %copy-start = (s32[2,512]{1,0:T(2,128)S(1)}, s32[2,512]{1,0:T(2,128)}, u32[]{:S(2)}) copy-start(s32[2,512]{1,0:T(2,128)} %param.8) | copy-start | bytes 12292
  97.7 11.3 %copy-start.1 = (s32[2,512]{1,0:T(2,128)S(1)}, s32[2,512]{1,0:T(2,128)}, u32[]{:S(2)}) copy-start(s32[2,512]{1,0:T(2,128)} %param.9) | copy-start | bytes 12292
  100.7 2.3 %collective-permute-start.16 = (f32[2,2,512]{2,1,0:T(2,128)S(1)}, f32[2,2,512]{2,1,0:T(2,128)S(1)}, u32[]{:S(2)}, u32[]{:S(2)}) collective-permute-start(f32[2,2,512]{2,1,0:T(2,128)S(1)} %copy_bitcast_fusion), channel_id=1, source_target_pairs={{0,4},{4,0},{8,12},{12,8},{1,5},{5,1},{9,13},{13,9},{2,6},{6,2},{1... | collective-permute-start | bytes 24584 | tf_op jit(solution)/shard_map/ppermute | solution.py:290
  100.9 3.7 %collective-permute-start.17 = (f32[2,2,512]{2,1,0:T(2,128)S(1)}, f32[2,2,512]{2,1,0:T(2,128)S(1)}, u32[]{:S(2)}, u32[]{:S(2)}) collective-permute-start(f32[2,2,512]{2,1,0:T(2,128)S(1)} %copy_bitcast_fusion), channel_id=1, source_target_pairs={{0,8},{4,12},{8,0},{12,4},{1,9},{5,13},{9,1},{13,5},{2,10},{6,14},... | collective-permute-start | bytes 24584 | tf_op jit(solution)/shard_map/ppermute | solution.py:290
  101.4 3.2 %collective-permute-start.18 = (f32[2,2,512]{2,1,0:T(2,128)S(1)}, f32[2,2,512]{2,1,0:T(2,128)S(1)}, u32[]{:S(2)}, u32[]{:S(2)}) collective-permute-start(f32[2,2,512]{2,1,0:T(2,128)S(1)} %copy_bitcast_fusion), channel_id=1, source_target_pairs={{0,12},{4,8},{8,4},{12,0},{1,13},{5,9},{9,5},{13,1},{2,14},{6,10},... | collective-permute-start | bytes 24584 | tf_op jit(solution)/shard_map/ppermute | solution.py:290
  104.6 4.5 %collective-permute-start.19 = (f32[2,2,512]{2,1,0:T(2,128)S(1)}, f32[2,2,512]{2,1,0:T(2,128)S(1)}, u32[]{:S(2)}, u32[]{:S(2)}) collective-permute-start(f32[2,2,512]{2,1,0:T(2,128)S(1)} %add_add_fusion), channel_id=1, source_target_pairs={{0,1},{1,0},{2,3},{3,2},{4,5},{5,4},{6,7},{7,6},{8,9},{9,8},{10,11... | collective-permute-start | bytes 24584 | tf_op jit(solution)/shard_map/ppermute | solution.py:290
  104.7 4.6 %collective-permute-start.20 = (f32[2,2,512]{2,1,0:T(2,128)S(1)}, f32[2,2,512]{2,1,0:T(2,128)S(1)}, u32[]{:S(2)}, u32[]{:S(2)}) collective-permute-start(f32[2,2,512]{2,1,0:T(2,128)S(1)} %add_add_fusion), channel_id=1, source_target_pairs={{0,2},{1,3},{2,0},{3,1},{4,6},{5,7},{6,4},{7,5},{8,10},{9,11},{10,... | collective-permute-start | bytes 24584 | tf_op jit(solution)/shard_map/ppermute | solution.py:290
  106.6 5.4 %collective-permute-start.21 = (f32[2,2,512]{2,1,0:T(2,128)S(1)}, f32[2,2,512]{2,1,0:T(2,128)S(1)}, u32[]{:S(2)}, u32[]{:S(2)}) collective-permute-start(f32[2,2,512]{2,1,0:T(2,128)S(1)} %add_add_fusion), channel_id=1, source_target_pairs={{0,3},{1,2},{2,1},{3,0},{4,7},{5,6},{6,5},{7,4},{8,11},{9,10},{10,... | collective-permute-start | bytes 24584 | tf_op jit(solution)/shard_map/ppermute | solution.py:290
